TPU v7x, 256 devices: a whole 4x4x8 slice. The times are simulated.
256 devices in a mesh: expert: 4 (over x_lo, core), tensor: 32 (over y, z), kv: 2 (over x_hi).
Axes of the slice: x: 4 (x_hi: 2, x_lo: 2; x = x_hi * 2 + x_lo), y: 4, z: 8, core: 2. Of those that a mesh axis runs over, the one named last changes fastest.
Arguments:
- residual_stream: bfloat16 [1024, 4096], P('expert', ('tensor', 'kv')), may hold values from -13 to 13
- grad_output: bfloat16 [1024, 4096], P('expert', ('tensor', 'kv')), may hold values from -6 to 6
- norm_gain: bfloat16 [4096], P(('tensor', 'kv')), may hold values from 0.5 to 1.5
- expert_ids: int32 [1024, 2], P('expert'), may hold values from 0 to 3, all different within a row; in each aligned block of 256 rows (0 to 255, 256 to 511, ...) at most 160 rows name the same one
- gate_probs: float32 [1024, 2], P('expert'), may hold values from 0.1 to 0.9
- w_gate: bfloat16 [4, 14336, 4096], P('expert', ('tensor', 'kv')), may hold values from -0.25 to 0.25
- w_up: bfloat16 [4, 14336, 4096], P('expert', ('tensor', 'kv')), may hold values from -0.25 to 0.25
- w_down: bfloat16 [4, 14336, 4096], P('expert', ('tensor', 'kv')), may hold values from -0.046875 to 0.046875
Outputs:
- input_grad: bfloat16 [1024, 4096], P('expert', ('tensor', 'kv'))
Inputs may be any that keep to these rules, and one draw needn't show every extreme that they name: `expert_ids`: each row names two different experts. In each aligned block of 256 rows (the rows of one index of the expert axis) no expert is named by more than 160 rows, a bound that some block reaches.
All inputs are finite; a program needn't handle non-finite values.
Results may differ from a plain program's by a relative error of at most 0.018.
Values may be sent and summed in bfloat16 or wider, within the bound.
No kernel may reach another device: no remote copies, remote signals or barrier semaphores. Data moves between devices by JAX's collectives and lax.ppermute only.
A program may use at most 128 MiB of HBM per device.

v0:
```python
import jax
import jax.numpy as jnp
from jax import lax
from jax.sharding import Mesh
from jax.sharding import PartitionSpec as P

D = 4096
CAP = 160
TENSOR_KV = ("tensor_0", "tensor_1", "kv")
TENSOR = ("tensor_0", "tensor_1")


epsilon = 1e-05
contract_width = (((1,), (1,)), ((), ()))
contract_hidden = (((0,), (1,)), ((), ()))
contract_slots = (((0,), (0,)), ((), ()))


def from_everyone(value, axis):
    length = lax.axis_size(axis)
    return lax.all_to_all(
        jnp.broadcast_to(value[None], (length, *value.shape)), axis, 0, 0, tiled=True
    )


def of_everyone(value, axis):
    everything = from_everyone(value, axis)
    return jnp.sum(everything, axis=0)


def in_one_piece(arrays, axis, dim, along):
    both = jnp.concatenate(arrays, axis=along)
    filled, at, finished = (lax.all_gather(both, axis, axis=dim, tiled=True), 0, [])
    for a in arrays:
        finished.append(lax.slice_in_dim(filled, at, at + a.shape[along], axis=along))
        at += a.shape[along]
    return tuple(finished)


def joined_along(tiles, dim):
    dims = list(tiles.shape[1:])
    dims[dim] *= tiles.shape[0]
    return jnp.moveaxis(tiles, 0, dim).reshape(dims)


def gather_packed(arrays, axis, dims):
    vector = jnp.concatenate([a.reshape(-1) for a in arrays])
    lines, at, finished = (lax.all_gather(vector, axis), 0, [])
    for a, dim in zip(arrays, dims):
        tiles = lines[:, at : at + a.size].reshape(-1, *a.shape)
        finished.append(joined_along(tiles, dim))
        at += a.size
    return tuple(finished)


def own_rows(terms, axes):
    subtotal = terms.astype(jnp.bfloat16)
    for axis in axes:
        subtotal = lax.psum_scatter(subtotal, axis, scatter_dimension=0, tiled=True)
    return subtotal.astype(jnp.float32)


def slot_matrix(ids_block, experts):
    flattened = ids_block.reshape(-1)
    onehot = (flattened[:, None] == jnp.arange(experts, dtype=jnp.int32)[None, :]).astype(jnp.int32)
    before = jnp.cumsum(onehot, axis=0) - onehot
    position = jnp.sum(before * onehot, axis=1)
    slot_index = flattened * CAP + position
    table = jnp.arange(experts * CAP, dtype=jnp.int32)
    return (slot_index[None, :] == table[:, None]).astype(jnp.bfloat16)


def shards(residual_stream, grad_output, norm_gain, expert_ids, gate_probs, w_gate, w_up, w_down):
    experts = lax.axis_size("expert")
    local_width = residual_stream.shape[1]
    tokens_here = residual_stream.shape[0]
    stream = residual_stream.astype(jnp.float32)
    squares = of_everyone(jnp.sum(stream * stream, axis=1), TENSOR_KV)
    inverse_rms = lax.rsqrt(squares / D + epsilon)[:, None]
    gains = norm_gain.astype(jnp.float32)
    normed = (stream * inverse_rms * gains).astype(jnp.bfloat16)
    table = slot_matrix(expert_ids, experts)
    repeated_x = jnp.repeat(normed, 2, axis=0)
    scaled = (
        jnp.repeat(grad_output.astype(jnp.float32), 2, axis=0) * gate_probs.reshape(-1, 1)
    ).astype(jnp.bfloat16)
    routed_x = jnp.dot(table, repeated_x, preferred_element_type=jnp.float32).astype(jnp.bfloat16)
    routed_grad = jnp.dot(table, scaled, preferred_element_type=jnp.float32).astype(jnp.bfloat16)
    routed_x = routed_x.reshape(experts, CAP, local_width)
    routed_grad = routed_grad.reshape(experts, CAP, local_width)
    gate_weight, up_weight, down_weight = in_one_piece((w_gate[0], w_up[0], w_down[0]), "kv", 0, 1)
    pieces_x = lax.all_to_all(routed_x, "expert", split_axis=0, concat_axis=0, tiled=True)
    pieces_dy = lax.all_to_all(routed_grad, "expert", split_axis=0, concat_axis=0, tiled=True)
    half_x = lax.all_to_all(pieces_x, "kv", split_axis=0, concat_axis=2, tiled=True)
    half_dy = lax.all_to_all(pieces_dy, "kv", split_axis=0, concat_axis=2, tiled=True)
    full_x, full_dy = gather_packed((half_x, half_dy), TENSOR, (2, 2))
    leading = full_x.shape[0]
    items = full_x.shape[1]
    matrix_x = full_x.reshape(leading * items, D)
    matrix_dy = full_dy.reshape(leading * items, D)
    gate_value = lax.dot_general(
        matrix_x, gate_weight, contract_width, preferred_element_type=jnp.float32
    )
    up_value = lax.dot_general(
        matrix_x, up_weight, contract_width, preferred_element_type=jnp.float32
    )
    act_grad = lax.dot_general(
        matrix_dy, down_weight, contract_width, preferred_element_type=jnp.float32
    )
    sigmoid_gate = jax.nn.sigmoid(gate_value)
    activated = gate_value * sigmoid_gate
    gate_grad = (
        act_grad * up_value * sigmoid_gate * (1.0 + gate_value * (1.0 - sigmoid_gate))
    ).astype(jnp.bfloat16)
    up_grad = (act_grad * activated).astype(jnp.bfloat16)
    total = lax.dot_general(
        gate_weight, gate_grad, contract_hidden, preferred_element_type=jnp.float32
    )
    summed = own_rows(
        total
        + lax.dot_general(up_weight, up_grad, contract_hidden, preferred_element_type=jnp.float32),
        TENSOR,
    )
    wide = summed.T.astype(jnp.bfloat16).reshape(leading, items, 2 * local_width)
    returned = lax.all_to_all(wide, "kv", split_axis=2, concat_axis=0, tiled=True)
    combined = lax.all_to_all(returned, "expert", split_axis=0, concat_axis=0, tiled=True)
    gathered = lax.dot_general(
        table,
        combined.reshape(experts * CAP, local_width),
        contract_slots,
        preferred_element_type=jnp.float32,
    )
    token_grad = gathered.reshape(tokens_here, 2, local_width).sum(axis=1)
    scaled_grad = token_grad * gains
    projection = of_everyone(jnp.sum(scaled_grad * stream, axis=1), TENSOR_KV)[:, None]
    result = inverse_rms * scaled_grad - stream * inverse_rms**3 * projection / D
    return result.astype(jnp.bfloat16)


def solution(mesh):
    torus = Mesh(
        mesh.devices.reshape(mesh.shape["expert"], 4, 8, mesh.shape["kv"]),
        ("expert", "tensor_0", "tensor_1", "kv"),
    )
    return jax.shard_map(
        shards,
        mesh=torus,
        in_specs=(
            P("expert", TENSOR_KV),
            P("expert", TENSOR_KV),
            P(TENSOR_KV),
            P("expert", None),
            P("expert", None),
            P("expert", TENSOR_KV, None),
            P("expert", TENSOR_KV, None),
            P("expert", TENSOR_KV, None),
        ),
        out_specs=P("expert", TENSOR_KV),
        check_vma=False,
    )
```

profile of v0, /device:TPU:1, one launch (start us, length us, event | category | flops | bytes accessed | tf_op | source)
XLA Modules:
  0.0 442.6 jit_solution(14402665509905295335)
XLA Ops:
  12.7 7.1 %all-to-all-start.3 = ((bf16[4,160,64]{1,2,0:T(8,128)(2,1)}), bf16[4,160,64]{1,2,0:T(8,128)(2,1)}, u32[]{:S(2)}, u32[]{:S(2)}) async-start(bf16[4,160,64]{1,2,0:T(8,128)(2,1)} %copy.103), calls=%async_computation.3 | async-start | bytes 262144 | tf_op jit(solution)/shard_map/all_to_all | solution.py:93
  24.2 12.5 %all-to-all-start = ((f32[64,1,256]{2,1,0:T(1,128)}), f32[64,1,256]{2,1,0:T(1,128)S(1)}, u32[]{:S(2)}, u32[]{:S(2)}) async-start(f32[64,1,256]{2,1,0:T(1,128)} %broadcast_in_dim.8), calls=%async_computation | async-start | bytes 131072 | tf_op jit(solution)/shard_map/all_to_all | solution.py:21
  37.4 10.2 %all-to-all-done = f32[64,1,256]{2,1,0:T(1,128)S(1)} async-done(((f32[64,1,256]{2,1,0:T(1,128)}), f32[64,1,256]{2,1,0:T(1,128)S(1)}, u32[]{:S(2)}, u32[]{:S(2)}) %all-to-all-start) | async-done | bytes 65568 | tf_op jit(solution)/shard_map/all_to_all | solution.py:21
  47.6 3.4 all-to-all-start.4
  52.7 3.1 all-to-all-done.4
  55.8 10.2 %all_to_all.75 = bf16[4,160,64]{1,2,0:T(8,128)(2,1)} all-to-all(bf16[4,160,64]{1,2,0:T(8,128)(2,1)S(1)} %copy.99), channel_id=1, replica_groups=mesh['expert'=4,'tensor_0'=4,'tensor_1'=8,'kv'=2] {'expert'}, dimensions={0} | all-to-all | bytes 163840 | tf_op jit(solution)/shard_map/all_to_all | solution.py:92
  66.0 3.4 all-to-all-start.2
  69.7 4.5 %all-to-all-done.2 = bf16[4,160,64]{1,2,0:T(8,128)(2,1)S(1)} async-done(((bf16[4,160,64]{1,2,0:T(8,128)(2,1)}), bf16[4,160,64]{1,2,0:T(8,128)(2,1)S(1)}, u32[]{:S(2)}, u32[]{:S(2)}) %all-to-all-start.2) | async-done | bytes 81952 | tf_op jit(solution)/shard_map/all_to_all | solution.py:94
  75.2 4.9 %pad_maximum_fusion = bf16[224,12288]{1,0:T(8,128)(2,1)} fusion(bf16[224,4096]{1,0:T(8,128)(2,1)S(1)} %bitcast.90, bf16[224,4096]{1,0:T(8,128)(2,1)} %bitcast.91, bf16[224,4096]{1,0:T(8,128)(2,1)} %bitcast.92), kind=kLoop, calls=%fused_computation.1 | loop fusion | flops 16515072 | bytes 11010048 | tf_op jit(solution)/shard_map/concatenate | solution.py:32
  80.2 72.0 %all-gather.6.cloned.1.call-done = bf16[2621440]{0:T(1024)(128)(2,1)} async-done(((bf16[81920]{0:T(1024)(128)(2,1)}), bf16[2621440]{0:T(1024)(128)(2,1)}) %all-gather.6.cloned.1.call-update) | async-done | bytes 5242896 | tf_op jit(solution)/shard_map/all_gather | solution.py:48
  152.2 6.4 %reshape.118 = bf16[32,81920]{1,0:T(8,128)(2,1)} reshape(bf16[2621440]{0:T(1024)(128)(2,1)} %all-gather.6.cloned.1.call-done) | data formatting | bytes 10485760 | tf_op jit(solution)/shard_map/all_gather | solution.py:48
  164.4 3.2 copy.106
  167.6 127.8 %all-gather.4.cloned.1.call-done = bf16[448,12288]{1,0:T(8,128)(2,1)} async-done(((bf16[224,12288]{1,0:T(8,128)(2,1)}), bf16[448,12288]{1,0:T(8,128)(2,1)}) %all-gather.4.cloned.1.call-update) | async-done | bytes 11010064 | tf_op jit(solution)/shard_map/all_gather | solution.py:33
  295.3 3.8 fusion.1
  299.1 4.6 %fusion.5 = f32[320,448]{1,0:T(8,128)} fusion(bf16[448,12288]{1,0:T(8,128)(2,1)} %all-gather.4.cloned.1.call-done, bf16[40,8,32,128]{3,2,1,0:T(8,128)(2,1)S(1)} %bitcast.88), kind=kOutput, calls=%fused_computation.7 | convolution fusion | flops 1174405120 | bytes 6864896 | tf_op jit(solution)/shard_map/dot_general | solution.py:101
  303.8 8.9 %fusion.3 = f32[4096,320]{0,1:T(8,128)} fusion(bf16[448,12288]{1,0:T(8,128)(2,1)} %all-gather.4.cloned.1.call-done, f32[320,448]{1,0:T(8,128)S(1)} %fusion.1, bf16[40,8,32,128]{3,2,1,0:T(8,128)(2,1)S(1)} %bitcast.89, f32[320,448]{1,0:T(8,128)} %fusion.5), kind=kOutput, calls=%fused_computation.5 | convolution fusion | flops 2350243840 | bytes 16433152 | tf_op jit(solution)/shard_map/dot_general | solution.py:116
  312.6 7.1 %fusion = bf16[4096,320]{0,1:T(8,128)(2,1)} fusion(f32[4096,320]{0,1:T(8,128)} %fusion.3, bf16[448,12288]{1,0:T(8,128)(2,1)} %all-gather.4.cloned.1.call-done, f32[320,448]{1,0:T(8,128)S(1)} %fusion.1, f32[320,448]{1,0:T(8,128)} %fusion.5), kind=kOutput, calls=%fused_computation.2 | convolution fusion | flops 1177886720 | bytes 12763136 | tf_op jit(solution)/shard_map/dot_general | solution.py:121
  319.8 36.2 %reduce-scatter.5.cloned.1.call-done = bf16[1024,320]{0,1:T(8,128)(2,1)} async-done(((bf16[4096,320]{0,1:T(8,128)(2,1)}), bf16[1024,320]{0,1:T(8,128)(2,1)}) %reduce-scatter.5.cloned.1.call-update) | async-done | bytes 655376 | tf_op jit(solution)/shard_map/reduce_scatter | solution.py:59
  358.2 33.3 %reduce-scatter.7.cloned.1.call-done = bf16[128,320]{1,0:T(8,128)(2,1)} async-done(((bf16[1024,320]{1,0:T(8,128)(2,1)}), bf16[128,320]{1,0:T(8,128)(2,1)}) %reduce-scatter.7.cloned.1.call-update) | async-done | bytes 81936
  393.3 3.6 all-to-all-start.5
  397.1 4.6 %all-to-all-done.5 = bf16[2,160,128]{1,0,2:T(2,128)(2,1)S(1)} async-done(((bf16[2,160,128]{1,0,2:T(2,128)(2,1)}), bf16[2,160,128]{1,0,2:T(2,128)(2,1)S(1)}, u32[]{:S(2)}, u32[]{:S(2)}) %all-to-all-start.5) | async-done | bytes 81952 | tf_op jit(solution)/shard_map/all_to_all | solution.py:125
  402.4 10.2 %all-to-all-start.6 = ((bf16[4,160,64]{1,2,0:T(8,128)(2,1)}), bf16[4,160,64]{1,2,0:T(8,128)(2,1)S(1)}, u32[]{:S(2)}, u32[]{:S(2)}) async-start(bf16[4,160,64]{1,2,0:T(8,128)(2,1)} %bitcast.17), calls=%async_computation.7 | async-start | bytes 262144 | tf_op jit(solution)/shard_map/all_to_all | solution.py:126
  412.6 3.6 all-to-all-done.6
  417.0 18.3 %all_to_all.76 = f32[64,1,256]{2,1,0:T(1,128)S(1)} all-to-all(f32[64,1,256]{2,1,0:T(1,128)S(1)} %broadcast_in_dim.11), channel_id=1, replica_groups=mesh['expert'=4,'tensor_0'=4,'tensor_1'=8,'kv'=2] {'tensor_0','tensor_1'..., dimensions={0} | all-to-all | bytes 131072 | tf_op jit(solution)/shard_map/all_to_all | solution.py:21
  (71 shorter events, 26.6 us)
Async XLA Ops:
  6.5 68.7 %copy-start.2 = (bf16[1,224,4096]{2,1,0:T(8,128)(2,1)S(1)}, bf16[1,224,4096]{2,1,0:T(8,128)(2,1)}, u32[]{:S(2)}) copy-start(bf16[1,224,4096]{2,1,0:T(8,128)(2,1)} %param.15) | copy-start | bytes 5505028
  12.7 10.8 %all-to-all-start.3 = ((bf16[4,160,64]{1,2,0:T(8,128)(2,1)}), bf16[4,160,64]{1,2,0:T(8,128)(2,1)}, u32[]{:S(2)}, u32[]{:S(2)}) async-start(bf16[4,160,64]{1,2,0:T(8,128)(2,1)} %copy.103), calls=%async_computation.3 | async-start | bytes 262144 | tf_op jit(solution)/shard_map/all_to_all | solution.py:93
  24.2 23.4 %all-to-all-start = ((f32[64,1,256]{2,1,0:T(1,128)}), f32[64,1,256]{2,1,0:T(1,128)S(1)}, u32[]{:S(2)}, u32[]{:S(2)}) async-start(f32[64,1,256]{2,1,0:T(1,128)} %broadcast_in_dim.8), calls=%async_computation | async-start | bytes 131072 | tf_op jit(solution)/shard_map/all_to_all | solution.py:21
  47.6 8.2 %all-to-all-start.4 = ((bf16[4,160,64]{1,2,0:T(8,128)(2,1)}), bf16[4,160,64]{1,2,0:T(8,128)(2,1)S(1)}, u32[]{:S(2)}, u32[]{:S(2)}) async-start(bf16[4,160,64]{1,2,0:T(8,128)(2,1)} %all-to-all-done.3), calls=%async_computation.4 | async-start | bytes 262144 | tf_op jit(solution)/shard_map/all_to_all | solution.py:95
  66.0 8.2 %all-to-all-start.2 = ((bf16[4,160,64]{1,2,0:T(8,128)(2,1)}), bf16[4,160,64]{1,2,0:T(8,128)(2,1)S(1)}, u32[]{:S(2)}, u32[]{:S(2)}) async-start(bf16[4,160,64]{1,2,0:T(8,128)(2,1)} %all_to_all.75), calls=%async_computation.2 | async-start | bytes 262144 | tf_op jit(solution)/shard_map/all_to_all | solution.py:94
  69.4 82.8 %all-gather.6.cloned.1.call-start = ((), (), s32[]{:S(2)}) async-start(), calls=%async_computation.12 | async-start | bytes 5406720 | tf_op jit(solution)/shard_map/all_gather | solution.py:48
  75.2 220.2 %all-gather.4.cloned.1.call-start = ((), (), s32[]{:S(2)}) async-start(), calls=%async_computation.10 | async-start | bytes 16515072 | tf_op jit(solution)/shard_map/all_gather | solution.py:33
  80.2 275.8 %reduce-scatter.5.cloned.1.call-start = ((), (), s32[]{:S(2)}) async-start(), calls=%async_computation.11 | async-start | bytes 3276800 | tf_op jit(solution)/shard_map/reduce_scatter | solution.py:59
  295.3 3.8 copy-start
  299.1 4.6 %copy-start.1 = (bf16[2,160,32,128]{3,2,1,0:T(8,128)(2,1)S(1)}, bf16[2,160,32,128]{3,2,1,0:T(8,128)(2,1)}, u32[]{:S(2)}) copy-start(bf16[2,160,32,128]{3,2,1,0:T(8,128)(2,1)} %copy.106) | copy-start | bytes 7864324
  319.7 92.8 %copy-start.4 = (s32[256,2]{0,1:T(2,128)S(1)}, s32[256,2]{0,1:T(2,128)}, u32[]{:S(2)}) copy-start(s32[256,2]{0,1:T(2,128)} %param.11) | copy-start | bytes 6148
  319.7 97.1 %copy-start.3 = (bf16[256,64]{0,1:T(8,128)(2,1)S(1)}, bf16[256,64]{0,1:T(8,128)(2,1)}, u32[]{:S(2)}) copy-start(bf16[256,64]{0,1:T(8,128)(2,1)} %param.8) | copy-start | bytes 98308
  319.8 71.8 %reduce-scatter.7.cloned.1.call-start = ((), (), s32[]{:S(2)}) async-start(), calls=%async_computation.13 | async-start | bytes 884736
  393.3 8.4 %all-to-all-start.5 = ((bf16[2,160,128]{1,0,2:T(2,128)(2,1)}), bf16[2,160,128]{1,0,2:T(2,128)(2,1)S(1)}, u32[]{:S(2)}, u32[]{:S(2)}) async-start(bf16[2,160,128]{1,0,2:T(2,128)(2,1)} %copy.107), calls=%async_computation.6 | async-start | bytes 262144 | tf_op jit(solution)/shard_map/all_to_all | solution.py:125
  402.4 13.8 %all-to-all-start.6 = ((bf16[4,160,64]{1,2,0:T(8,128)(2,1)}), bf16[4,160,64]{1,2,0:T(8,128)(2,1)S(1)}, u32[]{:S(2)}, u32[]{:S(2)}) async-start(bf16[4,160,64]{1,2,0:T(8,128)(2,1)} %bitcast.17), calls=%async_computation.7 | async-start | bytes 262144 | tf_op jit(solution)/shard_map/all_to_all | solution.py:126
Sparse Core Ops, SparseCore 0:
  75.3 76.8 all-gather.5
  154.0 141.2 all-gather.3
  319.9 36.0 reduce-scatter.4
  358.4 33.1 reduce-scatter.6
where the time goes:
time: 444 us; the launch traced here: 443 us
  waiting for transfers between devices  298 us (67%)
  starting transfers between devices  40.4 us (9%)
  blocking collectives  28.4 us (6%)
  local copies, waits for them, and re-layouts  26.2 us (6%)
  matrix products  25.6 us (6%)
  between operations  13.4 us (3%)
  other arithmetic  10.4 us (2%)
    all_gather x1, waiting for transfers between devices, in_one_piece(): lax.all_gather(both, axis, axis=dim, tiled=True)  128 us
    all_gather x1, waiting for transfers between devices, gather_packed(): lines, at, finished = (lax.all_gather(vector, axis), 0, [])  72 us
    reduce_scatter x1, waiting for transfers between devices, own_rows(): subtotal = lax.psum_scatter(subtotal, axis, scatter_dimension=0, tiled=True)  36.2 us
    unnamed x5, waiting for transfers between devices  33.4 us
    all_to_all x1, blocking collectives, from_everyone(): lax.all_to_all(jnp.broadcast_to(value[None], (length, *value.shape)), axi...  18.3 us
    all_to_all x1, starting transfers between devices, from_everyone(): lax.all_to_all(jnp.broadcast_to(value[None], (length, *value.shape)), axi...  12.5 us
    all_to_all x1, starting transfers between devices, shards(): lax.all_to_all(returned, 'expert', split_axis=0, concat_axis=0, tiled=True)  10.2 us
    all_to_all x1, waiting for transfers between devices, from_everyone(): lax.all_to_all(jnp.broadcast_to(value[None], (length, *value.shape)), axi...  10.2 us
  transfers between devices with their start and end apart: 10, of which 10 were waited for; matrix products, arithmetic and copies ran while one was open for 5% of the time, Pallas kernels for 0%

commit v1 on v0

v1 whole, which is shorter than its diff:
```python
import jax
import jax.numpy as jnp
from jax import lax
from jax.experimental import pallas as pl
from jax.experimental.pallas import tpu as pltpu
from jax.sharding import Mesh
from jax.sharding import PartitionSpec as P

D = 4096
CAP = 160
EPS = 1e-05
GROUPS = 4
NY = 4
NZ = 8
LANES = 128
ROWS = GROUPS * CAP
HALF = ROWS // 2
GAIN_ROWS = 16
MINE = CAP // 2
XROWS = HALF + GAIN_ROWS
SPLIT = 144
PADDED = 384
PART = HALF // 2
EXTRA = 16
TENSOR_KV = ("tensor_0", "tensor_1", "kv")
LINE = ("expert", "kv")
F32 = jnp.float32
BF16 = jnp.bfloat16
NT = (((1,), (1,)), ((), ()))
TN = (((0,), (0,)), ((), ()))
VMEM_LIMIT = 60 * 1024 * 1024


def call(kernel, outs, us, scratch=()):
    return pl.pallas_call(
        kernel,
        out_shape=[jax.ShapeDtypeStruct(s, t) for s, t in outs],
        scratch_shapes=list(scratch),
        compiler_params=pltpu.CompilerParams(vmem_limit_bytes=VMEM_LIMIT),
        cost_estimate=pl.CostEstimate(flops=us * 1_000_000_000, bytes_accessed=0, transcendentals=0),
    )


def slots_of(ids):
    tokens = ids.shape[1]
    first, second = ids[0:1], ids[1:2]
    groups = lax.broadcasted_iota(jnp.int32, (8, tokens), 0)
    named = jnp.where(first == groups, 1.0, 0.0) + jnp.where(second == groups, 1.0, 0.0)
    earlier = jnp.where(
        lax.broadcasted_iota(jnp.int32, (tokens, tokens), 0)
        < lax.broadcasted_iota(jnp.int32, (tokens, tokens), 1),
        1.0,
        0.0,
    ).astype(BF16)
    before = jnp.dot(named.astype(BF16), earlier, preferred_element_type=F32).astype(jnp.int32)
    at_first = jnp.sum(jnp.where(first == groups, before, 0), axis=0, keepdims=True)
    at_second = jnp.sum(jnp.where(second == groups, before, 0), axis=0, keepdims=True)
    return first * CAP + at_first, second * CAP + at_second


def dispatch_kernel(ids_ref, probs_ref, x_ref, grad_ref, gain_ref, out_ref):
    one, two = slots_of(ids_ref[...])
    tokens = ids_ref.shape[1]
    rows = lax.broadcasted_iota(jnp.int32, (ROWS, tokens), 0)
    x = x_ref[...]
    grad = grad_ref[...].astype(F32)
    probs = probs_ref[...]
    terms = []
    for slot, k in ((one, 0), (two, 1)):
        table = jnp.where(rows == slot, 1.0, 0.0).astype(BF16)
        values = jnp.concatenate([(grad * probs[k : k + 1]).astype(BF16), x], axis=0)
        terms.append(lax.dot_general(table, values, NT, preferred_element_type=F32))
    routed = terms[0] + terms[1]
    low = lax.broadcasted_iota(jnp.int32, (MINE, LANES), 1) < LANES // 2
    gain = jnp.broadcast_to(gain_ref[0:1, :].astype(F32), (MINE, LANES))
    for e in range(GROUPS):
        first = routed[e * CAP : e * CAP + MINE]
        second = routed[e * CAP + MINE : (e + 1) * CAP]
        for k in range(2):
            top = first if k == 0 else jnp.where(low, first, second)
            out_ref[e, k, pl.ds(0, MINE), :] = top.astype(BF16)
            out_ref[e, k, pl.ds(MINE, MINE), :] = jnp.where(low, second, gain).astype(BF16)


def assemble_kernel(got_ref, a_ref, b_ref):
    grads = []
    for g in range(GROUPS):
        low, high = got_ref[g, 0].astype(F32), got_ref[g, 1].astype(F32)
        x = jnp.concatenate([low[:, 64:], high[:, 64:]], axis=1).astype(BF16)
        grads.append(jnp.concatenate([low[:, :64], high[:, :64]], axis=1).astype(BF16))
        a_ref[pl.ds(g * MINE, MINE), :] = x[:MINE]
        if g == 0:
            a_ref[pl.ds(HALF, GAIN_ROWS), :] = x[MINE : MINE + GAIN_ROWS]
    a_ref[pl.ds(XROWS, SPLIT), :] = grads[0][:SPLIT]
    b_ref[pl.ds(0, CAP - SPLIT), :] = grads[0][SPLIT:]
    for g in range(1, GROUPS):
        b_ref[pl.ds(g * CAP - SPLIT, CAP), :] = grads[g]


def block(y, z):
    return pl.ds(pl.multiple_of((y * NZ + z) * LANES, LANES), LANES)


def column(a, b):
    y = lax.rem(lax.axis_index("tensor_0") + a, NY)
    z = lax.rem(lax.axis_index("tensor_1") + b, NZ)
    return block(y, z)


def a_piece(refs, a, b):
    x0, x1, x3, lo, hi = refs
    if a == 2:
        return (lo, b) if b < NZ // 2 else (hi, b - NZ // 2)
    return (x0, x1, None, x3)[a], b


def b_piece(refs, a, b):
    if b == NZ // 2:
        return refs[NZ - 1 + a // 2], a % 2
    return refs[b if b < NZ // 2 else b - 1], a


PLACES = [(a, b) for a in range(NY) for b in range(NZ)]


def act_kernel(*refs):
    a_refs, b_refs = refs[:5], refs[5:14]
    wd_ref, mine_ref, theirs_ref, grad_ref, act_ref = refs[14:]
    for a, b in PLACES:
        ref, at = a_piece(a_refs, a, b)
        grad_ref[pl.ds(0, SPLIT), column(a, b)] = ref[at, pl.ds(XROWS, SPLIT), :]
        ref, at = b_piece(b_refs, a, b)
        grad_ref[pl.ds(SPLIT, ROWS - SPLIT), column(a, b)] = ref[at]

    @pl.loop(0, 2)
    def _(r):
        rows = pl.ds(pl.multiple_of(r * HALF, HALF), HALF)
        act_ref[rows, :] = lax.dot_general(grad_ref[rows, :], wd_ref[...], NT, preferred_element_type=F32)

    kv = lax.axis_index("kv")
    for g in range(GROUPS):
        here = pl.ds(g * MINE, MINE)
        mine_ref[here, :] = act_ref[pl.ds(pl.multiple_of(g * CAP + kv * MINE, 16), MINE), :]
        theirs_ref[here, :] = act_ref[pl.ds(pl.multiple_of(g * CAP + (1 - kv) * MINE, 16), MINE), :].astype(BF16)


def to_row(column_ref, row_ref):
    for r in range(PADDED // LANES):
        rows = pl.ds(r * LANES, LANES)
        row_ref[:, rows] = jnp.transpose(column_ref[rows, :])[0:1]


def forward_kernel(*refs):
    a_refs = refs[:5]
    wg_ref, wu_ref, wgp_ref, wup_ref, gate_ref, up_ref, gatep_ref, upp_ref, inv_ref, xn_ref, column_ref = refs[5:]

    @pl.loop(0, HALF // 64)
    def _(r):
        rows = pl.ds(pl.multiple_of(r * 64, 64), 64)
        total = jnp.zeros((64, LANES), F32)
        for a, b in PLACES:
            ref, at = a_piece(a_refs, a, b)
            v = ref[at, rows, :].astype(F32)
            total = total + v * v
        inv = lax.rsqrt(jnp.sum(total, axis=1, keepdims=True) / D + EPS)
        column_ref[rows, :] = jnp.broadcast_to(inv, (64, LANES))
        for a, b in PLACES:
            ref, at = a_piece(a_refs, a, b)
            gain = ref[at, pl.ds(HALF, GAIN_ROWS), :].astype(F32)[0:1]
            xn_ref[rows, column(a, b)] = (ref[at, rows, :].astype(F32) * inv * gain).astype(BF16)

    column_ref[pl.ds(HALF, PADDED - HALF), :] = jnp.zeros((PADDED - HALF, LANES), F32)
    to_row(column_ref, inv_ref)
    x = xn_ref[...]
    for w_ref, out_ref in ((wg_ref, gate_ref), (wu_ref, up_ref), (wgp_ref, gatep_ref), (wup_ref, upp_ref)):
        out_ref[...] = lax.dot_general(x, w_ref[...], NT, preferred_element_type=F32)


def split3(value):
    terms = []
    for _ in range(3):
        terms.append(value.astype(BF16))
        value = value - terms[-1].astype(F32)
    return terms


def back_products(gs, ws, rows, a, outs):
    y = lax.rem(lax.axis_index("tensor_0") + a, NY)
    for z in range(0, NZ, 2):
        at = pl.ds(pl.multiple_of((y * NZ + z) * LANES, 2 * LANES), 2 * LANES)
        total = 0.0
        for g_ref, w_ref in zip(gs, ws):
            total = total + jnp.dot(g_ref[rows, :], w_ref[:, at], preferred_element_type=F32)
        total = total.astype(BF16)
        outs[a][z, pl.ds(0, PART), :] = total[:, :LANES]
        outs[a][z + 1, pl.ds(0, PART), :] = total[:, LANES:]


def carried(rows):
    terms = [t.astype(F32) for t in split3(rows)]
    return jnp.concatenate(terms + [jnp.zeros((7, LANES), F32)], axis=0).astype(BF16)


def gathered_up(carried_sum):
    return carried_sum[0:3] + carried_sum[3:6] + carried_sum[6:9]


def first_kernel(*refs):
    gate_ref, up_ref, gatep_ref, upp_ref, act_ref, actp_ref, *ws = refs[:10]
    gg_ref, ug_ref, ggp_ref, ugp_ref, *outs, column_ref = refs[10:]
    sums = 0.0
    for gate_in, up_in, act_in, gg_out, ug_out in (
        (gate_ref, up_ref, act_ref, gg_ref, ug_ref),
        (gatep_ref, upp_ref, actp_ref, ggp_ref, ugp_ref),
    ):
        gate, up, act = gate_in[...], up_in[...], act_in[...].astype(F32)
        sigma = jax.nn.sigmoid(gate)
        gg = (act * up * sigma * (1.0 + gate * (1.0 - sigma))).astype(BF16)
        ug = (act * (gate * sigma)).astype(BF16)
        gg_out[...] = gg
        ug_out[...] = ug
        sums = sums + jnp.sum(gg.astype(F32) * gate + ug.astype(F32) * up, axis=1, keepdims=True)
    column_ref[pl.ds(0, HALF), :] = jnp.broadcast_to(sums, (HALF, LANES))
    column_ref[pl.ds(HALF, PADDED - HALF), :] = jnp.zeros((PADDED - HALF, LANES), F32)
    rows = [jnp.transpose(column_ref[pl.ds(r * LANES, LANES), :])[0:1] for r in range(PADDED // LANES)]
    projection = carried(jnp.concatenate(rows, axis=0))
    for a in (2, 1, 3, 0):
        back_products((gg_ref, ug_ref, ggp_ref, ugp_ref), ws, pl.ds(0, PART), a, outs)
        for z in range(NZ):
            outs[a][z, pl.ds(PART, EXTRA), :] = projection


def second_kernel(gg_ref, ug_ref, ggp_ref, ugp_ref, wg_ref, wu_ref, wgp_ref, wup_ref, *outs):
    for a in (2, 1, 3, 0):
        back_products(
            (gg_ref, ug_ref, ggp_ref, ugp_ref), (wg_ref, wu_ref, wgp_ref, wup_ref), pl.ds(PART, PART), a, outs
        )


def sum_first_kernel(*refs):
    *shares, out_ref = refs
    for z in range(NZ):
        total = 0.0
        for ref in shares:
            total = total + ref[z].astype(F32)
        out_ref[z, pl.ds(0, PART), :] = total[:PART].astype(BF16)
        out_ref[z, pl.ds(PART, EXTRA), :] = carried(gathered_up(total[PART:]))


def sum_second_kernel(*refs):
    *shares, out_ref = refs
    for z in range(NZ):
        total = 0.0
        for ref in shares:
            total = total + ref[z].astype(F32)
        out_ref[z] = total.astype(BF16)


def finish_kernel(first_ref, second_ref, inv_ref, out_ref):
    first, second = first_ref[0].astype(F32), second_ref[0].astype(F32)
    for z in range(1, NZ):
        first = first + first_ref[z].astype(F32)
        second = second + second_ref[z].astype(F32)
    rows = gathered_up(first[PART:])
    projection = jnp.concatenate([rows[r : r + 1] for r in range(PADDED // LANES)], axis=1)
    inv = inv_ref[...]
    terms = split3(inv * inv * projection / D) + split3(inv)
    terms = jnp.concatenate([t.astype(F32) for t in terms] + [jnp.zeros((10, PADDED), F32)], axis=0)
    for b in range(GROUPS):
        here = (first, second)[b // 2][(b % 2) * MINE : (b % 2 + 1) * MINE].astype(BF16)
        scalars = terms[:, b * MINE : b * MINE + LANES]
        for k in range(2):
            out_ref[2 * b + k, pl.ds(0, MINE), :] = here
            out_ref[2 * b + k, pl.ds(MINE, EXTRA), :] = scalars.astype(BF16)


def combine_kernel(got_ref, ids_ref, x_ref, gain_ref, out_ref):
    one, two = slots_of(ids_ref[...])
    tokens = ids_ref.shape[1]
    rows = lax.broadcasted_iota(jnp.int32, (ROWS, tokens), 0)
    table = jnp.where((rows == one) | (rows == two), 1.0, 0.0).astype(BF16)
    slot_grad = jnp.concatenate([got_ref[i, pl.ds(0, MINE), :] for i in range(2 * GROUPS)], axis=0)
    both = lax.dot_general(slot_grad, table, TN, preferred_element_type=F32)
    token_grad = jnp.where(lax.axis_index("kv") == 0, both[:64], both[64:])
    scalars = jnp.concatenate(
        [got_ref[i, pl.ds(MINE, EXTRA), :].astype(F32)[:, :MINE] for i in range(2 * GROUPS)], axis=1
    )
    found = jnp.dot(scalars.astype(BF16), table, preferred_element_type=F32)
    coefficient = found[0:1] + found[1:2] + found[2:3]
    inverse_rms = 0.5 * (found[3:4] + found[4:5] + found[5:6])
    gain = jnp.transpose(gain_ref[...].astype(F32))[:, 0:1]
    x = x_ref[...].astype(F32)
    out_ref[...] = (inverse_rms * (token_grad * gain) - x * coefficient).astype(BF16)


def shift(value, axis, by):
    n = lax.axis_size(axis)
    return lax.ppermute(value, axis, [(i, (i + by) % n) for i in range(n)])


def gather_ring(value, axis, cut, meet=None):
    n = lax.axis_size(axis)
    got = {0: value}
    right = left = value
    for step in range(1, n // 2):
        right, left = shift(right, axis, 1), shift(left, axis, -1)
        got[n - step], got[step] = right, left
    if meet is not None:
        right, left, meet = lax.optimization_barrier((right, left, meet))
    far = (shift(right[:cut], axis, 1), shift(left[cut:], axis, -1))
    return got, far, meet


def shards(residual_stream, grad_output, norm_gain, expert_ids, gate_probs, w_gate, w_up, w_down):
    wg, wu, wd = w_gate[0], w_up[0], w_down[0]
    ids, probs = expert_ids.T, gate_probs.T
    x_t, grad_t = residual_stream.T, grad_output.T
    gain_rows = jnp.broadcast_to(jnp.concatenate([norm_gain, norm_gain])[None], (GAIN_ROWS, LANES))
    hidden = wg.shape[0]

    with jax.named_scope("weights"):
        wgp = shift(wg, "kv", 1)

    with jax.named_scope("dispatch"):
        [routed] = call(dispatch_kernel, [((GROUPS, 2, CAP, LANES), BF16)], 2)(
            ids, probs, x_t, grad_t, gain_rows
        )
        got = lax.all_to_all(routed.reshape(2 * GROUPS, CAP, LANES), LINE, 0, 0, tiled=True)
        piece_a, piece_b = call(
            assemble_kernel, [((XROWS + SPLIT, LANES), BF16), ((ROWS - SPLIT, LANES), BF16)], 2
        )(got.reshape(GROUPS, 2, CAP, LANES))

    with jax.named_scope("gather_a"):
        z_got, z_far, wgp = gather_ring(piece_a, "tensor_1", (XROWS + SPLIT) // 2, wgp)
        later, wgp = lax.optimization_barrier((wu, wgp))
        wup = shift(later, "kv", 1)
        z_got[4] = jnp.concatenate(z_far, axis=0)
        line = jnp.stack([z_got[b] for b in range(NZ)])
        a_got, a_far, wup = gather_ring(line, "tensor_0", NZ // 2, wup)
        a_refs = (a_got[0], a_got[1], a_got[3], *a_far)
    with jax.named_scope("gather_b"):
        line = jnp.stack([piece_b] + [shift(piece_b, "tensor_0", -a) for a in (1, 2, 3)])
        line, _ = lax.optimization_barrier((line, z_got[2]))
        b_got, b_far, _ = gather_ring(line, "tensor_1", NY // 2)
        b_refs = (*[b_got[b] for b in range(NZ) if b != 4], *b_far)

    with jax.named_scope("act"):
        act, theirs = call(
            act_kernel,
            [((HALF, hidden), F32), ((HALF, hidden), BF16)],
            7,
            [pltpu.VMEM((ROWS, D), BF16), pltpu.VMEM((ROWS, hidden), F32)],
        )(*a_refs, *b_refs, wd)
        actp = shift(theirs, "kv", 1)
    with jax.named_scope("forward"):
        gate, up, gatep, upp, inv = call(
            forward_kernel,
            [((HALF, hidden), F32)] * 4 + [((1, PADDED), F32)],
            8,
            [pltpu.VMEM((HALF, D), BF16), pltpu.VMEM((PADDED, LANES), F32)],
        )(*a_refs, wg, wu, wgp, wup)
    with jax.named_scope("back"):
        gg, ug, ggp, ugp, *first = call(
            first_kernel,
            [((HALF, hidden), BF16)] * 4 + [((NZ, PART + EXTRA, LANES), BF16)] * NY,
            5,
            [pltpu.VMEM((PADDED, LANES), F32)],
        )(gate, up, gatep, upp, act, actp, wg, wu, wgp, wup)
        second = call(second_kernel, [((NZ, PART, LANES), BF16)] * NY, 4)(
            gg, ug, ggp, ugp, wg, wu, wgp, wup
        )
    with jax.named_scope("scatter"):
        own_first, own_second = lax.optimization_barrier((first[0], second[0]))
        first = [own_first] + [shift(first[a], "tensor_0", a) for a in (2, 1, 3)]
        second = [own_second] + [shift(second[a], "tensor_0", a) for a in (2, 1, 3)]
        [first] = call(sum_first_kernel, [((NZ, PART + EXTRA, LANES), BF16)], 3)(*first)
        first = lax.all_to_all(first, "tensor_1", 0, 0, tiled=True)
        [second] = call(sum_second_kernel, [((NZ, PART, LANES), BF16)], 3)(*second)
        first, second = lax.optimization_barrier((first, second))
        second = lax.all_to_all(second, "tensor_1", 0, 0, tiled=True)

    with jax.named_scope("combine"):
        [pieces] = call(finish_kernel, [((2 * GROUPS, MINE + EXTRA, LANES), BF16)], 2)(first, second, inv)
        got = lax.all_to_all(pieces, LINE, 0, 0, tiled=True)
        gain_square = jnp.broadcast_to(norm_gain[None], (LANES, norm_gain.shape[0]))
        [out] = call(combine_kernel, [(x_t.shape, BF16)], 2)(
            got, ids, x_t, gain_square
        )
    return out.T


def solution(mesh):
    torus = Mesh(
        mesh.devices.reshape(mesh.shape["expert"], NY, NZ, mesh.shape["kv"]),
        ("expert", "tensor_0", "tensor_1", "kv"),
    )
    return jax.shard_map(
        shards,
        mesh=torus,
        in_specs=(
            P("expert", TENSOR_KV),
            P("expert", TENSOR_KV),
            P(TENSOR_KV),
            P("expert", None),
            P("expert", None),
            P("expert", TENSOR_KV, None),
            P("expert", TENSOR_KV, None),
            P("expert", TENSOR_KV, None),
        ),
        out_specs=P("expert", TENSOR_KV),
        check_vma=False,
    )
```

time: 444 us -> 248 us (0.56)
  waiting for transfers between devices: 298 us -> 70.9 us
  blocking collectives: 28.4 us -> 71.3 us
  Pallas kernels: 0 us -> 42.1 us
  matrix products: 25.6 us -> 0 us
  local copies, waits for them, and re-layouts: 26.2 us -> 7.52 us
  starting transfers between devices: 40.4 us -> 53.6 us
  between operations: 13.4 us -> 0.37 us
  other arithmetic: 10.4 us -> 1.79 us
    all_gather x2 -> x0, waiting for transfers between devices: 200 us -> none  [the longest x1 128 us: in_one_piece(): lax.all_gather(both, axis, axis=dim, tiled=True)]
    ppermute x0 -> x32, waiting for transfers between devices: none -> 70.9 us  [shift(): return lax.ppermute(value, axis, [(i, (i + by) % n) for i in range(n)])]
    ppermute x0 -> x32, starting transfers between devices: none -> 50.1 us  [shift(): return lax.ppermute(value, axis, [(i, (i + by) % n) for i in range(n)])]
    all_to_all x2 -> x3, blocking collectives: 28.4 us -> 71.3 us  [the longest x1 41 us: shards(): lax.all_to_all(routed.reshape(2 * GROUPS, CAP, LANES), LINE, 0, 0, tiled=...]
    pallas_call x0 -> x10, Pallas kernels: none -> 42.1 us  [the longest x1 9.47 us: shards(): call(forward_kernel, [((HALF, hidden), F32)] * 4 + [((1, PADDED), F32)],...]
    all_to_all x6 -> x1, starting transfers between devices: 40.2 us -> 3.44 us  [shards(): first = lax.all_to_all(first, 'tensor_1', 0, 0, tiled=True)]
    reduce_scatter x1 -> x0, waiting for transfers between devices: 36.2 us -> none  [own_rows(): subtotal = lax.psum_scatter(subtotal, axis, scatter_dimension=0, tiled=True)]
    unnamed x5 -> x0, waiting for transfers between devices: 33.4 us -> none
  transfers between devices with their start and end apart: 10 -> 33, of which waited for: 10 -> 13; matrix products, arithmetic and copies ran while one was open for 5% -> 1% of each run, Pallas kernels for 0% -> 9%
where the time goes in v1:
time: 248 us
  blocking collectives  71.3 us (29%)
  waiting for transfers between devices  70.9 us (29%)
  starting transfers between devices  53.6 us (22%)
  Pallas kernels  42.1 us (17%)
  local copies, waits for them, and re-layouts  7.52 us (3%)
    ppermute x32, waiting for transfers between devices, shift(): return lax.ppermute(value, axis, [(i, (i + by) % n) for i in range(n)])  70.9 us
    ppermute x32, starting transfers between devices, shift(): return lax.ppermute(value, axis, [(i, (i + by) % n) for i in range(n)])  50.1 us
    all_to_all x1, blocking collectives, shards(): lax.all_to_all(routed.reshape(2 * GROUPS, CAP, LANES), LINE, 0, 0, tiled=...  41 us
    all_to_all x1, blocking collectives, shards(): second = lax.all_to_all(second, 'tensor_1', 0, 0, tiled=True)  17.1 us
    all_to_all x1, blocking collectives, shards(): got = lax.all_to_all(pieces, LINE, 0, 0, tiled=True)  13.2 us
    pallas_call x1, Pallas kernels, shards(): call(forward_kernel, [((HALF, hidden), F32)] * 4 + [((1, PADDED), F32)],...  9.47 us
    pallas_call x1, Pallas kernels, shards(): call(act_kernel, [((HALF, hidden), F32), ((HALF, hidden), BF16)], 7, [plt...  7.98 us
    pallas_call x1, Pallas kernels, shards(): call(first_kernel, [((HALF, hidden), BF16)] * 4 + [((NZ, PART + EXTRA, LA...  6.73 us
  transfers between devices with their start and end apart: 33, of which 13 were waited for; matrix products, arithmetic and copies ran while one was open for 1% of the time, Pallas kernels for 9%

profile of v1, /device:TPU:1, one launch (start us, length us, event | category | flops | bytes accessed | tf_op | source)
XLA Modules:
  0.0 247.5 jit_solution(3271792462821104976)
XLA Ops:
  0.0 3.6 %collective-permute-start.6 = (bf16[224,4096]{1,0:T(8,128)(2,1)}, bf16[224,4096]{1,0:T(8,128)(2,1)S(1)}, u32[]{:S(2)}, u32[]{:S(2)}) collective-permute-start(bf16[224,4096]{1,0:T(8,128)(2,1)} %bitcast.39), channel_id=1, source_target_pairs={{0,1},{1,0},{2,3},{3,2},{4,5},{5,4},{6,7},{7,6},{8,9},{9,8},{10,11... | collective-permute-start | bytes 5505032 | tf_op jit(solution)/shard_map/weights/ppermute | solution.py:298
  7.0 41.0 %all_to_all.20 = bf16[8,160,128]{2,1,0:T(8,128)(2,1)} all-to-all(bf16[8,160,128]{2,1,0:T(8,128)(2,1)} %bitcast.33), channel_id=1, replica_groups=mesh['expert'=4,'tensor_0'=4,'tensor_1'=8,'kv'=2] {'expert','kv'}, dimensions={0} | all-to-all | bytes 655360 | tf_op jit(solution)/shard_map/dispatch/all_to_all | solution.py:328
  49.8 5.7 %collective-permute-start = (bf16[480,128]{1,0:T(8,128)(2,1)}, bf16[480,128]{1,0:T(8,128)(2,1)S(1)}, u32[]{:S(2)}, u32[]{:S(2)}) collective-permute-start(bf16[480,128]{1,0:T(8,128)(2,1)} %get-tuple-element.39), channel_id=1, source_target_pairs={{0,14},{2,0},{4,2},{6,4},{8,6},{10,8},{12,10},{14,12},{1,15},{3,1}... | collective-permute-start | bytes 368648 | tf_op jit(solution)/shard_map/gather_a/ppermute | solution.py:298
  55.4 2.7 %collective-permute-start.14 = (bf16[496,128]{1,0:T(8,128)(2,1)}, bf16[496,128]{1,0:T(8,128)(2,1)S(1)}, u32[]{:S(2)}, u32[]{:S(2)}) collective-permute-start(bf16[496,128]{1,0:T(8,128)(2,1)} %get-tuple-element.52), channel_id=1, source_target_pairs={{0,48},{16,0},{32,16},{48,32},{1,49},{17,1},{33,17},{49,33},{2,50}... | collective-permute-start | bytes 380936 | tf_op jit(solution)/shard_map/gather_b/ppermute | solution.py:298
  63.7 3.3 %collective-permute-done.16 = bf16[496,128]{1,0:T(8,128)(2,1)S(1)} collective-permute-done((bf16[496,128]{1,0:T(8,128)(2,1)}, bf16[496,128]{1,0:T(8,128)(2,1)S(1)}, u32[]{:S(2)}, u32[]{:S(2)}) %collective-permute-start.16) | collective-permute-done | bytes 127008 | tf_op jit(solution)/shard_map/gather_b/ppermute | solution.py:298
  72.2 10.2 %collective-permute-done.2 = bf16[480,128]{1,0:T(8,128)(2,1)S(1)} collective-permute-done((bf16[480,128]{1,0:T(8,128)(2,1)S(1)}, bf16[480,128]{1,0:T(8,128)(2,1)S(1)}, u32[]{:S(2)}, u32[]{:S(2)}) %collective-permute-start.2) | collective-permute-done | bytes 122912 | tf_op jit(solution)/shard_map/gather_a/ppermute | solution.py:298
  86.2 3.0 %collective-permute-start.11 = (bf16[224,4096]{1,0:T(8,128)(2,1)S(1)}, bf16[224,4096]{1,0:T(8,128)(2,1)S(1)}, u32[]{:S(2)}, u32[]{:S(2)}) collective-permute-start(bf16[224,4096]{1,0:T(8,128)(2,1)S(1)} %bitcast.46), channel_id=1, source_target_pairs={{0,1},{1,0},{2,3},{3,2},{4,5},{5,4},{6,7},{7,6},{8,9},{9,8},{10,11... | collective-permute-start | bytes 5505032 | tf_op jit(solution)/shard_map/gather_a/ppermute | solution.py:298
  95.0 7.9 %collective-permute-done.21.refs_10_ = bf16[4,496,128]{2,1,0:T(8,128)(2,1)S(1)} collective-permute-done((bf16[4,496,128]{2,1,0:T(8,128)(2,1)S(1)}, bf16[4,496,128]{2,1,0:T(8,128)(2,1)S(1)}, u32[]{:S(2)}, u32[]{:S(2)}) %collective-permute-start.21) | collective-permute-done | bytes 507936 | tf_op jit(solution)/shard_map/gather_b/ppermute | solution.py:298
  103.0 2.7 %collective-permute-start.19 = (bf16[4,496,128]{2,1,0:T(8,128)(2,1)S(1)}, bf16[4,496,128]{2,1,0:T(8,128)(2,1)S(1)}, u32[]{:S(2)}, u32[]{:S(2)}) collective-permute-start(bf16[4,496,128]{2,1,0:T(8,128)(2,1)S(1)} %collective-permute-done.18.refs_7_), channel_id=1, source_target_pairs={{0,14},{2,0},{4,2},{6,4},{8,6},{10,8},{12,10},{14,12},{1,15},{3,1}... | collective-permute-start | bytes 1523720 | tf_op jit(solution)/shard_map/gather_b/ppermute | solution.py:298
  105.7 5.3 %collective-permute-done.10.refs_2_ = bf16[8,480,128]{2,1,0:T(8,128)(2,1)S(1)} collective-permute-done((bf16[8,480,128]{2,1,0:T(8,128)(2,1)S(1)}, bf16[8,480,128]{2,1,0:T(8,128)(2,1)S(1)}, u32[]{:S(2)}, u32[]{:S(2)}) %collective-permute-start.10) | collective-permute-done | bytes 983072 | tf_op jit(solution)/shard_map/gather_a/ppermute | solution.py:298
  111.0 15.3 %collective-permute-done.11.refs_8_.refs_9_.wup_ref = bf16[224,4096]{1,0:T(8,128)(2,1)S(1)} collective-permute-done((bf16[224,4096]{1,0:T(8,128)(2,1)S(1)}, bf16[224,4096]{1,0:T(8,128)(2,1)S(1)}, u32[]{:S(2)}, u32[]{:S(2)}) %collective-permute-start.11) | collective-permute-done | bytes 1835040 | tf_op jit(solution)/shard_map/gather_a/ppermute | solution.py:298
  126.5 2.7 %collective-permute-start.13 = (bf16[4,480,128]{2,1,0:T(8,128)(2,1)S(1)}, bf16[4,480,128]{2,1,0:T(8,128)(2,1)S(1)}, u32[]{:S(2)}, u32[]{:S(2)}) collective-permute-start(bf16[4,480,128]{2,1,0:T(8,128)(2,1)S(1)} %slice.21), channel_id=1, source_target_pairs={{0,48},{16,0},{32,16},{48,32},{1,49},{17,1},{33,17},{49,33},{2,50}... | collective-permute-start | bytes 1474568 | tf_op jit(solution)/shard_map/gather_a/ppermute | solution.py:298
  132.1 3.9 %collective-permute-done.23.refs_12_ = bf16[2,496,128]{2,1,0:T(8,128)(2,1)S(1)} collective-permute-done((bf16[2,496,128]{2,1,0:T(8,128)(2,1)S(1)}, bf16[2,496,128]{2,1,0:T(8,128)(2,1)S(1)}, u32[]{:S(2)}, u32[]{:S(2)}) %collective-permute-start.23) | collective-permute-done | bytes 253984 | tf_op jit(solution)/shard_map/gather_b/ppermute | solution.py:298
  138.1 8.0 %act.1 = (f32[320,224]{1,0:T(8,128)}, bf16[320,224]{1,0:T(8,128)(2,1)}) custom-call(bf16[8,480,128]{2,1,0:T(8,128)(2,1)} %copy-done.6, bf16[8,480,128]{2,1,0:T(8,128)(2,1)} %copy-done.3, bf16[8,480,128]{2,1,0:T(8,128)(2,1)} %copy-done.2, bf16[4,480,128]{2,1,0:T(8,128)(2,1)} %copy-done.15, bf16[4,480,128]{2,1,0:T(8,128)(2,1)} %copy-done.16, ...), custom_call_target="tpu_custom_call" | custom-call | flops 7000000000 | tf_op jit(solution)/shard_map/act/pallas_call | solution.py:348
  146.1 3.2 %collective-permute-start.25 = (bf16[320,224]{1,0:T(8,128)(2,1)}, bf16[320,224]{1,0:T(8,128)(2,1)S(1)}, u32[]{:S(2)}, u32[]{:S(2)}) collective-permute-start(bf16[320,224]{1,0:T(8,128)(2,1)} %get-tuple-element.55), channel_id=1, source_target_pairs={{0,1},{1,0},{2,3},{3,2},{4,5},{5,4},{6,7},{7,6},{8,9},{9,8},{10,11... | collective-permute-start | bytes 430088 | tf_op jit(solution)/shard_map/act/ppermute | solution.py:298
  149.3 9.5 %forward.1 = (f32[320,224]{1,0:T(8,128)}, f32[320,224]{1,0:T(8,128)}, f32[320,224]{1,0:T(8,128)}, f32[320,224]{1,0:T(8,128)}, f32[1,384]{1,0:T(1,128)}) custom-call(bf16[8,480,128]{2,1,0:T(8,128)(2,1)} %copy-done.6, bf16[8,480,128]{2,1,0:T(8,128)(2,1)} %copy-done.3, bf16[8,480,128]{2,1,0:T(8,128)(2,1)} %copy-done.2, bf16[4,480,128]{2,1,0:T(8,128)(2,1)} %copy-done.15, ...), custom_call_target="tpu_custom_call" | custom-call | flops 8000000000 | tf_op jit(solution)/shard_map/forward/pallas_call | solution.py:356
  159.4 6.7 %back.2 = (bf16[320,224]{1,0:T(8,128)(2,1)}, bf16[320,224]{1,0:T(8,128)(2,1)}, bf16[320,224]{1,0:T(8,128)(2,1)}, bf16[320,224]{1,0:T(8,128)(2,1)}, bf16[8,176,12...) custom-call(f32[320,224]{1,0:T(8,128)} %get-tuple-element.48.refs_0_, ...), custom_call_target="tpu_custom_call" | custom-call | flops 5000000000 | tf_op jit(solution)/shard_map/back/pallas_call | solution.py:363
  169.2 5.7 %back.3 = (bf16[8,160,128]{2,1,0:T(8,128)(2,1)}, bf16[8,160,128]{2,1,0:T(8,128)(2,1)}, bf16[8,160,128]{2,1,0:T(8,128)(2,1)}, bf16[8,160,128]{2,1,0:T(8,128)(2,1)}) custom-call(bf16[320,224]{1,0:T(8,128)(2,1)} %get-tuple-element.57.gg_ref, bf16[320,224]{1,0:T(8,128)(2,1)} %get-tuple-element.58.ug_ref, bf16[320,224]{1,0:T(8,128)(2,1)} %get-tuple-element.59.ggp_ref, ...), custom_call_target="tpu_custom_call" | custom-call | flops 4000000000 | tf_op jit(solution)/shard_map/back/pallas_call | solution.py:369
  175.0 9.0 %collective-permute-done.27.refs_2_ = bf16[8,176,128]{2,1,0:T(8,128)(2,1)S(1)} collective-permute-done((bf16[8,176,128]{2,1,0:T(8,128)(2,1)}, bf16[8,176,128]{2,1,0:T(8,128)(2,1)S(1)}, u32[]{:S(2)}, u32[]{:S(2)}) %collective-permute-start.27) | collective-permute-done | bytes 360480 | tf_op jit(solution)/shard_map/scatter/ppermute | solution.py:298
  187.8 3.4 %all-to-all-start.1 = ((bf16[8,176,128]{2,1,0:T(8,128)(2,1)}), bf16[8,176,128]{2,1,0:T(8,128)(2,1)S(1)}, u32[]{:S(2)}, u32[]{:S(2)}) async-start(bf16[8,176,128]{2,1,0:T(8,128)(2,1)} %scatter.2), calls=%async_computation.1 | async-start | bytes 720896 | tf_op jit(solution)/shard_map/scatter/all_to_all | solution.py:377
  195.7 3.6 %collective-permute-done.29.refs_1_ = bf16[8,160,128]{2,1,0:T(8,128)(2,1)S(1)} collective-permute-done((bf16[8,160,128]{2,1,0:T(8,128)(2,1)S(1)}, bf16[8,160,128]{2,1,0:T(8,128)(2,1)S(1)}, u32[]{:S(2)}, u32[]{:S(2)}) %collective-permute-start.29) | collective-permute-done | bytes 327712 | tf_op jit(solution)/shard_map/scatter/ppermute | solution.py:298
  199.3 9.7 %collective-permute-done.30.refs_2_ = bf16[8,160,128]{2,1,0:T(8,128)(2,1)S(1)} collective-permute-done((bf16[8,160,128]{2,1,0:T(8,128)(2,1)S(1)}, bf16[8,160,128]{2,1,0:T(8,128)(2,1)S(1)}, u32[]{:S(2)}, u32[]{:S(2)}) %collective-permute-start.30) | collective-permute-done | bytes 327712 | tf_op jit(solution)/shard_map/scatter/ppermute | solution.py:298
  212.6 17.1 %all_to_all.21.second_ref = bf16[8,160,128]{2,1,0:T(8,128)(2,1)} all-to-all(bf16[8,160,128]{2,1,0:T(8,128)(2,1)} %scatter.3), channel_id=1, replica_groups=mesh['expert'=4,'tensor_0'=4,'tensor_1'=8,'kv'=2] {'tensor_1'}, dimensions={0} | all-to-all | bytes 655360 | tf_op jit(solution)/shard_map/scatter/all_to_all | solution.py:380
  231.7 13.2 %all_to_all.22.got_ref = bf16[8,96,128]{2,1,0:T(8,128)(2,1)} all-to-all(bf16[8,96,128]{2,1,0:T(8,128)(2,1)} %combine.2), channel_id=1, replica_groups=mesh['expert'=4,'tensor_0'=4,'tensor_1'=8,'kv'=2] {'expert','kv'}, dimensions={0} | all-to-all | bytes 393216 | tf_op jit(solution)/shard_map/combine/all_to_all | solution.py:384
  (131 shorter events, 50.6 us)
Async XLA Ops:
  0.0 83.4 %collective-permute-start.6 = (bf16[224,4096]{1,0:T(8,128)(2,1)}, bf16[224,4096]{1,0:T(8,128)(2,1)S(1)}, u32[]{:S(2)}, u32[]{:S(2)}) collective-permute-start(bf16[224,4096]{1,0:T(8,128)(2,1)} %bitcast.39), channel_id=1, source_target_pairs={{0,1},{1,0},{2,3},{3,2},{4,5},{5,4},{6,7},{7,6},{8,9},{9,8},{10,11... | collective-permute-start | bytes 5505032 | tf_op jit(solution)/shard_map/weights/ppermute | solution.py:298
  49.8 9.7 %collective-permute-start = (bf16[480,128]{1,0:T(8,128)(2,1)}, bf16[480,128]{1,0:T(8,128)(2,1)S(1)}, u32[]{:S(2)}, u32[]{:S(2)}) collective-permute-start(bf16[480,128]{1,0:T(8,128)(2,1)} %get-tuple-element.39), channel_id=1, source_target_pairs={{0,14},{2,0},{4,2},{6,4},{8,6},{10,8},{12,10},{14,12},{1,15},{3,1}... | collective-permute-start | bytes 368648 | tf_op jit(solution)/shard_map/gather_a/ppermute | solution.py:298
  63.0 8.2 %collective-permute-start.4 = (bf16[480,128]{1,0:T(8,128)(2,1)S(1)}, bf16[480,128]{1,0:T(8,128)(2,1)S(1)}, u32[]{:S(2)}, u32[]{:S(2)}) collective-permute-start(bf16[480,128]{1,0:T(8,128)(2,1)S(1)} %collective-permute-done.3), channel_id=1, source_target_pairs={{0,2},{2,4},{4,6},{6,8},{8,10},{10,12},{12,14},{14,0},{1,3},{3,5},... | collective-permute-start | bytes 368648 | tf_op jit(solution)/shard_map/gather_a/ppermute | solution.py:298
  67.9 24.4 %collective-permute-start.20 = (bf16[4,496,128]{2,1,0:T(8,128)(2,1)S(1)}, bf16[4,496,128]{2,1,0:T(8,128)(2,1)S(1)}, u32[]{:S(2)}, u32[]{:S(2)}) collective-permute-start(bf16[4,496,128]{2,1,0:T(8,128)(2,1)S(1)} %pad_maximum_fusion.refs_5_), channel_id=1, source_target_pairs={{0,2},{2,4},{4,6},{6,8},{8,10},{10,12},{12,14},{14,0},{1,3},{3,5},... | collective-permute-start | bytes 1523720 | tf_op jit(solution)/shard_map/gather_b/ppermute | solution.py:298
  68.0 24.3 %collective-permute-start.17 = (bf16[4,496,128]{2,1,0:T(8,128)(2,1)S(1)}, bf16[4,496,128]{2,1,0:T(8,128)(2,1)S(1)}, u32[]{:S(2)}, u32[]{:S(2)}) collective-permute-start(bf16[4,496,128]{2,1,0:T(8,128)(2,1)S(1)} %pad_maximum_fusion.refs_5_), channel_id=1, source_target_pairs={{0,14},{2,0},{4,2},{6,4},{8,6},{10,8},{12,10},{14,12},{1,15},{3,1}... | collective-permute-start | bytes 1523720 | tf_op jit(solution)/shard_map/gather_b/ppermute | solution.py:298
  70.7 11.7 %collective-permute-start.2 = (bf16[480,128]{1,0:T(8,128)(2,1)S(1)}, bf16[480,128]{1,0:T(8,128)(2,1)S(1)}, u32[]{:S(2)}, u32[]{:S(2)}) collective-permute-start(bf16[480,128]{1,0:T(8,128)(2,1)S(1)} %collective-permute-done.1), channel_id=1, source_target_pairs={{0,14},{2,0},{4,2},{6,4},{8,6},{10,8},{12,10},{14,12},{1,15},{3,1}... | collective-permute-start | bytes 368648 | tf_op jit(solution)/shard_map/gather_a/ppermute | solution.py:298
  71.2 12.2 %collective-permute-start.5 = (bf16[480,128]{1,0:T(8,128)(2,1)S(1)}, bf16[480,128]{1,0:T(8,128)(2,1)S(1)}, u32[]{:S(2)}, u32[]{:S(2)}) collective-permute-start(bf16[480,128]{1,0:T(8,128)(2,1)S(1)} %collective-permute-done.4), channel_id=1, source_target_pairs={{0,2},{2,4},{4,6},{6,8},{8,10},{10,12},{12,14},{14,0},{1,3},{3,5},... | collective-permute-start | bytes 368648 | tf_op jit(solution)/shard_map/gather_a/ppermute | solution.py:298
  86.2 40.1 %collective-permute-start.11 = (bf16[224,4096]{1,0:T(8,128)(2,1)S(1)}, bf16[224,4096]{1,0:T(8,128)(2,1)S(1)}, u32[]{:S(2)}, u32[]{:S(2)}) collective-permute-start(bf16[224,4096]{1,0:T(8,128)(2,1)S(1)} %bitcast.46), channel_id=1, source_target_pairs={{0,1},{1,0},{2,3},{3,2},{4,5},{5,4},{6,7},{7,6},{8,9},{9,8},{10,11... | collective-permute-start | bytes 5505032 | tf_op jit(solution)/shard_map/gather_a/ppermute | solution.py:298
  89.4 21.6 %collective-permute-start.10 = (bf16[8,480,128]{2,1,0:T(8,128)(2,1)S(1)}, bf16[8,480,128]{2,1,0:T(8,128)(2,1)S(1)}, u32[]{:S(2)}, u32[]{:S(2)}) collective-permute-start(bf16[8,480,128]{2,1,0:T(8,128)(2,1)S(1)} %bitcast_dynamic-update-slice_fusion.refs_0_), channel_id=1, source_target_pairs={{0,16},{16,32},{32,48},{48,0},{1,17},{17,33},{33,49},{49,1},{2,18}... | collective-permute-start | bytes 2949128 | tf_op jit(solution)/shard_map/gather_a/ppermute | solution.py:298
  89.7 21.3 %collective-permute-start.9 = (bf16[8,480,128]{2,1,0:T(8,128)(2,1)S(1)}, bf16[8,480,128]{2,1,0:T(8,128)(2,1)S(1)}, u32[]{:S(2)}, u32[]{:S(2)}) collective-permute-start(bf16[8,480,128]{2,1,0:T(8,128)(2,1)S(1)} %bitcast_dynamic-update-slice_fusion.refs_0_), channel_id=1, source_target_pairs={{0,48},{16,0},{32,16},{48,32},{1,49},{17,1},{33,17},{49,33},{2,50}... | collective-permute-start | bytes 2949128 | tf_op jit(solution)/shard_map/gather_a/ppermute | solution.py:298
  92.3 10.6 %collective-permute-start.21 = (bf16[4,496,128]{2,1,0:T(8,128)(2,1)S(1)}, bf16[4,496,128]{2,1,0:T(8,128)(2,1)S(1)}, u32[]{:S(2)}, u32[]{:S(2)}) collective-permute-start(bf16[4,496,128]{2,1,0:T(8,128)(2,1)S(1)} %collective-permute-done.20.refs_11_), channel_id=1, source_target_pairs={{0,2},{2,4},{4,6},{6,8},{8,10},{10,12},{12,14},{14,0},{1,3},{3,5},... | collective-permute-start | bytes 1523720 | tf_op jit(solution)/shard_map/gather_b/ppermute | solution.py:298
  92.4 10.6 %collective-permute-start.18 = (bf16[4,496,128]{2,1,0:T(8,128)(2,1)S(1)}, bf16[4,496,128]{2,1,0:T(8,128)(2,1)S(1)}, u32[]{:S(2)}, u32[]{:S(2)}) collective-permute-start(bf16[4,496,128]{2,1,0:T(8,128)(2,1)S(1)} %collective-permute-done.17.refs_6_), channel_id=1, source_target_pairs={{0,14},{2,0},{4,2},{6,4},{8,6},{10,8},{12,10},{14,12},{1,15},{3,1}... | collective-permute-start | bytes 1523720 | tf_op jit(solution)/shard_map/gather_b/ppermute | solution.py:298
  102.9 26.3 %collective-permute-start.22 = (bf16[4,496,128]{2,1,0:T(8,128)(2,1)S(1)}, bf16[4,496,128]{2,1,0:T(8,128)(2,1)S(1)}, u32[]{:S(2)}, u32[]{:S(2)}) collective-permute-start(bf16[4,496,128]{2,1,0:T(8,128)(2,1)S(1)} %collective-permute-done.21.refs_10_), channel_id=1, source_target_pairs={{0,2},{2,4},{4,6},{6,8},{8,10},{10,12},{12,14},{14,0},{1,3},{3,5},... | collective-permute-start | bytes 1523720 | tf_op jit(solution)/shard_map/gather_b/ppermute | solution.py:298
  103.0 26.4 %collective-permute-start.19 = (bf16[4,496,128]{2,1,0:T(8,128)(2,1)S(1)}, bf16[4,496,128]{2,1,0:T(8,128)(2,1)S(1)}, u32[]{:S(2)}, u32[]{:S(2)}) collective-permute-start(bf16[4,496,128]{2,1,0:T(8,128)(2,1)S(1)} %collective-permute-done.18.refs_7_), channel_id=1, source_target_pairs={{0,14},{2,0},{4,2},{6,4},{8,6},{10,8},{12,10},{14,12},{1,15},{3,1}... | collective-permute-start | bytes 1523720 | tf_op jit(solution)/shard_map/gather_b/ppermute | solution.py:298
  126.4 10.2 %collective-permute-start.12 = (bf16[4,480,128]{2,1,0:T(8,128)(2,1)S(1)}, bf16[4,480,128]{2,1,0:T(8,128)(2,1)S(1)}, u32[]{:S(2)}, u32[]{:S(2)}) collective-permute-start(bf16[4,480,128]{2,1,0:T(8,128)(2,1)S(1)} %slice.20), channel_id=1, source_target_pairs={{0,16},{16,32},{32,48},{48,0},{1,17},{17,33},{33,49},{49,1},{2,18}... | collective-permute-start | bytes 1474568 | tf_op jit(solution)/shard_map/gather_a/ppermute | solution.py:298
  126.5 10.0 %collective-permute-start.13 = (bf16[4,480,128]{2,1,0:T(8,128)(2,1)S(1)}, bf16[4,480,128]{2,1,0:T(8,128)(2,1)S(1)}, u32[]{:S(2)}, u32[]{:S(2)}) collective-permute-start(bf16[4,480,128]{2,1,0:T(8,128)(2,1)S(1)} %slice.21), channel_id=1, source_target_pairs={{0,48},{16,0},{32,16},{48,32},{1,49},{17,1},{33,17},{49,33},{2,50}... | collective-permute-start | bytes 1474568 | tf_op jit(solution)/shard_map/gather_a/ppermute | solution.py:298
  146.1 12.6 %collective-permute-start.25 = (bf16[320,224]{1,0:T(8,128)(2,1)}, bf16[320,224]{1,0:T(8,128)(2,1)S(1)}, u32[]{:S(2)}, u32[]{:S(2)}) collective-permute-start(bf16[320,224]{1,0:T(8,128)(2,1)} %get-tuple-element.55), channel_id=1, source_target_pairs={{0,1},{1,0},{2,3},{3,2},{4,5},{5,4},{6,7},{7,6},{8,9},{9,8},{10,11... | collective-permute-start | bytes 430088 | tf_op jit(solution)/shard_map/act/ppermute | solution.py:298
  166.1 8.9 %collective-permute-start.26 = (bf16[8,176,128]{2,1,0:T(8,128)(2,1)}, bf16[8,176,128]{2,1,0:T(8,128)(2,1)S(1)}, u32[]{:S(2)}, u32[]{:S(2)}) collective-permute-start(bf16[8,176,128]{2,1,0:T(8,128)(2,1)} %get-tuple-element.63), channel_id=1, source_target_pairs={{0,32},{16,48},{32,0},{48,16},{1,33},{17,49},{33,1},{49,17},{2,34}... | collective-permute-start | bytes 1081352 | tf_op jit(solution)/shard_map/scatter/ppermute | solution.py:298
  166.6 17.5 %collective-permute-start.27 = (bf16[8,176,128]{2,1,0:T(8,128)(2,1)}, bf16[8,176,128]{2,1,0:T(8,128)(2,1)S(1)}, u32[]{:S(2)}, u32[]{:S(2)}) collective-permute-start(bf16[8,176,128]{2,1,0:T(8,128)(2,1)} %get-tuple-element.64), channel_id=1, source_target_pairs={{0,16},{16,32},{32,48},{48,0},{1,17},{17,33},{33,49},{49,1},{2,18}... | collective-permute-start | bytes 1081352 | tf_op jit(solution)/shard_map/scatter/ppermute | solution.py:298
  168.5 15.6 %collective-permute-start.28 = (bf16[8,176,128]{2,1,0:T(8,128)(2,1)}, bf16[8,176,128]{2,1,0:T(8,128)(2,1)S(1)}, u32[]{:S(2)}, u32[]{:S(2)}) collective-permute-start(bf16[8,176,128]{2,1,0:T(8,128)(2,1)} %get-tuple-element.65), channel_id=1, source_target_pairs={{0,48},{16,0},{32,16},{48,32},{1,49},{17,1},{33,17},{49,33},{2,50}... | collective-permute-start | bytes 1081352 | tf_op jit(solution)/shard_map/scatter/ppermute | solution.py:298
  187.8 24.9 %all-to-all-start.1 = ((bf16[8,176,128]{2,1,0:T(8,128)(2,1)}), bf16[8,176,128]{2,1,0:T(8,128)(2,1)S(1)}, u32[]{:S(2)}, u32[]{:S(2)}) async-start(bf16[8,176,128]{2,1,0:T(8,128)(2,1)} %scatter.2), calls=%async_computation.1 | async-start | bytes 720896 | tf_op jit(solution)/shard_map/scatter/all_to_all | solution.py:377
  191.2 8.1 %collective-permute-start.29 = (bf16[8,160,128]{2,1,0:T(8,128)(2,1)S(1)}, bf16[8,160,128]{2,1,0:T(8,128)(2,1)S(1)}, u32[]{:S(2)}, u32[]{:S(2)}) collective-permute-start(bf16[8,160,128]{2,1,0:T(8,128)(2,1)S(1)} %copy-done.22), channel_id=1, source_target_pairs={{0,32},{16,48},{32,0},{48,16},{1,33},{17,49},{33,1},{49,17},{2,34}... | collective-permute-start | bytes 983048 | tf_op jit(solution)/shard_map/scatter/ppermute | solution.py:298
  193.0 16.0 %collective-permute-start.30 = (bf16[8,160,128]{2,1,0:T(8,128)(2,1)S(1)}, bf16[8,160,128]{2,1,0:T(8,128)(2,1)S(1)}, u32[]{:S(2)}, u32[]{:S(2)}) collective-permute-start(bf16[8,160,128]{2,1,0:T(8,128)(2,1)S(1)} %copy-done.21), channel_id=1, source_target_pairs={{0,16},{16,32},{32,48},{48,0},{1,17},{17,33},{33,49},{49,1},{2,18}... | collective-permute-start | bytes 983048 | tf_op jit(solution)/shard_map/scatter/ppermute | solution.py:298
  193.0 16.0 %collective-permute-start.31 = (bf16[8,160,128]{2,1,0:T(8,128)(2,1)S(1)}, bf16[8,160,128]{2,1,0:T(8,128)(2,1)S(1)}, u32[]{:S(2)}, u32[]{:S(2)}) collective-permute-start(bf16[8,160,128]{2,1,0:T(8,128)(2,1)S(1)} %copy-done.20), channel_id=1, source_target_pairs={{0,48},{16,0},{32,16},{48,32},{1,49},{17,1},{33,17},{49,33},{2,50}... | collective-permute-start | bytes 983048 | tf_op jit(solution)/shard_map/scatter/ppermute | solution.py:298
  (38 other events, 480.1 us)

commit v2 on v1

--- a/solution.py
+++ b/solution.py
@@ -20,7 +20,8 @@
 XROWS = HALF + GAIN_ROWS
 SPLIT = 144
 PADDED = 384
-PART = HALF // 2
+ZFIRST = 128
+YFIRST = HALF - ZFIRST
 EXTRA = 16
 TENSOR_KV = ("tensor_0", "tensor_1", "kv")
 LINE = ("expert", "kv")
@@ -107,11 +108,14 @@
     return block(y, z)
 
 
+def row_of(a, z):
+    return block(lax.rem(lax.axis_index("tensor_0") + a, NY), z)
+
+
 def a_piece(refs, a, b):
-    x0, x1, x3, lo, hi = refs
-    if a == 2:
-        return (lo, b) if b < NZ // 2 else (hi, b - NZ // 2)
-    return (x0, x1, None, x3)[a], b
+    if a == 0:
+        return refs[0], b
+    return refs[(None, 1, 5, 3)[a] + b // 4], b % 4
 
 
 def b_piece(refs, a, b):
@@ -124,11 +128,11 @@
 
 
 def act_kernel(*refs):
-    a_refs, b_refs = refs[:5], refs[5:14]
-    wd_ref, mine_ref, theirs_ref, grad_ref, act_ref = refs[14:]
+    a_refs, b_refs = refs[:7], refs[7:16]
+    wd_ref, mine_ref, theirs_ref, grad_ref, act_ref = refs[16:]
     for a, b in PLACES:
         ref, at = a_piece(a_refs, a, b)
-        grad_ref[pl.ds(0, SPLIT), column(a, b)] = ref[at, pl.ds(XROWS, SPLIT), :]
+        grad_ref[pl.ds(0, SPLIT), row_of(a, b)] = ref[at, pl.ds(XROWS, SPLIT), :]
         ref, at = b_piece(b_refs, a, b)
         grad_ref[pl.ds(SPLIT, ROWS - SPLIT), column(a, b)] = ref[at]
 
@@ -151,8 +155,8 @@
 
 
 def forward_kernel(*refs):
-    a_refs = refs[:5]
-    wg_ref, wu_ref, wgp_ref, wup_ref, gate_ref, up_ref, gatep_ref, upp_ref, inv_ref, xn_ref, column_ref = refs[5:]
+    a_refs = refs[:7]
+    wg_ref, wu_ref, wgp_ref, wup_ref, gate_ref, up_ref, gatep_ref, upp_ref, inv_ref, xn_ref, column_ref = refs[7:]
 
     @pl.loop(0, HALF // 64)
     def _(r):
@@ -167,7 +171,7 @@
         for a, b in PLACES:
             ref, at = a_piece(a_refs, a, b)
             gain = ref[at, pl.ds(HALF, GAIN_ROWS), :].astype(F32)[0:1]
-            xn_ref[rows, column(a, b)] = (ref[at, rows, :].astype(F32) * inv * gain).astype(BF16)
+            xn_ref[rows, row_of(a, b)] = (ref[at, rows, :].astype(F32) * inv * gain).astype(BF16)
 
     column_ref[pl.ds(HALF, PADDED - HALF), :] = jnp.zeros((PADDED - HALF, LANES), F32)
     to_row(column_ref, inv_ref)
@@ -184,18 +188,6 @@
     return terms
 
 
-def back_products(gs, ws, rows, a, outs):
-    y = lax.rem(lax.axis_index("tensor_0") + a, NY)
-    for z in range(0, NZ, 2):
-        at = pl.ds(pl.multiple_of((y * NZ + z) * LANES, 2 * LANES), 2 * LANES)
-        total = 0.0
-        for g_ref, w_ref in zip(gs, ws):
-            total = total + jnp.dot(g_ref[rows, :], w_ref[:, at], preferred_element_type=F32)
-        total = total.astype(BF16)
-        outs[a][z, pl.ds(0, PART), :] = total[:, :LANES]
-        outs[a][z + 1, pl.ds(0, PART), :] = total[:, LANES:]
-
-
 def carried(rows):
     terms = [t.astype(F32) for t in split3(rows)]
     return jnp.concatenate(terms + [jnp.zeros((7, LANES), F32)], axis=0).astype(BF16)
@@ -205,9 +197,9 @@
     return carried_sum[0:3] + carried_sum[3:6] + carried_sum[6:9]
 
 
-def first_kernel(*refs):
+def back_kernel(*refs):
     gate_ref, up_ref, gatep_ref, upp_ref, act_ref, actp_ref, *ws = refs[:10]
-    gg_ref, ug_ref, ggp_ref, ugp_ref, *outs, column_ref = refs[10:]
+    top_ref, *outs, gg_ref, ug_ref, ggp_ref, ugp_ref, column_ref = refs[10:]
     sums = 0.0
     for gate_in, up_in, act_in, gg_out, ug_out in (
         (gate_ref, up_ref, act_ref, gg_ref, ug_ref),
@@ -224,54 +216,59 @@
     column_ref[pl.ds(HALF, PADDED - HALF), :] = jnp.zeros((PADDED - HALF, LANES), F32)
     rows = [jnp.transpose(column_ref[pl.ds(r * LANES, LANES), :])[0:1] for r in range(PADDED // LANES)]
     projection = carried(jnp.concatenate(rows, axis=0))
-    for a in (2, 1, 3, 0):
-        back_products((gg_ref, ug_ref, ggp_ref, ugp_ref), ws, pl.ds(0, PART), a, outs)
-        for z in range(NZ):
-            outs[a][z, pl.ds(PART, EXTRA), :] = projection
-
-
-def second_kernel(gg_ref, ug_ref, ggp_ref, ugp_ref, wg_ref, wu_ref, wgp_ref, wup_ref, *outs):
-    for a in (2, 1, 3, 0):
-        back_products(
-            (gg_ref, ug_ref, ggp_ref, ugp_ref), (wg_ref, wu_ref, wgp_ref, wup_ref), pl.ds(PART, PART), a, outs
-        )
-
-
-def sum_first_kernel(*refs):
+    gs = (gg_ref, ug_ref, ggp_ref, ugp_ref)
+    for a in range(NY):
+        y = lax.rem(lax.axis_index("tensor_0") + a, NY)
+        for z in range(0, NZ, 2):
+            at = pl.ds(pl.multiple_of((y * NZ + z) * LANES, 2 * LANES), 2 * LANES)
+            total = 0.0
+            for g_ref, w_ref in zip(gs, ws):
+                total = total + jnp.dot(g_ref[...], w_ref[:, at], preferred_element_type=F32)
+            total = total.astype(BF16)
+            for k in range(2):
+                part = total[:, k * LANES : (k + 1) * LANES]
+                top_ref[z + k, a] = part[:ZFIRST]
+                outs[a][z + k, pl.ds(0, YFIRST), :] = part[ZFIRST:]
+                outs[a][z + k, pl.ds(YFIRST, EXTRA), :] = projection
+
+
+def sum_top_kernel(got_ref, *outs):
+    for a in range(NY):
+        total = got_ref[0, a].astype(F32)
+        for z in range(1, NZ):
+            total = total + got_ref[z, a].astype(F32)
+        outs[a][...] = total.astype(BF16)
+
+
+def sum_low_kernel(*refs):
     *shares, out_ref = refs
     for z in range(NZ):
         total = 0.0
         for ref in shares:
             total = total + ref[z].astype(F32)
-        out_ref[z, pl.ds(0, PART), :] = total[:PART].astype(BF16)
-        out_ref[z, pl.ds(PART, EXTRA), :] = carried(gathered_up(total[PART:]))
-
-
-def sum_second_kernel(*refs):
-    *shares, out_ref = refs
-    for z in range(NZ):
-        total = 0.0
-        for ref in shares:
-            total = total + ref[z].astype(F32)
-        out_ref[z] = total.astype(BF16)
-
-
-def finish_kernel(first_ref, second_ref, inv_ref, out_ref):
-    first, second = first_ref[0].astype(F32), second_ref[0].astype(F32)
+        out_ref[z, pl.ds(0, YFIRST), :] = total[:YFIRST].astype(BF16)
+        out_ref[z, pl.ds(YFIRST, EXTRA), :] = carried(gathered_up(total[YFIRST:]))
+
+
+def finish_kernel(*refs):
+    *tops, low_ref, inv_ref, out_ref = refs
+    top, low = 0.0, low_ref[0].astype(F32)
+    for ref in tops:
+        top = top + ref[...].astype(F32)
     for z in range(1, NZ):
-        first = first + first_ref[z].astype(F32)
-        second = second + second_ref[z].astype(F32)
-    rows = gathered_up(first[PART:])
+        low = low + low_ref[z].astype(F32)
+    slot_grad = jnp.concatenate([top, low[:YFIRST]], axis=0).astype(BF16)
+    rows = gathered_up(low[YFIRST:])
     projection = jnp.concatenate([rows[r : r + 1] for r in range(PADDED // LANES)], axis=1)
     inv = inv_ref[...]
     terms = split3(inv * inv * projection / D) + split3(inv)
     terms = jnp.concatenate([t.astype(F32) for t in terms] + [jnp.zeros((10, PADDED), F32)], axis=0)
     for b in range(GROUPS):
-        here = (first, second)[b // 2][(b % 2) * MINE : (b % 2 + 1) * MINE].astype(BF16)
-        scalars = terms[:, b * MINE : b * MINE + LANES]
+        here = slot_grad[b * MINE : (b + 1) * MINE]
+        scalars = terms[:, b * MINE : b * MINE + LANES].astype(BF16)
         for k in range(2):
             out_ref[2 * b + k, pl.ds(0, MINE), :] = here
-            out_ref[2 * b + k, pl.ds(MINE, EXTRA), :] = scalars.astype(BF16)
+            out_ref[2 * b + k, pl.ds(MINE, EXTRA), :] = scalars
 
 
 def combine_kernel(got_ref, ids_ref, x_ref, gain_ref, out_ref):
@@ -298,17 +295,16 @@
     return lax.ppermute(value, axis, [(i, (i + by) % n) for i in range(n)])
 
 
-def gather_ring(value, axis, cut, meet=None):
+def gather_ring(value, axis, cut, meet=lambda step, right, left: (right, left)):
     n = lax.axis_size(axis)
     got = {0: value}
     right = left = value
     for step in range(1, n // 2):
+        right, left = meet(step, right, left)
         right, left = shift(right, axis, 1), shift(left, axis, -1)
         got[n - step], got[step] = right, left
-    if meet is not None:
-        right, left, meet = lax.optimization_barrier((right, left, meet))
-    far = (shift(right[:cut], axis, 1), shift(left[cut:], axis, -1))
-    return got, far, meet
+    right, left = meet(n // 2, right, left)
+    return got, (shift(right[:cut], axis, 1), shift(left[cut:], axis, -1))
 
 
 def shards(residual_stream, grad_output, norm_gain, expert_ids, gate_probs, w_gate, w_up, w_down):
@@ -318,33 +314,47 @@
     gain_rows = jnp.broadcast_to(jnp.concatenate([norm_gain, norm_gain])[None], (GAIN_ROWS, LANES))
     hidden = wg.shape[0]
 
-    with jax.named_scope("weights"):
-        wgp = shift(wg, "kv", 1)
-
     with jax.named_scope("dispatch"):
         [routed] = call(dispatch_kernel, [((GROUPS, 2, CAP, LANES), BF16)], 2)(
             ids, probs, x_t, grad_t, gain_rows
         )
         got = lax.all_to_all(routed.reshape(2 * GROUPS, CAP, LANES), LINE, 0, 0, tiled=True)
+        got, own_wg = lax.optimization_barrier((got, wg))
         piece_a, piece_b = call(
             assemble_kernel, [((XROWS + SPLIT, LANES), BF16), ((ROWS - SPLIT, LANES), BF16)], 2
         )(got.reshape(GROUPS, 2, CAP, LANES))
 
-    with jax.named_scope("gather_a"):
-        z_got, z_far, wgp = gather_ring(piece_a, "tensor_1", (XROWS + SPLIT) // 2, wgp)
-        later, wgp = lax.optimization_barrier((wu, wgp))
-        wup = shift(later, "kv", 1)
-        z_got[4] = jnp.concatenate(z_far, axis=0)
-        line = jnp.stack([z_got[b] for b in range(NZ)])
-        a_got, a_far, wup = gather_ring(line, "tensor_0", NZ // 2, wup)
-        a_refs = (a_got[0], a_got[1], a_got[3], *a_far)
-    with jax.named_scope("gather_b"):
-        line = jnp.stack([piece_b] + [shift(piece_b, "tensor_0", -a) for a in (1, 2, 3)])
-        line, _ = lax.optimization_barrier((line, z_got[2]))
-        b_got, b_far, _ = gather_ring(line, "tensor_1", NY // 2)
+    with jax.named_scope("weights"):
+        wgp = shift(own_wg, "kv", 1)
+    with jax.named_scope("gather"):
+        copies = jnp.broadcast_to(piece_a[None], (NZ, *piece_a.shape))
+        line_a = lax.all_to_all(copies, "tensor_1", 0, 0, tiled=True)
+        line_b = jnp.stack([piece_b] + [shift(piece_b, "tensor_0", -a) for a in (1, 2, 3)])
+
+        near, far = [], []
+
+        def meet(step, right, left):
+            nonlocal line_a, wgp
+            if step == 2:
+                right, left, line_a = lax.optimization_barrier((right, left, line_a))
+                near[:] = [shift(line_a[: NZ // 2], "tensor_0", by) for by in (1, -1)]
+                far[:] = [shift(line_a[NZ // 2 :], "tensor_0", by) for by in (1, -1)]
+            if step == 3:
+                right, left, wgp, *near[:] = lax.optimization_barrier((right, left, wgp, *near))
+            if step == 4:
+                right, left, *far[:] = lax.optimization_barrier((right, left, *far))
+            return right, left
+
+        b_got, b_far = gather_ring(line_b, "tensor_1", NY // 2, meet)
         b_refs = (*[b_got[b] for b in range(NZ) if b != 4], *b_far)
+        a_far = (shift(near[0], "tensor_0", 1), shift(far[1], "tensor_0", -1))
+        a_refs = (line_a, near[1], far[1], near[0], far[0], *a_far)
+    with jax.named_scope("weights"):
+        wgp, own_wu = lax.optimization_barrier((wgp, wu))
+        wup = shift(own_wu, "kv", 1)
 
     with jax.named_scope("act"):
+        wd, wgp, wup = lax.optimization_barrier((wd, wgp, wup))
         act, theirs = call(
             act_kernel,
             [((HALF, hidden), F32), ((HALF, hidden), BF16)],
@@ -360,27 +370,23 @@
             [pltpu.VMEM((HALF, D), BF16), pltpu.VMEM((PADDED, LANES), F32)],
         )(*a_refs, wg, wu, wgp, wup)
     with jax.named_scope("back"):
-        gg, ug, ggp, ugp, *first = call(
-            first_kernel,
-            [((HALF, hidden), BF16)] * 4 + [((NZ, PART + EXTRA, LANES), BF16)] * NY,
-            5,
-            [pltpu.VMEM((PADDED, LANES), F32)],
+        top, *low = call(
+            back_kernel,
+            [((NZ, NY, ZFIRST, LANES), BF16)] + [((NZ, YFIRST + EXTRA, LANES), BF16)] * NY,
+            8,
+            [pltpu.VMEM((HALF, hidden), BF16)] * 4 + [pltpu.VMEM((PADDED, LANES), F32)],
         )(gate, up, gatep, upp, act, actp, wg, wu, wgp, wup)
-        second = call(second_kernel, [((NZ, PART, LANES), BF16)] * NY, 4)(
-            gg, ug, ggp, ugp, wg, wu, wgp, wup
-        )
     with jax.named_scope("scatter"):
-        own_first, own_second = lax.optimization_barrier((first[0], second[0]))
-        first = [own_first] + [shift(first[a], "tensor_0", a) for a in (2, 1, 3)]
-        second = [own_second] + [shift(second[a], "tensor_0", a) for a in (2, 1, 3)]
-        [first] = call(sum_first_kernel, [((NZ, PART + EXTRA, LANES), BF16)], 3)(*first)
-        first = lax.all_to_all(first, "tensor_1", 0, 0, tiled=True)
-        [second] = call(sum_second_kernel, [((NZ, PART, LANES), BF16)], 3)(*second)
-        first, second = lax.optimization_barrier((first, second))
-        second = lax.all_to_all(second, "tensor_1", 0, 0, tiled=True)
+        top = lax.all_to_all(top, "tensor_1", 0, 0, tiled=True)
+        low = [low[0]] + [shift(low[a], "tensor_0", a) for a in (2, 1, 3)]
+        [low] = call(sum_low_kernel, [((NZ, YFIRST + EXTRA, LANES), BF16)], 3)(*low)
+        top, low = lax.optimization_barrier((top, low))
+        top = call(sum_top_kernel, [((ZFIRST, LANES), BF16)] * NY, 3)(top)
+        low = lax.all_to_all(low, "tensor_1", 0, 0, tiled=True)
+        top = [top[0]] + [shift(top[a], "tensor_0", a) for a in (2, 1, 3)]
 
     with jax.named_scope("combine"):
-        [pieces] = call(finish_kernel, [((2 * GROUPS, MINE + EXTRA, LANES), BF16)], 2)(first, second, inv)
+        [pieces] = call(finish_kernel, [((2 * GROUPS, MINE + EXTRA, LANES), BF16)], 2)(*top, low, inv)
         got = lax.all_to_all(pieces, LINE, 0, 0, tiled=True)
         gain_square = jnp.broadcast_to(norm_gain[None], (LANES, norm_gain.shape[0]))
         [out] = call(combine_kernel, [(x_t.shape, BF16)], 2)(

time: 248 us -> 220 us (0.89)
  blocking collectives: 71.3 us -> 27 us
  waiting for transfers between devices: 70.9 us -> 91.2 us
  Pallas kernels: 42.1 us -> 37.9 us
    all_to_all x1, blocking collectives: 41 us -> 14.9 us  [shards(): lax.all_to_all(routed.reshape(2 * GROUPS, CAP, LANES), LINE, 0, 0, tiled=...]
    all_to_all x1 -> x0, blocking collectives: 17.1 us -> none  [shards(): second = lax.all_to_all(second, 'tensor_1', 0, 0, tiled=True)]
    ppermute x32 -> x26, starting transfers between devices: 50.1 us -> 34.9 us  [shift(): return lax.ppermute(value, axis, [(i, (i + by) % n) for i in range(n)])]
    all_to_all x1 -> x3, starting transfers between devices: 3.44 us -> 18.3 us  [the longest x1 6.8 us: shards(): line_a = lax.all_to_all(copies, 'tensor_1', 0, 0, tiled=True)]
    ppermute x32 -> x26, waiting for transfers between devices: 70.9 us -> 84.9 us  [shift(): return lax.ppermute(value, axis, [(i, (i + by) % n) for i in range(n)])]
    all_to_all x1 -> x3, waiting for transfers between devices: 0.01 us -> 6.28 us  [the longest x1 5.13 us: shards(): low = lax.all_to_all(low, 'tensor_1', 0, 0, tiled=True)]
    pallas_call x4 -> x3, Pallas kernels: 16.9 us -> 12.6 us  [the longest x1 8.25 us: shards(): call(back_kernel, [((NZ, NY, ZFIRST, LANES), BF16)] + [((NZ, YFIRST + EXT...]
    unnamed x64 -> x62, local copies, waits for them, and re-layouts: 6.18 us -> 5.22 us
  transfers between devices with their start and end apart: 33 -> 29, of which waited for: 13 -> 12; matrix products, arithmetic and copies ran while one was open for 1% -> 0% of each run, Pallas kernels for 9% -> 6%
where the time goes in v2:
time: 220 us; the launch traced here: 219 us
  waiting for transfers between devices  91.2 us (41%)
  starting transfers between devices  53.2 us (24%)
  Pallas kernels  37.9 us (17%)
  blocking collectives  27 us (12%)
  local copies, waits for them, and re-layouts  8.65 us (4%)
    ppermute x26, waiting for transfers between devices, shift(): return lax.ppermute(value, axis, [(i, (i + by) % n) for i in range(n)])  84.9 us
    ppermute x26, starting transfers between devices, shift(): return lax.ppermute(value, axis, [(i, (i + by) % n) for i in range(n)])  34.9 us
    all_to_all x1, blocking collectives, shards(): lax.all_to_all(routed.reshape(2 * GROUPS, CAP, LANES), LINE, 0, 0, tiled=...  14.9 us
    all_to_all x1, blocking collectives, shards(): got = lax.all_to_all(pieces, LINE, 0, 0, tiled=True)  12.2 us
    pallas_call x1, Pallas kernels, shards(): call(forward_kernel, [((HALF, hidden), F32)] * 4 + [((1, PADDED), F32)],...  9.55 us
    pallas_call x1, Pallas kernels, shards(): call(back_kernel, [((NZ, NY, ZFIRST, LANES), BF16)] + [((NZ, YFIRST + EXT...  8.25 us
    pallas_call x1, Pallas kernels, shards(): call(act_kernel, [((HALF, hidden), F32), ((HALF, hidden), BF16)], 7, [plt...  7.94 us
    all_to_all x1, starting transfers between devices, shards(): line_a = lax.all_to_all(copies, 'tensor_1', 0, 0, tiled=True)  6.8 us
  transfers between devices with their start and end apart: 29, of which 12 were waited for; matrix products, arithmetic and copies ran while one was open for 0% of the time, Pallas kernels for 6%

profile of v2, /device:TPU:1, one launch (start us, length us, event | category | flops | bytes accessed | tf_op | source)
XLA Modules:
  0.0 219.2 jit_solution(9490318461080013631)
XLA Ops:
  3.4 14.9 %all_to_all.25 = bf16[8,160,128]{2,1,0:T(8,128)(2,1)} all-to-all(bf16[8,160,128]{2,1,0:T(8,128)(2,1)} %bitcast.15), channel_id=1, replica_groups=mesh['expert'=4,'tensor_0'=4,'tensor_1'=8,'kv'=2] {'expert','kv'}, dimensions={0} | all-to-all | bytes 655360 | tf_op jit(solution)/shard_map/dispatch/all_to_all | solution.py:321
  20.1 2.1 broadcast_in_dim.7
  22.2 6.8 %all-to-all-start.1 = ((bf16[8,480,128]{2,1,0:T(8,128)(2,1)}), bf16[8,480,128]{2,1,0:T(8,128)(2,1)S(1)}, u32[]{:S(2)}, u32[]{:S(2)}) async-start(bf16[8,480,128]{2,1,0:T(8,128)(2,1)} %broadcast_in_dim.7), calls=%async_computation.1 | async-start | bytes 1966080 | tf_op jit(solution)/shard_map/gather/all_to_all | solution.py:331
  35.4 4.3 %collective-permute-done.1 = bf16[496,128]{1,0:T(8,128)(2,1)S(1)} collective-permute-done((bf16[496,128]{1,0:T(8,128)(2,1)S(1)}, bf16[496,128]{1,0:T(8,128)(2,1)S(1)}, u32[]{:S(2)}, u32[]{:S(2)}) %collective-permute-start.1) | collective-permute-done | bytes 127008 | tf_op jit(solution)/shard_map/gather/ppermute | solution.py:295
  42.5 21.7 %collective-permute-done.3.refs_13_ = bf16[4,496,128]{2,1,0:T(8,128)(2,1)S(1)} collective-permute-done((bf16[4,496,128]{2,1,0:T(8,128)(2,1)S(1)}, bf16[4,496,128]{2,1,0:T(8,128)(2,1)S(1)}, u32[]{:S(2)}, u32[]{:S(2)}) %collective-permute-start.3) | collective-permute-done | bytes 507936 | tf_op jit(solution)/shard_map/gather/ppermute | solution.py:295
  65.1 2.7 %collective-permute-start.6 = (bf16[4,496,128]{2,1,0:T(8,128)(2,1)}, bf16[4,496,128]{2,1,0:T(8,128)(2,1)S(1)}, u32[]{:S(2)}, u32[]{:S(2)}) collective-permute-start(bf16[4,496,128]{2,1,0:T(8,128)(2,1)} %collective-permute-done.4.refs_8_), channel_id=1, source_target_pairs={{0,14},{2,0},{4,2},{6,4},{8,6},{10,8},{12,10},{14,12},{1,15},{3,1}... | collective-permute-start | bytes 1523720 | tf_op jit(solution)/shard_map/gather/ppermute | solution.py:295
  71.6 8.5 %collective-permute-done.8.refs_3_ = bf16[4,480,128]{2,1,0:T(8,128)(2,1)S(1)} collective-permute-done((bf16[4,480,128]{2,1,0:T(8,128)(2,1)S(1)}, bf16[4,480,128]{2,1,0:T(8,128)(2,1)S(1)}, u32[]{:S(2)}, u32[]{:S(2)}) %collective-permute-start.8) | collective-permute-done | bytes 491552 | tf_op jit(solution)/shard_map/gather/ppermute | solution.py:295
  80.8 2.7 %collective-permute-start.11 = (bf16[4,496,128]{2,1,0:T(8,128)(2,1)S(1)}, bf16[4,496,128]{2,1,0:T(8,128)(2,1)S(1)}, u32[]{:S(2)}, u32[]{:S(2)}) collective-permute-start(bf16[4,496,128]{2,1,0:T(8,128)(2,1)S(1)} %collective-permute-done.6.refs_9_), channel_id=1, source_target_pairs={{0,14},{2,0},{4,2},{6,4},{8,6},{10,8},{12,10},{14,12},{1,15},{3,1}... | collective-permute-start | bytes 1523720 | tf_op jit(solution)/shard_map/gather/ppermute | solution.py:295
  86.1 7.5 %collective-permute-done.12.refs_4_ = bf16[4,480,128]{2,1,0:T(8,128)(2,1)S(1)} collective-permute-done((bf16[4,480,128]{2,1,0:T(8,128)(2,1)S(1)}, bf16[4,480,128]{2,1,0:T(8,128)(2,1)S(1)}, u32[]{:S(2)}, u32[]{:S(2)}) %collective-permute-start.12) | collective-permute-done | bytes 491552 | tf_op jit(solution)/shard_map/gather/ppermute | solution.py:295
  93.7 2.7 %collective-permute-start.15 = (bf16[4,480,128]{2,1,0:T(8,128)(2,1)S(1)}, bf16[4,480,128]{2,1,0:T(8,128)(2,1)}, u32[]{:S(2)}, u32[]{:S(2)}) collective-permute-start(bf16[4,480,128]{2,1,0:T(8,128)(2,1)S(1)} %collective-permute-done.13.refs_2_), channel_id=1, source_target_pairs={{0,48},{16,0},{32,16},{48,32},{1,49},{17,1},{33,17},{49,33},{2,50}... | collective-permute-start | bytes 1474568 | tf_op jit(solution)/shard_map/gather/ppermute | solution.py:295
  96.6 2.7 %collective-permute-start.18 = (bf16[2,496,128]{2,1,0:T(8,128)(2,1)S(1)}, bf16[2,496,128]{2,1,0:T(8,128)(2,1)S(1)}, u32[]{:S(2)}, u32[]{:S(2)}) collective-permute-start(bf16[2,496,128]{2,1,0:T(8,128)(2,1)S(1)} %slice.17), channel_id=1, source_target_pairs={{0,14},{2,0},{4,2},{6,4},{8,6},{10,8},{12,10},{14,12},{1,15},{3,1}... | collective-permute-start | bytes 761864 | tf_op jit(solution)/shard_map/gather/ppermute | solution.py:295
  99.3 21.2 %collective-permute-done.16.refs_10_.refs_9_ = bf16[224,4096]{1,0:T(8,128)(2,1)S(1)} collective-permute-done((bf16[224,4096]{1,0:T(8,128)(2,1)S(1)}, bf16[224,4096]{1,0:T(8,128)(2,1)S(1)}, u32[]{:S(2)}, u32[]{:S(2)}) %collective-permute-start.16) | collective-permute-done | bytes 1835040 | tf_op jit(solution)/shard_map/weights/ppermute | solution.py:295
  122.6 7.9 %act.1 = (f32[320,224]{1,0:T(8,128)}, bf16[320,224]{1,0:T(8,128)(2,1)}) custom-call(bf16[8,480,128]{2,1,0:T(8,128)(2,1)} %copy-done, bf16[4,480,128]{2,1,0:T(8,128)(2,1)} %copy-done.15, bf16[4,480,128]{2,1,0:T(8,128)(2,1)} %copy-done.17, bf16[4,480,128]{2,1,0:T(8,128)(2,1)} %copy-done.14, bf16[4,480,128]{2,1,0:T(8,128)(2,1)} %copy-done.16, ...), custom_call_target="tpu_custom_call" | custom-call | flops 7000000000 | tf_op jit(solution)/shard_map/act/pallas_call | solution.py:358
  130.9 9.6 %forward.1 = (f32[320,224]{1,0:T(8,128)}, f32[320,224]{1,0:T(8,128)}, f32[320,224]{1,0:T(8,128)}, f32[320,224]{1,0:T(8,128)}, f32[1,384]{1,0:T(1,128)}) custom-call(bf16[8,480,128]{2,1,0:T(8,128)(2,1)} %copy-done, bf16[4,480,128]{2,1,0:T(8,128)(2,1)} %copy-done.15, bf16[4,480,128]{2,1,0:T(8,128)(2,1)} %copy-done.17, bf16[4,480,128]{2,1,0:T(8,128)(2,1)} %copy-done.14, ...), custom_call_target="tpu_custom_call" | custom-call | flops 8000000000 | tf_op jit(solution)/shard_map/forward/pallas_call | solution.py:366
  141.2 8.3 %back.1 = (bf16[8,4,128,128]{3,2,1,0:T(8,128)(2,1)}, bf16[8,208,128]{2,1,0:T(8,128)(2,1)}, bf16[8,208,128]{2,1,0:T(8,128)(2,1)}, bf16[8,208,128]{2,1,0:T(8,128)(2,1)}, bf16[8,208,128]{2,1,0:T(8,128)(2,1)}) custom-call(f32[320,224]{1,0:T(8,128)} %get-tuple-element.62.refs_0_, f32[320,224]{1,0:T(8,128)} %get-tuple-element.63.refs_1_, ...), custom_call_target="tpu_custom_call" | custom-call | flops 8000000000 | tf_op jit(solution)/shard_map/back/pallas_call | solution.py:373
  149.4 6.4 %all-to-all-start.2 = ((bf16[8,4,128,128]{3,2,1,0:T(8,128)(2,1)}), bf16[8,4,128,128]{3,2,1,0:T(8,128)(2,1)S(1)}, u32[]{:S(2)}, u32[]{:S(2)}) async-start(bf16[8,4,128,128]{3,2,1,0:T(8,128)(2,1)} %get-tuple-element.71), calls=%async_computation.2 | async-start | bytes 2097152 | tf_op jit(solution)/shard_map/scatter/all_to_all | solution.py:380
  160.5 5.1 %collective-permute-done.20.refs_1_ = bf16[8,208,128]{2,1,0:T(8,128)(2,1)S(1)} collective-permute-done((bf16[8,208,128]{2,1,0:T(8,128)(2,1)S(1)}, bf16[8,208,128]{2,1,0:T(8,128)(2,1)S(1)}, u32[]{:S(2)}, u32[]{:S(2)}) %collective-permute-start.20) | collective-permute-done | bytes 426016 | tf_op jit(solution)/shard_map/scatter/ppermute | solution.py:295
  165.6 12.5 %collective-permute-done.21.refs_2_ = bf16[8,208,128]{2,1,0:T(8,128)(2,1)S(1)} collective-permute-done((bf16[8,208,128]{2,1,0:T(8,128)(2,1)S(1)}, bf16[8,208,128]{2,1,0:T(8,128)(2,1)S(1)}, u32[]{:S(2)}, u32[]{:S(2)}) %collective-permute-start.21) | collective-permute-done | bytes 426016 | tf_op jit(solution)/shard_map/scatter/ppermute | solution.py:295
  179.0 2.4 %scatter.2 = bf16[8,208,128]{2,1,0:T(8,128)(2,1)} custom-call(bf16[8,208,128]{2,1,0:T(8,128)(2,1)} %get-tuple-element.72.refs_0_, bf16[8,208,128]{2,1,0:T(8,128)(2,1)} %copy-done.22, bf16[8,208,128]{2,1,0:T(8,128)(2,1)} %copy-done.23, bf16[8,208,128]{2,1,0:T(8,128)(2,1)} %copy-done.24), custom_call_target="tpu_custom_call" | custom-call | flops 3000000000 | tf_op jit(solution)/shard_map/scatter/pallas_call | solution.py:382
  182.6 5.1 %all-to-all-start.3 = ((bf16[8,208,128]{2,1,0:T(8,128)(2,1)}), bf16[8,208,128]{2,1,0:T(8,128)(2,1)S(1)}, u32[]{:S(2)}, u32[]{:S(2)}) async-start(bf16[8,208,128]{2,1,0:T(8,128)(2,1)} %scatter.2), calls=%async_computation.3 | async-start | bytes 851968 | tf_op jit(solution)/shard_map/scatter/all_to_all | solution.py:385
  191.9 2.5 %collective-permute-start.25 = (bf16[128,128]{1,0:T(8,128)(2,1)}, bf16[128,128]{1,0:T(8,128)(2,1)S(1)}, u32[]{:S(2)}, u32[]{:S(2)}) collective-permute-start(bf16[128,128]{1,0:T(8,128)(2,1)} %get-tuple-element.80), channel_id=1, source_target_pairs={{0,48},{16,0},{32,16},{48,32},{1,49},{17,1},{33,17},{49,33},{2,50}... | collective-permute-start | bytes 98312 | tf_op jit(solution)/shard_map/scatter/ppermute | solution.py:295
  194.4 2.1 collective-permute-done.24.refs_2_
  196.6 5.1 %all-to-all-done.3.refs_4_ = bf16[8,208,128]{2,1,0:T(8,128)(2,1)S(1)} async-done(((bf16[8,208,128]{2,1,0:T(8,128)(2,1)}), bf16[8,208,128]{2,1,0:T(8,128)(2,1)S(1)}, u32[]{:S(2)}, u32[]{:S(2)}) %all-to-all-start.3) | async-done | bytes 426016 | tf_op jit(solution)/shard_map/scatter/all_to_all | solution.py:385
  204.4 12.2 %all_to_all.26.got_ref = bf16[8,96,128]{2,1,0:T(8,128)(2,1)} all-to-all(bf16[8,96,128]{2,1,0:T(8,128)(2,1)} %combine.2), channel_id=1, replica_groups=mesh['expert'=4,'tensor_0'=4,'tensor_1'=8,'kv'=2] {'expert','kv'}, dimensions={0} | all-to-all | bytes 393216 | tf_op jit(solution)/shard_map/combine/all_to_all | solution.py:390
  (115 shorter events, 41.9 us)
Async XLA Ops:
  22.2 42.8 %all-to-all-start.1 = ((bf16[8,480,128]{2,1,0:T(8,128)(2,1)}), bf16[8,480,128]{2,1,0:T(8,128)(2,1)S(1)}, u32[]{:S(2)}, u32[]{:S(2)}) async-start(bf16[8,480,128]{2,1,0:T(8,128)(2,1)} %broadcast_in_dim.7), calls=%async_computation.1 | async-start | bytes 1966080 | tf_op jit(solution)/shard_map/gather/all_to_all | solution.py:331
  29.0 42.6 %collective-permute-start.7 = (bf16[224,4096]{1,0:T(8,128)(2,1)S(1)}, bf16[224,4096]{1,0:T(8,128)(2,1)}, u32[]{:S(2)}, u32[]{:S(2)}) collective-permute-start(bf16[224,4096]{1,0:T(8,128)(2,1)S(1)} %bitcast.23), channel_id=1, source_target_pairs={{0,1},{1,0},{2,3},{3,2},{4,5},{5,4},{6,7},{7,6},{8,9},{9,8},{10,11... | collective-permute-start | bytes 5505032 | tf_op jit(solution)/shard_map/weights/ppermute | solution.py:295
  32.7 7.0 %collective-permute-start.1 = (bf16[496,128]{1,0:T(8,128)(2,1)S(1)}, bf16[496,128]{1,0:T(8,128)(2,1)S(1)}, u32[]{:S(2)}, u32[]{:S(2)}) collective-permute-start(bf16[496,128]{1,0:T(8,128)(2,1)S(1)} %copy-done.6), channel_id=1, source_target_pairs={{0,32},{16,48},{32,0},{48,16},{1,33},{17,49},{33,1},{49,17},{2,34}... | collective-permute-start | bytes 380936 | tf_op jit(solution)/shard_map/gather/ppermute | solution.py:295
  39.8 24.4 %collective-permute-start.3 = (bf16[4,496,128]{2,1,0:T(8,128)(2,1)S(1)}, bf16[4,496,128]{2,1,0:T(8,128)(2,1)S(1)}, u32[]{:S(2)}, u32[]{:S(2)}) collective-permute-start(bf16[4,496,128]{2,1,0:T(8,128)(2,1)S(1)} %pad_maximum_fusion.refs_7_), channel_id=1, source_target_pairs={{0,2},{2,4},{4,6},{6,8},{8,10},{10,12},{12,14},{14,0},{1,3},{3,5},... | collective-permute-start | bytes 1523720 | tf_op jit(solution)/shard_map/gather/ppermute | solution.py:295
  41.0 24.0 %collective-permute-start.4 = (bf16[4,496,128]{2,1,0:T(8,128)(2,1)S(1)}, bf16[4,496,128]{2,1,0:T(8,128)(2,1)}, u32[]{:S(2)}, u32[]{:S(2)}) collective-permute-start(bf16[4,496,128]{2,1,0:T(8,128)(2,1)S(1)} %pad_maximum_fusion.refs_7_), channel_id=1, source_target_pairs={{0,14},{2,0},{4,2},{6,4},{8,6},{10,8},{12,10},{14,12},{1,15},{3,1}... | collective-permute-start | bytes 1523720 | tf_op jit(solution)/shard_map/gather/ppermute | solution.py:295
  65.0 15.1 %collective-permute-start.5 = (bf16[4,496,128]{2,1,0:T(8,128)(2,1)}, bf16[4,496,128]{2,1,0:T(8,128)(2,1)S(1)}, u32[]{:S(2)}, u32[]{:S(2)}) collective-permute-start(bf16[4,496,128]{2,1,0:T(8,128)(2,1)} %copy-done.11), channel_id=1, source_target_pairs={{0,2},{2,4},{4,6},{6,8},{8,10},{10,12},{12,14},{14,0},{1,3},{3,5},... | collective-permute-start | bytes 1523720 | tf_op jit(solution)/shard_map/gather/ppermute | solution.py:295
  65.1 15.0 %collective-permute-start.6 = (bf16[4,496,128]{2,1,0:T(8,128)(2,1)}, bf16[4,496,128]{2,1,0:T(8,128)(2,1)S(1)}, u32[]{:S(2)}, u32[]{:S(2)}) collective-permute-start(bf16[4,496,128]{2,1,0:T(8,128)(2,1)} %collective-permute-done.4.refs_8_), channel_id=1, source_target_pairs={{0,14},{2,0},{4,2},{6,4},{8,6},{10,8},{12,10},{14,12},{1,15},{3,1}... | collective-permute-start | bytes 1523720 | tf_op jit(solution)/shard_map/gather/ppermute | solution.py:295
  67.8 12.3 %collective-permute-start.8 = (bf16[4,480,128]{2,1,0:T(8,128)(2,1)S(1)}, bf16[4,480,128]{2,1,0:T(8,128)(2,1)S(1)}, u32[]{:S(2)}, u32[]{:S(2)}) collective-permute-start(bf16[4,480,128]{2,1,0:T(8,128)(2,1)S(1)} %get-tuple-element.84), channel_id=1, source_target_pairs={{0,16},{16,32},{32,48},{48,0},{1,17},{17,33},{33,49},{49,1},{2,18}... | collective-permute-start | bytes 1474568 | tf_op jit(solution)/shard_map/gather/ppermute | solution.py:295
  69.2 10.9 %collective-permute-start.9 = (bf16[4,480,128]{2,1,0:T(8,128)(2,1)S(1)}, bf16[4,480,128]{2,1,0:T(8,128)(2,1)S(1)}, u32[]{:S(2)}, u32[]{:S(2)}) collective-permute-start(bf16[4,480,128]{2,1,0:T(8,128)(2,1)S(1)} %get-tuple-element.84), channel_id=1, source_target_pairs={{0,48},{16,0},{32,16},{48,32},{1,49},{17,1},{33,17},{49,33},{2,50}... | collective-permute-start | bytes 1474568 | tf_op jit(solution)/shard_map/gather/ppermute | solution.py:295
  80.2 40.4 %collective-permute-start.16 = (bf16[224,4096]{1,0:T(8,128)(2,1)S(1)}, bf16[224,4096]{1,0:T(8,128)(2,1)S(1)}, u32[]{:S(2)}, u32[]{:S(2)}) collective-permute-start(bf16[224,4096]{1,0:T(8,128)(2,1)S(1)} %bitcast.26), channel_id=1, source_target_pairs={{0,1},{1,0},{2,3},{3,2},{4,5},{5,4},{6,7},{7,6},{8,9},{9,8},{10,11... | collective-permute-start | bytes 5505032 | tf_op jit(solution)/shard_map/weights/ppermute | solution.py:295
  80.8 12.9 %collective-permute-start.10 = (bf16[4,496,128]{2,1,0:T(8,128)(2,1)S(1)}, bf16[4,496,128]{2,1,0:T(8,128)(2,1)S(1)}, u32[]{:S(2)}, u32[]{:S(2)}) collective-permute-start(bf16[4,496,128]{2,1,0:T(8,128)(2,1)S(1)} %collective-permute-done.5.refs_12_), channel_id=1, source_target_pairs={{0,2},{2,4},{4,6},{6,8},{8,10},{10,12},{12,14},{14,0},{1,3},{3,5},... | collective-permute-start | bytes 1523720 | tf_op jit(solution)/shard_map/gather/ppermute | solution.py:295
  80.8 12.9 %collective-permute-start.11 = (bf16[4,496,128]{2,1,0:T(8,128)(2,1)S(1)}, bf16[4,496,128]{2,1,0:T(8,128)(2,1)S(1)}, u32[]{:S(2)}, u32[]{:S(2)}) collective-permute-start(bf16[4,496,128]{2,1,0:T(8,128)(2,1)S(1)} %collective-permute-done.6.refs_9_), channel_id=1, source_target_pairs={{0,14},{2,0},{4,2},{6,4},{8,6},{10,8},{12,10},{14,12},{1,15},{3,1}... | collective-permute-start | bytes 1523720 | tf_op jit(solution)/shard_map/gather/ppermute | solution.py:295
  83.4 10.2 %collective-permute-start.12 = (bf16[4,480,128]{2,1,0:T(8,128)(2,1)S(1)}, bf16[4,480,128]{2,1,0:T(8,128)(2,1)S(1)}, u32[]{:S(2)}, u32[]{:S(2)}) collective-permute-start(bf16[4,480,128]{2,1,0:T(8,128)(2,1)S(1)} %get-tuple-element.83), channel_id=1, source_target_pairs={{0,16},{16,32},{32,48},{48,0},{1,17},{17,33},{33,49},{49,1},{2,18}... | collective-permute-start | bytes 1474568 | tf_op jit(solution)/shard_map/gather/ppermute | solution.py:295
  84.4 9.3 %collective-permute-start.13 = (bf16[4,480,128]{2,1,0:T(8,128)(2,1)S(1)}, bf16[4,480,128]{2,1,0:T(8,128)(2,1)S(1)}, u32[]{:S(2)}, u32[]{:S(2)}) collective-permute-start(bf16[4,480,128]{2,1,0:T(8,128)(2,1)S(1)} %get-tuple-element.83), channel_id=1, source_target_pairs={{0,48},{16,0},{32,16},{48,32},{1,49},{17,1},{33,17},{49,33},{2,50}... | collective-permute-start | bytes 1474568 | tf_op jit(solution)/shard_map/gather/ppermute | solution.py:295
  93.6 26.9 %collective-permute-start.14 = (bf16[4,480,128]{2,1,0:T(8,128)(2,1)S(1)}, bf16[4,480,128]{2,1,0:T(8,128)(2,1)S(1)}, u32[]{:S(2)}, u32[]{:S(2)}) collective-permute-start(bf16[4,480,128]{2,1,0:T(8,128)(2,1)S(1)} %collective-permute-done.8.refs_3_), channel_id=1, source_target_pairs={{0,16},{16,32},{32,48},{48,0},{1,17},{17,33},{33,49},{49,1},{2,18}... | collective-permute-start | bytes 1474568 | tf_op jit(solution)/shard_map/gather/ppermute | solution.py:295
  93.7 28.9 %collective-permute-start.15 = (bf16[4,480,128]{2,1,0:T(8,128)(2,1)S(1)}, bf16[4,480,128]{2,1,0:T(8,128)(2,1)}, u32[]{:S(2)}, u32[]{:S(2)}) collective-permute-start(bf16[4,480,128]{2,1,0:T(8,128)(2,1)S(1)} %collective-permute-done.13.refs_2_), channel_id=1, source_target_pairs={{0,48},{16,0},{32,16},{48,32},{1,49},{17,1},{33,17},{49,33},{2,50}... | collective-permute-start | bytes 1474568 | tf_op jit(solution)/shard_map/gather/ppermute | solution.py:295
  96.5 24.1 %collective-permute-start.17 = (bf16[2,496,128]{2,1,0:T(8,128)(2,1)S(1)}, bf16[2,496,128]{2,1,0:T(8,128)(2,1)S(1)}, u32[]{:S(2)}, u32[]{:S(2)}) collective-permute-start(bf16[2,496,128]{2,1,0:T(8,128)(2,1)S(1)} %slice.16), channel_id=1, source_target_pairs={{0,2},{2,4},{4,6},{6,8},{8,10},{10,12},{12,14},{14,0},{1,3},{3,5},... | collective-permute-start | bytes 761864 | tf_op jit(solution)/shard_map/gather/ppermute | solution.py:295
  96.6 24.0 %collective-permute-start.18 = (bf16[2,496,128]{2,1,0:T(8,128)(2,1)S(1)}, bf16[2,496,128]{2,1,0:T(8,128)(2,1)S(1)}, u32[]{:S(2)}, u32[]{:S(2)}) collective-permute-start(bf16[2,496,128]{2,1,0:T(8,128)(2,1)S(1)} %slice.17), channel_id=1, source_target_pairs={{0,14},{2,0},{4,2},{6,4},{8,6},{10,8},{12,10},{14,12},{1,15},{3,1}... | collective-permute-start | bytes 761864 | tf_op jit(solution)/shard_map/gather/ppermute | solution.py:295
  130.6 9.9 %collective-permute-start.19 = (bf16[320,224]{1,0:T(8,128)(2,1)}, bf16[320,224]{1,0:T(8,128)(2,1)S(1)}, u32[]{:S(2)}, u32[]{:S(2)}) collective-permute-start(bf16[320,224]{1,0:T(8,128)(2,1)} %get-tuple-element.70), channel_id=1, source_target_pairs={{0,1},{1,0},{2,3},{3,2},{4,5},{5,4},{6,7},{7,6},{8,9},{9,8},{10,11... | collective-permute-start | bytes 430088 | tf_op jit(solution)/shard_map/act/ppermute | solution.py:295
  149.4 33.1 %all-to-all-start.2 = ((bf16[8,4,128,128]{3,2,1,0:T(8,128)(2,1)}), bf16[8,4,128,128]{3,2,1,0:T(8,128)(2,1)S(1)}, u32[]{:S(2)}, u32[]{:S(2)}) async-start(bf16[8,4,128,128]{3,2,1,0:T(8,128)(2,1)} %get-tuple-element.71), calls=%async_computation.2 | async-start | bytes 2097152 | tf_op jit(solution)/shard_map/scatter/all_to_all | solution.py:380
  155.9 9.7 %collective-permute-start.20 = (bf16[8,208,128]{2,1,0:T(8,128)(2,1)S(1)}, bf16[8,208,128]{2,1,0:T(8,128)(2,1)S(1)}, u32[]{:S(2)}, u32[]{:S(2)}) collective-permute-start(bf16[8,208,128]{2,1,0:T(8,128)(2,1)S(1)} %copy-done.21), channel_id=1, source_target_pairs={{0,32},{16,48},{32,0},{48,16},{1,33},{17,49},{33,1},{49,17},{2,34}... | collective-permute-start | bytes 1277960 | tf_op jit(solution)/shard_map/scatter/ppermute | solution.py:295
  157.8 20.3 %collective-permute-start.21 = (bf16[8,208,128]{2,1,0:T(8,128)(2,1)S(1)}, bf16[8,208,128]{2,1,0:T(8,128)(2,1)S(1)}, u32[]{:S(2)}, u32[]{:S(2)}) collective-permute-start(bf16[8,208,128]{2,1,0:T(8,128)(2,1)S(1)} %copy-done.20), channel_id=1, source_target_pairs={{0,16},{16,32},{32,48},{48,0},{1,17},{17,33},{33,49},{49,1},{2,18}... | collective-permute-start | bytes 1277960 | tf_op jit(solution)/shard_map/scatter/ppermute | solution.py:295
  158.8 19.3 %collective-permute-start.22 = (bf16[8,208,128]{2,1,0:T(8,128)(2,1)S(1)}, bf16[8,208,128]{2,1,0:T(8,128)(2,1)S(1)}, u32[]{:S(2)}, u32[]{:S(2)}) collective-permute-start(bf16[8,208,128]{2,1,0:T(8,128)(2,1)S(1)} %copy-done.19), channel_id=1, source_target_pairs={{0,48},{16,0},{32,16},{48,32},{1,49},{17,1},{33,17},{49,33},{2,50}... | collective-permute-start | bytes 1277960 | tf_op jit(solution)/shard_map/scatter/ppermute | solution.py:295
  182.6 19.1 %all-to-all-start.3 = ((bf16[8,208,128]{2,1,0:T(8,128)(2,1)}), bf16[8,208,128]{2,1,0:T(8,128)(2,1)S(1)}, u32[]{:S(2)}, u32[]{:S(2)}) async-start(bf16[8,208,128]{2,1,0:T(8,128)(2,1)} %scatter.2), calls=%async_computation.3 | async-start | bytes 851968 | tf_op jit(solution)/shard_map/scatter/all_to_all | solution.py:385
  (36 other events, 558.6 us)

commit v3 on v2

--- a/solution.py
+++ b/solution.py
@@ -29,17 +29,24 @@
 BF16 = jnp.bfloat16
 NT = (((1,), (1,)), ((), ()))
 TN = (((0,), (0,)), ((), ()))
-VMEM_LIMIT = 60 * 1024 * 1024
-
-
-def call(kernel, outs, us, scratch=()):
-    return pl.pallas_call(
+
+
+def call(kernel, outs, us, scratch=(), limit=16):
+    here = pl.BlockSpec(memory_space=pltpu.VMEM)
+
+    def called(*arrays):
+        return run(arrays)(*arrays)
+
+    run = lambda arrays: pl.pallas_call(
         kernel,
+        in_specs=[here] * len(arrays),
+        out_specs=[here] * len(outs),
         out_shape=[jax.ShapeDtypeStruct(s, t) for s, t in outs],
         scratch_shapes=list(scratch),
-        compiler_params=pltpu.CompilerParams(vmem_limit_bytes=VMEM_LIMIT),
+        compiler_params=pltpu.CompilerParams(vmem_limit_bytes=limit * 1024 * 1024),
         cost_estimate=pl.CostEstimate(flops=us * 1_000_000_000, bytes_accessed=0, transcendentals=0),
     )
+    return called
 
 
 def slots_of(ids):
@@ -73,7 +80,8 @@
         terms.append(lax.dot_general(table, values, NT, preferred_element_type=F32))
     routed = terms[0] + terms[1]
     low = lax.broadcasted_iota(jnp.int32, (MINE, LANES), 1) < LANES // 2
-    gain = jnp.broadcast_to(gain_ref[0:1, :].astype(F32), (MINE, LANES))
+    gain = gain_ref[...].astype(F32)
+    gain = jnp.broadcast_to(jnp.concatenate([gain, gain], axis=1), (MINE, LANES))
     for e in range(GROUPS):
         first = routed[e * CAP : e * CAP + MINE]
         second = routed[e * CAP + MINE : (e + 1) * CAP]
@@ -83,7 +91,8 @@
             out_ref[e, k, pl.ds(MINE, MINE), :] = jnp.where(low, second, gain).astype(BF16)
 
 
-def assemble_kernel(got_ref, a_ref, b_ref):
+def assemble_kernel(got_ref, copies_ref, b_ref):
+    a_ref = copies_ref.at[0]
     grads = []
     for g in range(GROUPS):
         low, high = got_ref[g, 0].astype(F32), got_ref[g, 1].astype(F32)
@@ -96,6 +105,8 @@
     b_ref[pl.ds(0, CAP - SPLIT), :] = grads[0][SPLIT:]
     for g in range(1, GROUPS):
         b_ref[pl.ds(g * CAP - SPLIT, CAP), :] = grads[g]
+    for z in range(1, NZ):
+        copies_ref[z] = copies_ref[0]
 
 
 def block(y, z):
@@ -285,7 +296,8 @@
     found = jnp.dot(scalars.astype(BF16), table, preferred_element_type=F32)
     coefficient = found[0:1] + found[1:2] + found[2:3]
     inverse_rms = 0.5 * (found[3:4] + found[4:5] + found[5:6])
-    gain = jnp.transpose(gain_ref[...].astype(F32))[:, 0:1]
+    gain = jnp.broadcast_to(gain_ref[...].astype(F32), (LANES, gain_ref.shape[1]))
+    gain = jnp.transpose(gain)[:, 0:1]
     x = x_ref[...].astype(F32)
     out_ref[...] = (inverse_rms * (token_grad * gain) - x * coefficient).astype(BF16)
 
@@ -311,23 +323,22 @@
     wg, wu, wd = w_gate[0], w_up[0], w_down[0]
     ids, probs = expert_ids.T, gate_probs.T
     x_t, grad_t = residual_stream.T, grad_output.T
-    gain_rows = jnp.broadcast_to(jnp.concatenate([norm_gain, norm_gain])[None], (GAIN_ROWS, LANES))
+    gain_row = norm_gain[None]
     hidden = wg.shape[0]
 
     with jax.named_scope("dispatch"):
         [routed] = call(dispatch_kernel, [((GROUPS, 2, CAP, LANES), BF16)], 2)(
-            ids, probs, x_t, grad_t, gain_rows
+            ids, probs, x_t, grad_t, gain_row
         )
         got = lax.all_to_all(routed.reshape(2 * GROUPS, CAP, LANES), LINE, 0, 0, tiled=True)
         got, own_wg = lax.optimization_barrier((got, wg))
-        piece_a, piece_b = call(
-            assemble_kernel, [((XROWS + SPLIT, LANES), BF16), ((ROWS - SPLIT, LANES), BF16)], 2
+        copies, piece_b = call(
+            assemble_kernel, [((NZ, XROWS + SPLIT, LANES), BF16), ((ROWS - SPLIT, LANES), BF16)], 2
         )(got.reshape(GROUPS, 2, CAP, LANES))
 
     with jax.named_scope("weights"):
         wgp = shift(own_wg, "kv", 1)
     with jax.named_scope("gather"):
-        copies = jnp.broadcast_to(piece_a[None], (NZ, *piece_a.shape))
         line_a = lax.all_to_all(copies, "tensor_1", 0, 0, tiled=True)
         line_b = jnp.stack([piece_b] + [shift(piece_b, "tensor_0", -a) for a in (1, 2, 3)])
 
@@ -336,11 +347,11 @@
         def meet(step, right, left):
             nonlocal line_a, wgp
             if step == 2:
-                right, left, line_a = lax.optimization_barrier((right, left, line_a))
+                right, left, line_a, wgp = lax.optimization_barrier((right, left, line_a, wgp))
                 near[:] = [shift(line_a[: NZ // 2], "tensor_0", by) for by in (1, -1)]
                 far[:] = [shift(line_a[NZ // 2 :], "tensor_0", by) for by in (1, -1)]
             if step == 3:
-                right, left, wgp, *near[:] = lax.optimization_barrier((right, left, wgp, *near))
+                right, left, *near[:] = lax.optimization_barrier((right, left, *near))
             if step == 4:
                 right, left, *far[:] = lax.optimization_barrier((right, left, *far))
             return right, left
@@ -354,7 +365,6 @@
         wup = shift(own_wu, "kv", 1)
 
     with jax.named_scope("act"):
-        wd, wgp, wup = lax.optimization_barrier((wd, wgp, wup))
         act, theirs = call(
             act_kernel,
             [((HALF, hidden), F32), ((HALF, hidden), BF16)],
@@ -388,9 +398,8 @@
     with jax.named_scope("combine"):
         [pieces] = call(finish_kernel, [((2 * GROUPS, MINE + EXTRA, LANES), BF16)], 2)(*top, low, inv)
         got = lax.all_to_all(pieces, LINE, 0, 0, tiled=True)
-        gain_square = jnp.broadcast_to(norm_gain[None], (LANES, norm_gain.shape[0]))
         [out] = call(combine_kernel, [(x_t.shape, BF16)], 2)(
-            got, ids, x_t, gain_square
+            got, ids, x_t, gain_row
         )
     return out.T
 

time: 220 us -> 185 us (0.84)
  Pallas kernels: 37.9 us -> 20.9 us
  waiting for transfers between devices: 91.2 us -> 82.2 us
  starting transfers between devices: 53.2 us -> 47.8 us
  local copies, waits for them, and re-layouts: 8.65 us -> 4.44 us
    pallas_call x9, Pallas kernels: 37.9 us -> 20.9 us  [called(): return run(arrays)(*arrays)]
    ppermute x26, waiting for transfers between devices: 84.9 us -> 73.3 us  [shift(): return lax.ppermute(value, axis, [(i, (i + by) % n) for i in range(n)])]
    all_to_all x1, blocking collectives: 12.2 us -> 15.9 us  [shards(): got = lax.all_to_all(pieces, LINE, 0, 0, tiled=True)]
    broadcast_in_dim x3 -> x0, local copies, waits for them, and re-layouts: 3.33 us -> none  [the longest x1 2.12 us: shards(): copies = jnp.broadcast_to(piece_a[None], (NZ, *piece_a.shape))]
    ppermute x26, starting transfers between devices: 34.9 us -> 32.1 us  [shift(): return lax.ppermute(value, axis, [(i, (i + by) % n) for i in range(n)])]
    all_to_all x1, waiting for transfers between devices: 1.15 us -> 3.57 us  [shards(): top = lax.all_to_all(top, 'tensor_1', 0, 0, tiled=True)]
    all_to_all x1, starting transfers between devices: 6.43 us -> 4.09 us  [shards(): top = lax.all_to_all(top, 'tensor_1', 0, 0, tiled=True)]
    unnamed x62 -> x24, local copies, waits for them, and re-layouts: 5.22 us -> 4.34 us
  transfers between devices with their start and end apart: 29 -> 29, of which waited for: 12 -> 17; matrix products, arithmetic and copies ran while one was open for 0% -> 0% of each run, Pallas kernels for 6% -> 7%
where the time goes in v3:
time: 185 us
  waiting for transfers between devices  82.2 us (44%)
  starting transfers between devices  47.8 us (26%)
  blocking collectives  29.1 us (16%)
  Pallas kernels  20.9 us (11%)
  local copies, waits for them, and re-layouts  4.44 us (2%)
    ppermute x26, waiting for transfers between devices, shift(): return lax.ppermute(value, axis, [(i, (i + by) % n) for i in range(n)])  73.3 us
    ppermute x26, starting transfers between devices, shift(): return lax.ppermute(value, axis, [(i, (i + by) % n) for i in range(n)])  32.1 us
    pallas_call x9, Pallas kernels, called(): return run(arrays)(*arrays)  20.9 us
    all_to_all x1, blocking collectives, shards(): got = lax.all_to_all(pieces, LINE, 0, 0, tiled=True)  15.9 us
    all_to_all x1, blocking collectives, shards(): lax.all_to_all(routed.reshape(2 * GROUPS, CAP, LANES), LINE, 0, 0, tiled=...  13.2 us
    all_to_all x1, starting transfers between devices, shards(): line_a = lax.all_to_all(copies, 'tensor_1', 0, 0, tiled=True)  8.17 us
    all_to_all x1, waiting for transfers between devices, shards(): low = lax.all_to_all(low, 'tensor_1', 0, 0, tiled=True)  5.33 us
    unnamed x24, local copies, waits for them, and re-layouts  4.34 us
  transfers between devices with their start and end apart: 29, of which 17 were waited for; matrix products, arithmetic and copies ran while one was open for 0% of the time, Pallas kernels for 7%

profile of v3, /device:TPU:1, one launch (start us, length us, event | category | flops | bytes accessed | tf_op | source)
XLA Modules:
  0.0 184.6 jit_solution(16673361595108882924)
XLA Ops:
  4.0 13.2 %all_to_all.25 = bf16[8,160,128]{2,1,0:T(8,128)(2,1)S(1)} all-to-all(bf16[8,160,128]{2,1,0:T(8,128)(2,1)S(1)} %bitcast.16), channel_id=1, replica_groups=mesh['expert'=4,'tensor_0'=4,'tensor_1'=8,'kv'=2] {'expert','kv'}, dimensions={0} | all-to-all | bytes 655360 | tf_op jit(solution)/shard_map/dispatch/all_to_all | solution.py:333
  19.2 8.2 %all-to-all-start.1 = ((bf16[8,480,128]{2,1,0:T(8,128)(2,1)}), bf16[8,480,128]{2,1,0:T(8,128)(2,1)S(1)}, u32[]{:S(2)}, u32[]{:S(2)}) async-start(bf16[8,480,128]{2,1,0:T(8,128)(2,1)} %get-tuple-element.43), calls=%async_computation.1 | async-start | bytes 1966080 | tf_op jit(solution)/shard_map/gather/all_to_all | solution.py:342
  28.7 2.6 %collective-permute-start.1 = (bf16[496,128]{1,0:T(8,128)(2,1)S(1)}, bf16[496,128]{1,0:T(8,128)(2,1)S(1)}, u32[]{:S(2)}, u32[]{:S(2)}) collective-permute-start(bf16[496,128]{1,0:T(8,128)(2,1)S(1)} %get-tuple-element.42), channel_id=1, source_target_pairs={{0,32},{16,48},{32,0},{48,16},{1,33},{17,49},{33,1},{49,17},{2,34}... | collective-permute-start | bytes 380936 | tf_op jit(solution)/shard_map/gather/ppermute | solution.py:307
  32.8 3.4 %collective-permute-done.1 = bf16[496,128]{1,0:T(8,128)(2,1)S(1)} collective-permute-done((bf16[496,128]{1,0:T(8,128)(2,1)S(1)}, bf16[496,128]{1,0:T(8,128)(2,1)S(1)}, u32[]{:S(2)}, u32[]{:S(2)}) %collective-permute-start.1) | collective-permute-done | bytes 127008 | tf_op jit(solution)/shard_map/gather/ppermute | solution.py:307
  36.9 2.6 %collective-permute-start.4 = (bf16[4,496,128]{2,1,0:T(8,128)(2,1)S(1)}, bf16[4,496,128]{2,1,0:T(8,128)(2,1)S(1)}, u32[]{:S(2)}, u32[]{:S(2)}) collective-permute-start(bf16[4,496,128]{2,1,0:T(8,128)(2,1)S(1)} %pad_maximum_fusion.refs_7_), channel_id=1, source_target_pairs={{0,14},{2,0},{4,2},{6,4},{8,6},{10,8},{12,10},{14,12},{1,15},{3,1}... | collective-permute-start | bytes 1523720 | tf_op jit(solution)/shard_map/gather/ppermute | solution.py:307
  39.5 21.1 %collective-permute-done.4.refs_8_ = bf16[4,496,128]{2,1,0:T(8,128)(2,1)S(1)} collective-permute-done((bf16[4,496,128]{2,1,0:T(8,128)(2,1)S(1)}, bf16[4,496,128]{2,1,0:T(8,128)(2,1)S(1)}, u32[]{:S(2)}, u32[]{:S(2)}) %collective-permute-start.4) | collective-permute-done | bytes 507936 | tf_op jit(solution)/shard_map/gather/ppermute | solution.py:307
  62.6 3.2 %collective-permute-start.7 = (bf16[4,496,128]{2,1,0:T(8,128)(2,1)}, bf16[4,496,128]{2,1,0:T(8,128)(2,1)S(1)}, u32[]{:S(2)}, u32[]{:S(2)}) collective-permute-start(bf16[4,496,128]{2,1,0:T(8,128)(2,1)} %copy-done.2), channel_id=1, source_target_pairs={{0,14},{2,0},{4,2},{6,4},{8,6},{10,8},{12,10},{14,12},{1,15},{3,1}... | collective-permute-start | bytes 1523720 | tf_op jit(solution)/shard_map/gather/ppermute | solution.py:307
  65.9 2.8 %collective-permute-start.9 = (bf16[4,480,128]{2,1,0:T(8,128)(2,1)S(1)}, bf16[4,480,128]{2,1,0:T(8,128)(2,1)S(1)}, u32[]{:S(2)}, u32[]{:S(2)}) collective-permute-start(bf16[4,480,128]{2,1,0:T(8,128)(2,1)S(1)} %get-tuple-element.78), channel_id=1, source_target_pairs={{0,48},{16,0},{32,16},{48,32},{1,49},{17,1},{33,17},{49,33},{2,50}... | collective-permute-start | bytes 1474568 | tf_op jit(solution)/shard_map/gather/ppermute | solution.py:307
  68.7 1.6 collective-permute-start.16
  70.3 7.4 %collective-permute-done.9.refs_1_ = bf16[4,480,128]{2,1,0:T(8,128)(2,1)S(1)} collective-permute-done((bf16[4,480,128]{2,1,0:T(8,128)(2,1)S(1)}, bf16[4,480,128]{2,1,0:T(8,128)(2,1)S(1)}, u32[]{:S(2)}, u32[]{:S(2)}) %collective-permute-start.9) | collective-permute-done | bytes 491552 | tf_op jit(solution)/shard_map/gather/ppermute | solution.py:307
  77.7 3.1 %collective-permute-done.8.refs_3_ = bf16[4,480,128]{2,1,0:T(8,128)(2,1)S(1)} collective-permute-done((bf16[4,480,128]{2,1,0:T(8,128)(2,1)S(1)}, bf16[4,480,128]{2,1,0:T(8,128)(2,1)S(1)}, u32[]{:S(2)}, u32[]{:S(2)}) %collective-permute-start.8) | collective-permute-done | bytes 491552 | tf_op jit(solution)/shard_map/gather/ppermute | solution.py:307
  80.8 2.7 %collective-permute-start.11 = (bf16[4,496,128]{2,1,0:T(8,128)(2,1)S(1)}, bf16[4,496,128]{2,1,0:T(8,128)(2,1)S(1)}, u32[]{:S(2)}, u32[]{:S(2)}) collective-permute-start(bf16[4,496,128]{2,1,0:T(8,128)(2,1)S(1)} %collective-permute-done.7.refs_9_), channel_id=1, source_target_pairs={{0,14},{2,0},{4,2},{6,4},{8,6},{10,8},{12,10},{14,12},{1,15},{3,1}... | collective-permute-start | bytes 1523720 | tf_op jit(solution)/shard_map/gather/ppermute | solution.py:307
  85.0 8.0 %collective-permute-done.13.refs_2_ = bf16[4,480,128]{2,1,0:T(8,128)(2,1)S(1)} collective-permute-done((bf16[4,480,128]{2,1,0:T(8,128)(2,1)S(1)}, bf16[4,480,128]{2,1,0:T(8,128)(2,1)S(1)}, u32[]{:S(2)}, u32[]{:S(2)}) %collective-permute-start.13) | collective-permute-done | bytes 491552 | tf_op jit(solution)/shard_map/gather/ppermute | solution.py:307
  97.3 8.3 %collective-permute-done.14.refs_5_ = bf16[4,480,128]{2,1,0:T(8,128)(2,1)S(1)} collective-permute-done((bf16[4,480,128]{2,1,0:T(8,128)(2,1)S(1)}, bf16[4,480,128]{2,1,0:T(8,128)(2,1)S(1)}, u32[]{:S(2)}, u32[]{:S(2)}) %collective-permute-start.14) | collective-permute-done | bytes 491552 | tf_op jit(solution)/shard_map/gather/ppermute | solution.py:307
  105.6 4.4 %act.1 = (f32[320,224]{1,0:T(8,128)S(1)}, bf16[320,224]{1,0:T(8,128)(2,1)S(1)}) custom-call(bf16[8,480,128]{2,1,0:T(8,128)(2,1)S(1)} %all-to-all-done.1.refs_0_, bf16[4,480,128]{2,1,0:T(8,128)(2,1)S(1)} %collective-permute-done.9.refs_1_, bf16[4,480,128]{2,1,0:T(8,128)(2,1)S(1)} %collective-permute-done.13.refs_2_, ...), custom_call_target="tpu_custom_call" | custom-call | flops 7000000000 | tf_op jit(solution)/shard_map/act/pallas_call | solution.py:38
  111.3 6.4 %forward.1 = (f32[320,224]{1,0:T(8,128)S(1)}, f32[320,224]{1,0:T(8,128)S(1)}, f32[320,224]{1,0:T(8,128)S(1)}, f32[320,224]{1,0:T(8,128)S(1)}, f32[1,384]{1,0:T(1,128)S(1)}) custom-call(bf16[8,480,128]{2,1,0:T(8,128)(2,1)S(1)} %all-to-all-done.1.refs_0_, bf16[4,480,128]{2,1,0:T(8,128)(2,1)S(1)} %collective-permute-done.9.refs_1_, ...), custom_call_target="tpu_custom_call" | custom-call | flops 8000000000 | tf_op jit(solution)/shard_map/forward/pallas_call | solution.py:38
  117.7 6.1 %back.1 = (bf16[8,4,128,128]{3,2,1,0:T(8,128)(2,1)}, bf16[8,208,128]{2,1,0:T(8,128)(2,1)S(1)}, bf16[8,208,128]{2,1,0:T(8,128)(2,1)S(1)}, bf16[8,208,128]{2,1,0:T(8,128)(2,1)S(1)}, bf16[8,208,128]{2,1,0:T(8,128)(2,1)S(1)}) custom-call(f32[320,224]{1,0:T(8,128)S(1)} %get-tuple-element.57.refs_0_, f32[320,224]{1,0:T(8,128)S(1)} %get-tuple-element.58.refs_1_, ...), custom_call_target="tpu_custom_call" | custom-call | flops 8000000000 | tf_op jit(solution)/shard_map/back/pallas_call | solution.py:38
  123.8 4.1 %all-to-all-start.2 = ((bf16[8,4,128,128]{3,2,1,0:T(8,128)(2,1)}), bf16[8,4,128,128]{3,2,1,0:T(8,128)(2,1)S(1)}, u32[]{:S(2)}, u32[]{:S(2)}) async-start(bf16[8,4,128,128]{3,2,1,0:T(8,128)(2,1)} %get-tuple-element.65), calls=%async_computation.2 | async-start | bytes 2097152 | tf_op jit(solution)/shard_map/scatter/all_to_all | solution.py:390
  131.8 4.7 %collective-permute-done.20.refs_1_ = bf16[8,208,128]{2,1,0:T(8,128)(2,1)S(1)} collective-permute-done((bf16[8,208,128]{2,1,0:T(8,128)(2,1)S(1)}, bf16[8,208,128]{2,1,0:T(8,128)(2,1)S(1)}, u32[]{:S(2)}, u32[]{:S(2)}) %collective-permute-start.20) | collective-permute-done | bytes 426016 | tf_op jit(solution)/shard_map/scatter/ppermute | solution.py:307
  136.5 12.0 %collective-permute-done.21.refs_2_ = bf16[8,208,128]{2,1,0:T(8,128)(2,1)S(1)} collective-permute-done((bf16[8,208,128]{2,1,0:T(8,128)(2,1)S(1)}, bf16[8,208,128]{2,1,0:T(8,128)(2,1)S(1)}, u32[]{:S(2)}, u32[]{:S(2)}) %collective-permute-start.21) | collective-permute-done | bytes 426016 | tf_op jit(solution)/shard_map/scatter/ppermute | solution.py:307
  149.4 3.6 %all-to-all-done.2.got_ref = bf16[8,4,128,128]{3,2,1,0:T(8,128)(2,1)S(1)} async-done(((bf16[8,4,128,128]{3,2,1,0:T(8,128)(2,1)}), bf16[8,4,128,128]{3,2,1,0:T(8,128)(2,1)S(1)}, u32[]{:S(2)}, u32[]{:S(2)}) %all-to-all-start.2) | async-done | bytes 1048608 | tf_op jit(solution)/shard_map/scatter/all_to_all | solution.py:390
  153.0 3.5 %all-to-all-start.3 = ((bf16[8,208,128]{2,1,0:T(8,128)(2,1)}), bf16[8,208,128]{2,1,0:T(8,128)(2,1)S(1)}, u32[]{:S(2)}, u32[]{:S(2)}) async-start(bf16[8,208,128]{2,1,0:T(8,128)(2,1)} %scatter.2), calls=%async_computation.3 | async-start | bytes 851968 | tf_op jit(solution)/shard_map/scatter/all_to_all | solution.py:395
  162.2 5.3 %all-to-all-done.3.refs_4_ = bf16[8,208,128]{2,1,0:T(8,128)(2,1)S(1)} async-done(((bf16[8,208,128]{2,1,0:T(8,128)(2,1)}), bf16[8,208,128]{2,1,0:T(8,128)(2,1)S(1)}, u32[]{:S(2)}, u32[]{:S(2)}) %all-to-all-start.3) | async-done | bytes 426016 | tf_op jit(solution)/shard_map/scatter/all_to_all | solution.py:395
  167.7 15.9 %all_to_all.26.got_ref = bf16[8,96,128]{2,1,0:T(8,128)(2,1)S(1)} all-to-all(bf16[8,96,128]{2,1,0:T(8,128)(2,1)S(1)} %combine.2), channel_id=1, replica_groups=mesh['expert'=4,'tensor_0'=4,'tensor_1'=8,'kv'=2] {'expert','kv'}, dimensions={0} | all-to-all | bytes 393216 | tf_op jit(solution)/shard_map/combine/all_to_all | solution.py:400
  (73 shorter events, 30.5 us)
Async XLA Ops:
  17.2 45.3 %collective-permute-start.5 = (bf16[224,4096]{1,0:T(8,128)(2,1)}, bf16[224,4096]{1,0:T(8,128)(2,1)}, u32[]{:S(2)}, u32[]{:S(2)}) collective-permute-start(bf16[224,4096]{1,0:T(8,128)(2,1)} %bitcast.6.refs_7_.refs_6_), channel_id=1, source_target_pairs={{0,1},{1,0},{2,3},{3,2},{4,5},{5,4},{6,7},{7,6},{8,9},{9,8},{10,11... | collective-permute-start | bytes 5505032 | tf_op jit(solution)/shard_map/weights/ppermute | solution.py:307
  19.2 43.3 %all-to-all-start.1 = ((bf16[8,480,128]{2,1,0:T(8,128)(2,1)}), bf16[8,480,128]{2,1,0:T(8,128)(2,1)S(1)}, u32[]{:S(2)}, u32[]{:S(2)}) async-start(bf16[8,480,128]{2,1,0:T(8,128)(2,1)} %get-tuple-element.43), calls=%async_computation.1 | async-start | bytes 1966080 | tf_op jit(solution)/shard_map/gather/all_to_all | solution.py:342
  28.7 7.6 %collective-permute-start.1 = (bf16[496,128]{1,0:T(8,128)(2,1)S(1)}, bf16[496,128]{1,0:T(8,128)(2,1)S(1)}, u32[]{:S(2)}, u32[]{:S(2)}) collective-permute-start(bf16[496,128]{1,0:T(8,128)(2,1)S(1)} %get-tuple-element.42), channel_id=1, source_target_pairs={{0,32},{16,48},{32,0},{48,16},{1,33},{17,49},{33,1},{49,17},{2,34}... | collective-permute-start | bytes 380936 | tf_op jit(solution)/shard_map/gather/ppermute | solution.py:307
  36.9 23.6 %collective-permute-start.4 = (bf16[4,496,128]{2,1,0:T(8,128)(2,1)S(1)}, bf16[4,496,128]{2,1,0:T(8,128)(2,1)S(1)}, u32[]{:S(2)}, u32[]{:S(2)}) collective-permute-start(bf16[4,496,128]{2,1,0:T(8,128)(2,1)S(1)} %pad_maximum_fusion.refs_7_), channel_id=1, source_target_pairs={{0,14},{2,0},{4,2},{6,4},{8,6},{10,8},{12,10},{14,12},{1,15},{3,1}... | collective-permute-start | bytes 1523720 | tf_op jit(solution)/shard_map/gather/ppermute | solution.py:307
  39.5 23.0 %collective-permute-start.3 = (bf16[4,496,128]{2,1,0:T(8,128)(2,1)S(1)}, bf16[4,496,128]{2,1,0:T(8,128)(2,1)}, u32[]{:S(2)}, u32[]{:S(2)}) collective-permute-start(bf16[4,496,128]{2,1,0:T(8,128)(2,1)S(1)} %pad_maximum_fusion.refs_7_), channel_id=1, source_target_pairs={{0,2},{2,4},{4,6},{6,8},{8,10},{10,12},{12,14},{14,0},{1,3},{3,5},... | collective-permute-start | bytes 1523720 | tf_op jit(solution)/shard_map/gather/ppermute | solution.py:307
  62.5 18.3 %collective-permute-start.6 = (bf16[4,496,128]{2,1,0:T(8,128)(2,1)}, bf16[4,496,128]{2,1,0:T(8,128)(2,1)S(1)}, u32[]{:S(2)}, u32[]{:S(2)}) collective-permute-start(bf16[4,496,128]{2,1,0:T(8,128)(2,1)} %collective-permute-done.3.refs_13_), channel_id=1, source_target_pairs={{0,2},{2,4},{4,6},{6,8},{8,10},{10,12},{12,14},{14,0},{1,3},{3,5},... | collective-permute-start | bytes 1523720 | tf_op jit(solution)/shard_map/gather/ppermute | solution.py:307
  62.6 18.2 %collective-permute-start.7 = (bf16[4,496,128]{2,1,0:T(8,128)(2,1)}, bf16[4,496,128]{2,1,0:T(8,128)(2,1)S(1)}, u32[]{:S(2)}, u32[]{:S(2)}) collective-permute-start(bf16[4,496,128]{2,1,0:T(8,128)(2,1)} %copy-done.2), channel_id=1, source_target_pairs={{0,14},{2,0},{4,2},{6,4},{8,6},{10,8},{12,10},{14,12},{1,15},{3,1}... | collective-permute-start | bytes 1523720 | tf_op jit(solution)/shard_map/gather/ppermute | solution.py:307
  65.9 11.8 %collective-permute-start.9 = (bf16[4,480,128]{2,1,0:T(8,128)(2,1)S(1)}, bf16[4,480,128]{2,1,0:T(8,128)(2,1)S(1)}, u32[]{:S(2)}, u32[]{:S(2)}) collective-permute-start(bf16[4,480,128]{2,1,0:T(8,128)(2,1)S(1)} %get-tuple-element.78), channel_id=1, source_target_pairs={{0,48},{16,0},{32,16},{48,32},{1,49},{17,1},{33,17},{49,33},{2,50}... | collective-permute-start | bytes 1474568 | tf_op jit(solution)/shard_map/gather/ppermute | solution.py:307
  68.7 12.1 %collective-permute-start.8 = (bf16[4,480,128]{2,1,0:T(8,128)(2,1)S(1)}, bf16[4,480,128]{2,1,0:T(8,128)(2,1)S(1)}, u32[]{:S(2)}, u32[]{:S(2)}) collective-permute-start(bf16[4,480,128]{2,1,0:T(8,128)(2,1)S(1)} %get-tuple-element.78), channel_id=1, source_target_pairs={{0,16},{16,32},{32,48},{48,0},{1,17},{17,33},{33,49},{49,1},{2,18}... | collective-permute-start | bytes 1474568 | tf_op jit(solution)/shard_map/gather/ppermute | solution.py:307
  68.7 42.6 %collective-permute-start.16 = (bf16[224,4096]{1,0:T(8,128)(2,1)}, bf16[224,4096]{1,0:T(8,128)(2,1)S(1)}, u32[]{:S(2)}, u32[]{:S(2)}) collective-permute-start(bf16[224,4096]{1,0:T(8,128)(2,1)} %bitcast.19), channel_id=1, source_target_pairs={{0,1},{1,0},{2,3},{3,2},{4,5},{5,4},{6,7},{7,6},{8,9},{9,8},{10,11... | collective-permute-start | bytes 5505032 | tf_op jit(solution)/shard_map/weights/ppermute | solution.py:307
  80.8 13.7 %collective-permute-start.10 = (bf16[4,496,128]{2,1,0:T(8,128)(2,1)S(1)}, bf16[4,496,128]{2,1,0:T(8,128)(2,1)S(1)}, u32[]{:S(2)}, u32[]{:S(2)}) collective-permute-start(bf16[4,496,128]{2,1,0:T(8,128)(2,1)S(1)} %collective-permute-done.6.refs_12_), channel_id=1, source_target_pairs={{0,2},{2,4},{4,6},{6,8},{8,10},{10,12},{12,14},{14,0},{1,3},{3,5},... | collective-permute-start | bytes 1523720 | tf_op jit(solution)/shard_map/gather/ppermute | solution.py:307
  80.8 13.7 %collective-permute-start.11 = (bf16[4,496,128]{2,1,0:T(8,128)(2,1)S(1)}, bf16[4,496,128]{2,1,0:T(8,128)(2,1)S(1)}, u32[]{:S(2)}, u32[]{:S(2)}) collective-permute-start(bf16[4,496,128]{2,1,0:T(8,128)(2,1)S(1)} %collective-permute-done.7.refs_9_), channel_id=1, source_target_pairs={{0,14},{2,0},{4,2},{6,4},{8,6},{10,8},{12,10},{14,12},{1,15},{3,1}... | collective-permute-start | bytes 1523720 | tf_op jit(solution)/shard_map/gather/ppermute | solution.py:307
  83.5 9.4 %collective-permute-start.13 = (bf16[4,480,128]{2,1,0:T(8,128)(2,1)S(1)}, bf16[4,480,128]{2,1,0:T(8,128)(2,1)S(1)}, u32[]{:S(2)}, u32[]{:S(2)}) collective-permute-start(bf16[4,480,128]{2,1,0:T(8,128)(2,1)S(1)} %get-tuple-element.77), channel_id=1, source_target_pairs={{0,48},{16,0},{32,16},{48,32},{1,49},{17,1},{33,17},{49,33},{2,50}... | collective-permute-start | bytes 1474568 | tf_op jit(solution)/shard_map/gather/ppermute | solution.py:307
  83.9 10.7 %collective-permute-start.12 = (bf16[4,480,128]{2,1,0:T(8,128)(2,1)S(1)}, bf16[4,480,128]{2,1,0:T(8,128)(2,1)S(1)}, u32[]{:S(2)}, u32[]{:S(2)}) collective-permute-start(bf16[4,480,128]{2,1,0:T(8,128)(2,1)S(1)} %get-tuple-element.77), channel_id=1, source_target_pairs={{0,16},{16,32},{32,48},{48,0},{1,17},{17,33},{33,49},{49,1},{2,18}... | collective-permute-start | bytes 1474568 | tf_op jit(solution)/shard_map/gather/ppermute | solution.py:307
  93.0 12.6 %collective-permute-start.14 = (bf16[4,480,128]{2,1,0:T(8,128)(2,1)S(1)}, bf16[4,480,128]{2,1,0:T(8,128)(2,1)S(1)}, u32[]{:S(2)}, u32[]{:S(2)}) collective-permute-start(bf16[4,480,128]{2,1,0:T(8,128)(2,1)S(1)} %collective-permute-done.8.refs_3_), channel_id=1, source_target_pairs={{0,16},{16,32},{32,48},{48,0},{1,17},{17,33},{33,49},{49,1},{2,18}... | collective-permute-start | bytes 1474568 | tf_op jit(solution)/shard_map/gather/ppermute | solution.py:307
  94.5 11.1 %collective-permute-start.15 = (bf16[4,480,128]{2,1,0:T(8,128)(2,1)S(1)}, bf16[4,480,128]{2,1,0:T(8,128)(2,1)S(1)}, u32[]{:S(2)}, u32[]{:S(2)}) collective-permute-start(bf16[4,480,128]{2,1,0:T(8,128)(2,1)S(1)} %collective-permute-done.13.refs_2_), channel_id=1, source_target_pairs={{0,48},{16,0},{32,16},{48,32},{1,49},{17,1},{33,17},{49,33},{2,50}... | collective-permute-start | bytes 1474568 | tf_op jit(solution)/shard_map/gather/ppermute | solution.py:307
  95.8 9.8 %collective-permute-start.18 = (bf16[2,496,128]{2,1,0:T(8,128)(2,1)S(1)}, bf16[2,496,128]{2,1,0:T(8,128)(2,1)S(1)}, u32[]{:S(2)}, u32[]{:S(2)}) collective-permute-start(bf16[2,496,128]{2,1,0:T(8,128)(2,1)S(1)} %slice.17), channel_id=1, source_target_pairs={{0,14},{2,0},{4,2},{6,4},{8,6},{10,8},{12,10},{14,12},{1,15},{3,1}... | collective-permute-start | bytes 761864 | tf_op jit(solution)/shard_map/gather/ppermute | solution.py:307
  95.9 9.7 %collective-permute-start.17 = (bf16[2,496,128]{2,1,0:T(8,128)(2,1)S(1)}, bf16[2,496,128]{2,1,0:T(8,128)(2,1)S(1)}, u32[]{:S(2)}, u32[]{:S(2)}) collective-permute-start(bf16[2,496,128]{2,1,0:T(8,128)(2,1)S(1)} %slice.16), channel_id=1, source_target_pairs={{0,2},{2,4},{4,6},{6,8},{8,10},{10,12},{12,14},{14,0},{1,3},{3,5},... | collective-permute-start | bytes 761864 | tf_op jit(solution)/shard_map/gather/ppermute | solution.py:307
  110.1 7.6 %collective-permute-start.19 = (bf16[320,224]{1,0:T(8,128)(2,1)S(1)}, bf16[320,224]{1,0:T(8,128)(2,1)S(1)}, u32[]{:S(2)}, u32[]{:S(2)}) collective-permute-start(bf16[320,224]{1,0:T(8,128)(2,1)S(1)} %get-tuple-element.64), channel_id=1, source_target_pairs={{0,1},{1,0},{2,3},{3,2},{4,5},{5,4},{6,7},{7,6},{8,9},{9,8},{10,11... | collective-permute-start | bytes 430088 | tf_op jit(solution)/shard_map/act/ppermute | solution.py:307
  123.8 29.2 %all-to-all-start.2 = ((bf16[8,4,128,128]{3,2,1,0:T(8,128)(2,1)}), bf16[8,4,128,128]{3,2,1,0:T(8,128)(2,1)S(1)}, u32[]{:S(2)}, u32[]{:S(2)}) async-start(bf16[8,4,128,128]{3,2,1,0:T(8,128)(2,1)} %get-tuple-element.65), calls=%async_computation.2 | async-start | bytes 2097152 | tf_op jit(solution)/shard_map/scatter/all_to_all | solution.py:390
  127.9 8.6 %collective-permute-start.20 = (bf16[8,208,128]{2,1,0:T(8,128)(2,1)S(1)}, bf16[8,208,128]{2,1,0:T(8,128)(2,1)S(1)}, u32[]{:S(2)}, u32[]{:S(2)}) collective-permute-start(bf16[8,208,128]{2,1,0:T(8,128)(2,1)S(1)} %get-tuple-element.67), channel_id=1, source_target_pairs={{0,32},{16,48},{32,0},{48,16},{1,33},{17,49},{33,1},{49,17},{2,34}... | collective-permute-start | bytes 1277960 | tf_op jit(solution)/shard_map/scatter/ppermute | solution.py:307
  129.1 19.3 %collective-permute-start.21 = (bf16[8,208,128]{2,1,0:T(8,128)(2,1)S(1)}, bf16[8,208,128]{2,1,0:T(8,128)(2,1)S(1)}, u32[]{:S(2)}, u32[]{:S(2)}) collective-permute-start(bf16[8,208,128]{2,1,0:T(8,128)(2,1)S(1)} %get-tuple-element.68), channel_id=1, source_target_pairs={{0,16},{16,32},{32,48},{48,0},{1,17},{17,33},{33,49},{49,1},{2,18}... | collective-permute-start | bytes 1277960 | tf_op jit(solution)/shard_map/scatter/ppermute | solution.py:307
  130.6 17.8 %collective-permute-start.22 = (bf16[8,208,128]{2,1,0:T(8,128)(2,1)S(1)}, bf16[8,208,128]{2,1,0:T(8,128)(2,1)S(1)}, u32[]{:S(2)}, u32[]{:S(2)}) collective-permute-start(bf16[8,208,128]{2,1,0:T(8,128)(2,1)S(1)} %get-tuple-element.69), channel_id=1, source_target_pairs={{0,48},{16,0},{32,16},{48,32},{1,49},{17,1},{33,17},{49,33},{2,50}... | collective-permute-start | bytes 1277960 | tf_op jit(solution)/shard_map/scatter/ppermute | solution.py:307
  153.0 14.5 %all-to-all-start.3 = ((bf16[8,208,128]{2,1,0:T(8,128)(2,1)}), bf16[8,208,128]{2,1,0:T(8,128)(2,1)S(1)}, u32[]{:S(2)}, u32[]{:S(2)}) async-start(bf16[8,208,128]{2,1,0:T(8,128)(2,1)} %scatter.2), calls=%async_computation.3 | async-start | bytes 851968 | tf_op jit(solution)/shard_map/scatter/all_to_all | solution.py:395
  (17 other events, 191.9 us)

commit v4 on v3

--- a/solution.py
+++ b/solution.py
@@ -20,7 +20,7 @@
 XROWS = HALF + GAIN_ROWS
 SPLIT = 144
 PADDED = 384
-ZFIRST = 128
+ZFIRST = 112
 YFIRST = HALF - ZFIRST
 EXTRA = 16
 TENSOR_KV = ("tensor_0", "tensor_1", "kv")
@@ -31,22 +31,22 @@
 TN = (((0,), (0,)), ((), ()))
 
 
-def call(kernel, outs, us, scratch=(), limit=16):
-    here = pl.BlockSpec(memory_space=pltpu.VMEM)
-
-    def called(*arrays):
-        return run(arrays)(*arrays)
-
-    run = lambda arrays: pl.pallas_call(
-        kernel,
-        in_specs=[here] * len(arrays),
-        out_specs=[here] * len(outs),
-        out_shape=[jax.ShapeDtypeStruct(s, t) for s, t in outs],
-        scratch_shapes=list(scratch),
-        compiler_params=pltpu.CompilerParams(vmem_limit_bytes=limit * 1024 * 1024),
-        cost_estimate=pl.CostEstimate(flops=us * 1_000_000_000, bytes_accessed=0, transcendentals=0),
-    )
-    return called
+def call(kernel, outs, us, scratch=(), limit=6, aliases=None):
+    here = pl.BlockSpec(memory_space=pltpu.VMEM) if limit < 32 else pl.BlockSpec()
+
+    def run(*arrays):
+        return pl.pallas_call(
+            kernel,
+            in_specs=[here] * len(arrays),
+            out_specs=[here] * len(outs),
+            out_shape=[jax.ShapeDtypeStruct(s, t) for s, t in outs],
+            scratch_shapes=list(scratch),
+            input_output_aliases=aliases or {},
+            compiler_params=pltpu.CompilerParams(vmem_limit_bytes=limit * 1024 * 1024),
+            cost_estimate=pl.CostEstimate(flops=us * 1_000_000_000, bytes_accessed=0, transcendentals=0),
+        )(*arrays)
+
+    return run
 
 
 def slots_of(ids):
@@ -123,34 +123,50 @@
     return block(lax.rem(lax.axis_index("tensor_0") + a, NY), z)
 
 
-def a_piece(refs, a, b):
-    if a == 0:
-        return refs[0], b
-    return refs[(None, 1, 5, 3)[a] + b // 4], b % 4
-
-
-def b_piece(refs, a, b):
-    if b == NZ // 2:
-        return refs[NZ - 1 + a // 2], a % 2
-    return refs[b if b < NZ // 2 else b - 1], a
-
-
-PLACES = [(a, b) for a in range(NY) for b in range(NZ)]
-
-
-def act_kernel(*refs):
-    a_refs, b_refs = refs[:7], refs[7:16]
-    wd_ref, mine_ref, theirs_ref, grad_ref, act_ref = refs[16:]
-    for a, b in PLACES:
-        ref, at = a_piece(a_refs, a, b)
-        grad_ref[pl.ds(0, SPLIT), row_of(a, b)] = ref[at, pl.ds(XROWS, SPLIT), :]
-        ref, at = b_piece(b_refs, a, b)
-        grad_ref[pl.ds(SPLIT, ROWS - SPLIT), column(a, b)] = ref[at]
+def place_x(pieces, xs_ref, sq_ref, begins):
+    @pl.loop(0, HALF // 64)
+    def _(r):
+        rows = pl.ds(pl.multiple_of(r * 64, 64), 64)
+        total = jnp.zeros((64, LANES), F32) if begins else sq_ref[rows, :]
+        for ref, at, a, z in pieces:
+            v = ref[at, rows, :].astype(F32)
+            total = total + v * v
+            gain = ref[at, pl.ds(HALF, GAIN_ROWS), :].astype(F32)[0:1]
+            xs_ref[rows, row_of(a, z)] = (v * gain).astype(BF16)
+        sq_ref[rows, :] = total
+
+
+def place_grad(a_pieces, b_pieces, ds_ref):
+    for ref, at, a, z in a_pieces:
+        ds_ref[pl.ds(0, SPLIT), row_of(a, z)] = ref[at, pl.ds(XROWS, SPLIT), :]
+    for ref, at, a, b in b_pieces:
+        ds_ref[pl.ds(SPLIT, ROWS - SPLIT), column(a, b)] = ref[at]
+
+
+def place_first_kernel(line_ref, near1_ref, near3_ref, b0, b1, b2, b6, b7, xs_ref, ds_ref, sq_ref):
+    a_pieces = [(line_ref, z, 0, z) for z in range(NZ)]
+    a_pieces += [(ref, z, a, z) for a, ref in ((1, near1_ref), (3, near3_ref)) for z in range(NZ // 2)]
+    b_pieces = [(ref, a, a, b) for b, ref in ((0, b0), (1, b1), (2, b2), (6, b6), (7, b7)) for a in range(NY)]
+    place_grad(a_pieces, b_pieces, ds_ref)
+    place_x(a_pieces, xs_ref, sq_ref, True)
+
+
+def place_second_kernel(_xs, _ds, _sq, far1_ref, far3_ref, b3, b5, xs_ref, ds_ref, sq_ref):
+    a_pieces = [(ref, z, a, NZ // 2 + z) for a, ref in ((1, far1_ref), (3, far3_ref)) for z in range(NZ // 2)]
+    b_pieces = [(ref, a, a, b) for b, ref in ((3, b3), (5, b5)) for a in range(NY)]
+    place_grad(a_pieces, b_pieces, ds_ref)
+    place_x(a_pieces, xs_ref, sq_ref, False)
+
+
+def act_kernel(_ds, lo_ref, hi_ref, b4lo_ref, b4hi_ref, wd_ref, ds_ref, mine_ref, theirs_ref, act_ref):
+    a_pieces = [((lo_ref, hi_ref)[z // 4], z % 4, 2, z) for z in range(NZ)]
+    b_pieces = [((b4lo_ref, b4hi_ref)[a // 2], a % 2, a, NZ // 2) for a in range(NY)]
+    place_grad(a_pieces, b_pieces, ds_ref)
 
     @pl.loop(0, 2)
     def _(r):
         rows = pl.ds(pl.multiple_of(r * HALF, HALF), HALF)
-        act_ref[rows, :] = lax.dot_general(grad_ref[rows, :], wd_ref[...], NT, preferred_element_type=F32)
+        act_ref[rows, :] = lax.dot_general(ds_ref[rows, :], wd_ref[...], NT, preferred_element_type=F32)
 
     kv = lax.axis_index("kv")
     for g in range(GROUPS):
@@ -166,29 +182,16 @@
 
 
 def forward_kernel(*refs):
-    a_refs = refs[:7]
-    wg_ref, wu_ref, wgp_ref, wup_ref, gate_ref, up_ref, gatep_ref, upp_ref, inv_ref, xn_ref, column_ref = refs[7:]
-
-    @pl.loop(0, HALF // 64)
-    def _(r):
-        rows = pl.ds(pl.multiple_of(r * 64, 64), 64)
-        total = jnp.zeros((64, LANES), F32)
-        for a, b in PLACES:
-            ref, at = a_piece(a_refs, a, b)
-            v = ref[at, rows, :].astype(F32)
-            total = total + v * v
-        inv = lax.rsqrt(jnp.sum(total, axis=1, keepdims=True) / D + EPS)
-        column_ref[rows, :] = jnp.broadcast_to(inv, (64, LANES))
-        for a, b in PLACES:
-            ref, at = a_piece(a_refs, a, b)
-            gain = ref[at, pl.ds(HALF, GAIN_ROWS), :].astype(F32)[0:1]
-            xn_ref[rows, row_of(a, b)] = (ref[at, rows, :].astype(F32) * inv * gain).astype(BF16)
-
+    _xs, _sq, lo_ref, hi_ref, wg_ref, wu_ref, wgp_ref, wup_ref = refs[:8]
+    xs_ref, sq_ref, gate_ref, up_ref, gatep_ref, upp_ref, inv_ref, column_ref = refs[8:]
+    place_x([((lo_ref, hi_ref)[z // 4], z % 4, 2, z) for z in range(NZ)], xs_ref, sq_ref, False)
+    inv = lax.rsqrt(jnp.sum(sq_ref[...], axis=1, keepdims=True) / D + EPS)
+    column_ref[pl.ds(0, HALF), :] = jnp.broadcast_to(inv, (HALF, LANES))
     column_ref[pl.ds(HALF, PADDED - HALF), :] = jnp.zeros((PADDED - HALF, LANES), F32)
     to_row(column_ref, inv_ref)
-    x = xn_ref[...]
+    x = xs_ref[...]
     for w_ref, out_ref in ((wg_ref, gate_ref), (wu_ref, up_ref), (wgp_ref, gatep_ref), (wup_ref, upp_ref)):
-        out_ref[...] = lax.dot_general(x, w_ref[...], NT, preferred_element_type=F32)
+        out_ref[...] = inv * lax.dot_general(x, w_ref[...], NT, preferred_element_type=F32)
 
 
 def split3(value):
@@ -307,15 +310,15 @@
     return lax.ppermute(value, axis, [(i, (i + by) % n) for i in range(n)])
 
 
-def gather_ring(value, axis, cut, meet=lambda step, right, left: (right, left)):
+def gather_ring(value, axis, cut, meet=lambda step, right, left, got: (right, left)):
     n = lax.axis_size(axis)
     got = {0: value}
     right = left = value
     for step in range(1, n // 2):
-        right, left = meet(step, right, left)
+        right, left = meet(step, right, left, got)
         right, left = shift(right, axis, 1), shift(left, axis, -1)
         got[n - step], got[step] = right, left
-    right, left = meet(n // 2, right, left)
+    right, left = meet(n // 2, right, left, got)
     return got, (shift(right[:cut], axis, 1), shift(left[cut:], axis, -1))
 
 
@@ -327,7 +330,7 @@
     hidden = wg.shape[0]
 
     with jax.named_scope("dispatch"):
-        [routed] = call(dispatch_kernel, [((GROUPS, 2, CAP, LANES), BF16)], 2)(
+        [routed] = call(dispatch_kernel, [((GROUPS, 2, CAP, LANES), BF16)], 2, limit=60)(
             ids, probs, x_t, grad_t, gain_row
         )
         got = lax.all_to_all(routed.reshape(2 * GROUPS, CAP, LANES), LINE, 0, 0, tiled=True)
@@ -342,43 +345,50 @@
         line_a = lax.all_to_all(copies, "tensor_1", 0, 0, tiled=True)
         line_b = jnp.stack([piece_b] + [shift(piece_b, "tensor_0", -a) for a in (1, 2, 3)])
 
-        near, far = [], []
-
-        def meet(step, right, left):
-            nonlocal line_a, wgp
+        near, far, state = [], [], None
+        placed = [((HALF, D), BF16), ((ROWS, D), BF16), ((HALF, LANES), F32)]
+
+        def meet(step, right, left, got):
+            nonlocal line_a, wgp, state
             if step == 2:
                 right, left, line_a, wgp = lax.optimization_barrier((right, left, line_a, wgp))
                 near[:] = [shift(line_a[: NZ // 2], "tensor_0", by) for by in (1, -1)]
                 far[:] = [shift(line_a[NZ // 2 :], "tensor_0", by) for by in (1, -1)]
             if step == 3:
                 right, left, *near[:] = lax.optimization_barrier((right, left, *near))
+                early = [got[b] for b in (0, 1, 2, 6, 7)]
+                state = [*call(place_first_kernel, placed, 5)(line_a, near[1], near[0], *early)]
             if step == 4:
-                right, left, *far[:] = lax.optimization_barrier((right, left, *far))
+                right, left, state[2], *far[:] = lax.optimization_barrier((right, left, state[2], *far))
             return right, left
 
         b_got, b_far = gather_ring(line_b, "tensor_1", NY // 2, meet)
-        b_refs = (*[b_got[b] for b in range(NZ) if b != 4], *b_far)
-        a_far = (shift(near[0], "tensor_0", 1), shift(far[1], "tensor_0", -1))
-        a_refs = (line_a, near[1], far[1], near[0], far[0], *a_far)
+        lo, hi = shift(near[0], "tensor_0", 1), shift(far[1], "tensor_0", -1)
+    with jax.named_scope("place"):
+        xs, ds, sq = call(place_second_kernel, placed, 3, aliases={0: 0, 1: 1, 2: 2})(
+            *state, far[1], far[0], b_got[3], b_got[5]
+        )
     with jax.named_scope("weights"):
         wgp, own_wu = lax.optimization_barrier((wgp, wu))
         wup = shift(own_wu, "kv", 1)
 
     with jax.named_scope("act"):
-        act, theirs = call(
+        _, act, theirs = call(
             act_kernel,
-            [((HALF, hidden), F32), ((HALF, hidden), BF16)],
-            7,
-            [pltpu.VMEM((ROWS, D), BF16), pltpu.VMEM((ROWS, hidden), F32)],
-        )(*a_refs, *b_refs, wd)
+            [placed[1], ((HALF, hidden), F32), ((HALF, hidden), BF16)],
+            3,
+            [pltpu.VMEM((ROWS, hidden), F32)],
+            aliases={0: 0},
+        )(ds, lo, hi, *b_far, wd)
         actp = shift(theirs, "kv", 1)
     with jax.named_scope("forward"):
-        gate, up, gatep, upp, inv = call(
+        _, _, gate, up, gatep, upp, inv = call(
             forward_kernel,
-            [((HALF, hidden), F32)] * 4 + [((1, PADDED), F32)],
-            8,
-            [pltpu.VMEM((HALF, D), BF16), pltpu.VMEM((PADDED, LANES), F32)],
-        )(*a_refs, wg, wu, wgp, wup)
+            [placed[0], placed[2]] + [((HALF, hidden), F32)] * 4 + [((1, PADDED), F32)],
+            5,
+            [pltpu.VMEM((PADDED, LANES), F32)],
+            aliases={0: 0, 1: 1},
+        )(xs, sq, lo, hi, wg, wu, wgp, wup)
     with jax.named_scope("back"):
         top, *low = call(
             back_kernel,

time: 185 us -> 181 us (0.978)
  waiting for transfers between devices: 82.2 us -> 65 us
  starting transfers between devices: 47.8 us -> 59.9 us
    ppermute x26, waiting for transfers between devices: 73.3 us -> 61.6 us  [shift(): return lax.ppermute(value, axis, [(i, (i + by) % n) for i in range(n)])]
    ppermute x26, starting transfers between devices: 32.1 us -> 40.9 us  [shift(): return lax.ppermute(value, axis, [(i, (i + by) % n) for i in range(n)])]
    all_to_all x1, waiting for transfers between devices: 3.57 us -> 0.01 us  [shards(): top = lax.all_to_all(top, 'tensor_1', 0, 0, tiled=True)]
    all_to_all x1, starting transfers between devices: 3.46 us -> 6.37 us  [shards(): low = lax.all_to_all(low, 'tensor_1', 0, 0, tiled=True)]
    all_to_all x1, waiting for transfers between devices: 5.33 us -> 3.44 us  [shards(): low = lax.all_to_all(low, 'tensor_1', 0, 0, tiled=True)]
    unnamed x24 -> x20, local copies, waits for them, and re-layouts: 4.34 us -> 3.63 us
    pallas_call x9 -> x11, Pallas kernels: 20.9 us -> 20.9 us  [run(): pl.pallas_call(kernel, in_specs=[here] * len(arrays), out_specs=[here] *...]
  transfers between devices with their start and end apart: 29 -> 29, of which waited for: 17 -> 11; matrix products, arithmetic and copies ran while one was open for 0% -> 0% of each run, Pallas kernels for 7% -> 7%
where the time goes in v4:
time: 181 us; the launch traced here: 180 us
  waiting for transfers between devices  65 us (36%)
  starting transfers between devices  59.9 us (33%)
  blocking collectives  29.9 us (17%)
  Pallas kernels  20.9 us (12%)
  local copies, waits for them, and re-layouts  3.73 us (2%)
    ppermute x26, waiting for transfers between devices, shift(): return lax.ppermute(value, axis, [(i, (i + by) % n) for i in range(n)])  61.6 us
    ppermute x26, starting transfers between devices, shift(): return lax.ppermute(value, axis, [(i, (i + by) % n) for i in range(n)])  40.9 us
    pallas_call x11, Pallas kernels, run(): pl.pallas_call(kernel, in_specs=[here] * len(arrays), out_specs=[here] *...  20.9 us
    all_to_all x1, blocking collectives, shards(): got = lax.all_to_all(pieces, LINE, 0, 0, tiled=True)  15.7 us
    all_to_all x1, blocking collectives, shards(): lax.all_to_all(routed.reshape(2 * GROUPS, CAP, LANES), LINE, 0, 0, tiled=...  14.1 us
    all_to_all x1, starting transfers between devices, shards(): line_a = lax.all_to_all(copies, 'tensor_1', 0, 0, tiled=True)  7.41 us
    all_to_all x1, starting transfers between devices, shards(): low = lax.all_to_all(low, 'tensor_1', 0, 0, tiled=True)  6.37 us
    all_to_all x1, starting transfers between devices, shards(): top = lax.all_to_all(top, 'tensor_1', 0, 0, tiled=True)  5.19 us
  transfers between devices with their start and end apart: 29, of which 11 were waited for; matrix products, arithmetic and copies ran while one was open for 0% of the time, Pallas kernels for 7%

profile of v4, /device:TPU:1, one launch (start us, length us, event | category | flops | bytes accessed | tf_op | source)
XLA Modules:
  0.0 179.6 jit_solution(17109364935895575830)
XLA Ops:
  2.2 14.1 %all_to_all.25 = bf16[8,160,128]{2,1,0:T(8,128)(2,1)S(1)} all-to-all(bf16[8,160,128]{2,1,0:T(8,128)(2,1)} %bitcast.30), channel_id=1, replica_groups=mesh['expert'=4,'tensor_0'=4,'tensor_1'=8,'kv'=2] {'expert','kv'}, dimensions={0} | all-to-all | bytes 655360 | tf_op jit(solution)/shard_map/dispatch/all_to_all | solution.py:336
  18.3 7.4 %all-to-all-start.1 = ((bf16[8,480,128]{2,1,0:T(8,128)(2,1)}), bf16[8,480,128]{2,1,0:T(8,128)(2,1)S(1)}, u32[]{:S(2)}, u32[]{:S(2)}) async-start(bf16[8,480,128]{2,1,0:T(8,128)(2,1)} %get-tuple-element.50), calls=%async_computation.1 | async-start | bytes 1966080 | tf_op jit(solution)/shard_map/gather/all_to_all | solution.py:345
  25.7 2.9 %collective-permute-start.1 = (bf16[496,128]{1,0:T(8,128)(2,1)S(1)}, bf16[496,128]{1,0:T(8,128)(2,1)S(1)}, u32[]{:S(2)}, u32[]{:S(2)}) collective-permute-start(bf16[496,128]{1,0:T(8,128)(2,1)S(1)} %get-tuple-element.49), channel_id=1, source_target_pairs={{0,32},{16,48},{32,0},{48,16},{1,33},{17,49},{33,1},{49,17},{2,34}... | collective-permute-start | bytes 380936 | tf_op jit(solution)/shard_map/gather/ppermute | solution.py:310
  31.4 3.6 %collective-permute-done.2 = bf16[496,128]{1,0:T(8,128)(2,1)S(1)} collective-permute-done((bf16[496,128]{1,0:T(8,128)(2,1)S(1)}, bf16[496,128]{1,0:T(8,128)(2,1)S(1)}, u32[]{:S(2)}, u32[]{:S(2)}) %collective-permute-start.2) | collective-permute-done | bytes 127008 | tf_op jit(solution)/shard_map/gather/ppermute | solution.py:310
  38.0 22.7 %collective-permute-done.3.b7 = bf16[4,496,128]{2,1,0:T(8,128)(2,1)S(1)} collective-permute-done((bf16[4,496,128]{2,1,0:T(8,128)(2,1)S(1)}, bf16[4,496,128]{2,1,0:T(8,128)(2,1)S(1)}, u32[]{:S(2)}, u32[]{:S(2)}) %collective-permute-start.3) | collective-permute-done | bytes 507936 | tf_op jit(solution)/shard_map/gather/ppermute | solution.py:310
  61.6 2.7 %collective-permute-start.7 = (bf16[4,496,128]{2,1,0:T(8,128)(2,1)}, bf16[4,496,128]{2,1,0:T(8,128)(2,1)S(1)}, u32[]{:S(2)}, u32[]{:S(2)}) collective-permute-start(bf16[4,496,128]{2,1,0:T(8,128)(2,1)} %collective-permute-done.4.b1), channel_id=1, source_target_pairs={{0,14},{2,0},{4,2},{6,4},{8,6},{10,8},{12,10},{14,12},{1,15},{3,1}... | collective-permute-start | bytes 1523720 | tf_op jit(solution)/shard_map/gather/ppermute | solution.py:310
  69.4 8.9 %collective-permute-done.8.near3_ref = bf16[4,480,128]{2,1,0:T(8,128)(2,1)S(1)} collective-permute-done((bf16[4,480,128]{2,1,0:T(8,128)(2,1)S(1)}, bf16[4,480,128]{2,1,0:T(8,128)(2,1)S(1)}, u32[]{:S(2)}, u32[]{:S(2)}) %collective-permute-start.8) | collective-permute-done | bytes 491552 | tf_op jit(solution)/shard_map/gather/ppermute | solution.py:310
  78.5 2.7 %collective-permute-start.11 = (bf16[4,496,128]{2,1,0:T(8,128)(2,1)S(1)}, bf16[4,496,128]{2,1,0:T(8,128)(2,1)S(1)}, u32[]{:S(2)}, u32[]{:S(2)}) collective-permute-start(bf16[4,496,128]{2,1,0:T(8,128)(2,1)S(1)} %collective-permute-done.7.b2), channel_id=1, source_target_pairs={{0,14},{2,0},{4,2},{6,4},{8,6},{10,8},{12,10},{14,12},{1,15},{3,1}... | collective-permute-start | bytes 1523720 | tf_op jit(solution)/shard_map/gather/ppermute | solution.py:310
  87.1 4.2 %collective-permute-done.12.far3_ref = bf16[4,480,128]{2,1,0:T(8,128)(2,1)S(1)} collective-permute-done((bf16[4,480,128]{2,1,0:T(8,128)(2,1)S(1)}, bf16[4,480,128]{2,1,0:T(8,128)(2,1)S(1)}, u32[]{:S(2)}, u32[]{:S(2)}) %collective-permute-start.12) | collective-permute-done | bytes 491552 | tf_op jit(solution)/shard_map/gather/ppermute | solution.py:310
  91.4 2.7 %collective-permute-start.15 = (bf16[4,480,128]{2,1,0:T(8,128)(2,1)S(1)}, bf16[4,480,128]{2,1,0:T(8,128)(2,1)S(1)}, u32[]{:S(2)}, u32[]{:S(2)}) collective-permute-start(bf16[4,480,128]{2,1,0:T(8,128)(2,1)S(1)} %collective-permute-done.13.far1_ref), channel_id=1, source_target_pairs={{0,48},{16,0},{32,16},{48,32},{1,49},{17,1},{33,17},{49,33},{2,50}... | collective-permute-start | bytes 1474568 | tf_op jit(solution)/shard_map/gather/ppermute | solution.py:310
  94.3 2.7 %collective-permute-start.18 = (bf16[2,496,128]{2,1,0:T(8,128)(2,1)S(1)}, bf16[2,496,128]{2,1,0:T(8,128)(2,1)S(1)}, u32[]{:S(2)}, u32[]{:S(2)}) collective-permute-start(bf16[2,496,128]{2,1,0:T(8,128)(2,1)S(1)} %slice.17), channel_id=1, source_target_pairs={{0,14},{2,0},{4,2},{6,4},{8,6},{10,8},{12,10},{14,12},{1,15},{3,1}... | collective-permute-start | bytes 761864 | tf_op jit(solution)/shard_map/gather/ppermute | solution.py:310
  97.7 3.3 %collective-permute-done.14.refs_2_.lo_ref = bf16[4,480,128]{2,1,0:T(8,128)(2,1)S(1)} collective-permute-done((bf16[4,480,128]{2,1,0:T(8,128)(2,1)S(1)}, bf16[4,480,128]{2,1,0:T(8,128)(2,1)S(1)}, u32[]{:S(2)}, u32[]{:S(2)}) %collective-permute-start.14) | collective-permute-done | bytes 491552 | tf_op jit(solution)/shard_map/gather/ppermute | solution.py:310
  105.5 4.7 %forward.1 = (bf16[320,4096]{1,0:T(8,128)(2,1)S(1)}, f32[320,128]{1,0:T(8,128)S(1)}, f32[320,224]{1,0:T(8,128)S(1)}, f32[320,224]{1,0:T(8,128)S(1)}, f32[320,224...) custom-call(bf16[320,4096]{1,0:T(8,128)(2,1)S(1)} %get-tuple-element, ...), custom_call_target="tpu_custom_call", output_to_operand_aliasing={{0}: (0, {}), {1}: (1, {})} | custom-call | flops 5000000000 | tf_op jit(solution)/shard_map/forward/pallas_call | solution.py:38
  110.2 5.5 %back.1 = (bf16[8,4,112,128]{3,2,1,0:T(8,128)(2,1)}, bf16[8,224,128]{2,1,0:T(8,128)(2,1)S(1)}, bf16[8,224,128]{2,1,0:T(8,128)(2,1)S(1)}, bf16[8,224,128]{2,1,0:T(8,128)(2,1)S(1)}, bf16[8,224,128]{2,1,0:T(8,128)(2,1)S(1)}) custom-call(f32[320,224]{1,0:T(8,128)S(1)} %get-tuple-element.70.refs_0_, f32[320,224]{1,0:T(8,128)S(1)} %get-tuple-element.71.refs_1_, ...), custom_call_target="tpu_custom_call" | custom-call | flops 8000000000 | tf_op jit(solution)/shard_map/back/pallas_call | solution.py:38
  116.5 5.2 %all-to-all-start.2 = ((bf16[8,4,112,128]{3,2,1,0:T(8,128)(2,1)}), bf16[8,4,112,128]{3,2,1,0:T(8,128)(2,1)S(1)}, u32[]{:S(2)}, u32[]{:S(2)}) async-start(bf16[8,4,112,128]{3,2,1,0:T(8,128)(2,1)} %get-tuple-element.79), calls=%async_computation.2 | async-start | bytes 1835008 | tf_op jit(solution)/shard_map/scatter/all_to_all | solution.py:400
  121.7 2.9 %collective-permute-start.20 = (bf16[8,224,128]{2,1,0:T(8,128)(2,1)S(1)}, bf16[8,224,128]{2,1,0:T(8,128)(2,1)S(1)}, u32[]{:S(2)}, u32[]{:S(2)}) collective-permute-start(bf16[8,224,128]{2,1,0:T(8,128)(2,1)S(1)} %get-tuple-element.81), channel_id=1, source_target_pairs={{0,32},{16,48},{32,0},{48,16},{1,33},{17,49},{33,1},{49,17},{2,34}... | collective-permute-start | bytes 1376264 | tf_op jit(solution)/shard_map/scatter/ppermute | solution.py:310
  125.0 2.3 %collective-permute-start.22 = (bf16[8,224,128]{2,1,0:T(8,128)(2,1)S(1)}, bf16[8,224,128]{2,1,0:T(8,128)(2,1)S(1)}, u32[]{:S(2)}, u32[]{:S(2)}) collective-permute-start(bf16[8,224,128]{2,1,0:T(8,128)(2,1)S(1)} %get-tuple-element.83), channel_id=1, source_target_pairs={{0,48},{16,0},{32,16},{48,32},{1,49},{17,1},{33,17},{49,33},{2,50}... | collective-permute-start | bytes 1376264 | tf_op jit(solution)/shard_map/scatter/ppermute | solution.py:310
  127.3 3.3 %collective-permute-done.20.refs_1_ = bf16[8,224,128]{2,1,0:T(8,128)(2,1)S(1)} collective-permute-done((bf16[8,224,128]{2,1,0:T(8,128)(2,1)S(1)}, bf16[8,224,128]{2,1,0:T(8,128)(2,1)S(1)}, u32[]{:S(2)}, u32[]{:S(2)}) %collective-permute-start.20) | collective-permute-done | bytes 458784 | tf_op jit(solution)/shard_map/scatter/ppermute | solution.py:310
  130.6 12.6 %collective-permute-done.21.refs_2_ = bf16[8,224,128]{2,1,0:T(8,128)(2,1)S(1)} collective-permute-done((bf16[8,224,128]{2,1,0:T(8,128)(2,1)S(1)}, bf16[8,224,128]{2,1,0:T(8,128)(2,1)S(1)}, u32[]{:S(2)}, u32[]{:S(2)}) %collective-permute-start.21) | collective-permute-done | bytes 458784 | tf_op jit(solution)/shard_map/scatter/ppermute | solution.py:310
  145.2 6.4 %all-to-all-start.3 = ((bf16[8,224,128]{2,1,0:T(8,128)(2,1)}), bf16[8,224,128]{2,1,0:T(8,128)(2,1)S(1)}, u32[]{:S(2)}, u32[]{:S(2)}) async-start(bf16[8,224,128]{2,1,0:T(8,128)(2,1)} %scatter.2), calls=%async_computation.3 | async-start | bytes 917504 | tf_op jit(solution)/shard_map/scatter/all_to_all | solution.py:405
  151.7 3.5 %collective-permute-start.23 = (bf16[112,128]{1,0:T(8,128)(2,1)S(1)}, bf16[112,128]{1,0:T(8,128)(2,1)S(1)}, u32[]{:S(2)}, u32[]{:S(2)}) collective-permute-start(bf16[112,128]{1,0:T(8,128)(2,1)S(1)} %get-tuple-element.86), channel_id=1, source_target_pairs={{0,32},{16,48},{32,0},{48,16},{1,33},{17,49},{33,1},{49,17},{2,34}... | collective-permute-start | bytes 86024 | tf_op jit(solution)/shard_map/scatter/ppermute | solution.py:310
  155.6 2.4 %collective-permute-start.25 = (bf16[112,128]{1,0:T(8,128)(2,1)S(1)}, bf16[112,128]{1,0:T(8,128)(2,1)S(1)}, u32[]{:S(2)}, u32[]{:S(2)}) collective-permute-start(bf16[112,128]{1,0:T(8,128)(2,1)S(1)} %get-tuple-element.88), channel_id=1, source_target_pairs={{0,48},{16,0},{32,16},{48,32},{1,49},{17,1},{33,17},{49,33},{2,50}... | collective-permute-start | bytes 86024 | tf_op jit(solution)/shard_map/scatter/ppermute | solution.py:310
  159.2 3.4 %all-to-all-done.3.refs_4_ = bf16[8,224,128]{2,1,0:T(8,128)(2,1)S(1)} async-done(((bf16[8,224,128]{2,1,0:T(8,128)(2,1)}), bf16[8,224,128]{2,1,0:T(8,128)(2,1)S(1)}, u32[]{:S(2)}, u32[]{:S(2)}) %all-to-all-start.3) | async-done | bytes 458784 | tf_op jit(solution)/shard_map/scatter/all_to_all | solution.py:405
  162.8 15.7 %all_to_all.26.got_ref = bf16[8,96,128]{2,1,0:T(8,128)(2,1)S(1)} all-to-all(bf16[8,96,128]{2,1,0:T(8,128)(2,1)S(1)} %combine.2), channel_id=1, replica_groups=mesh['expert'=4,'tensor_0'=4,'tensor_1'=8,'kv'=2] {'expert','kv'}, dimensions={0} | all-to-all | bytes 393216 | tf_op jit(solution)/shard_map/combine/all_to_all | solution.py:410
  (71 shorter events, 33.4 us)
Async XLA Ops:
  16.3 45.2 %collective-permute-start.5 = (bf16[224,4096]{1,0:T(8,128)(2,1)S(1)}, bf16[224,4096]{1,0:T(8,128)(2,1)}, u32[]{:S(2)}, u32[]{:S(2)}) collective-permute-start(bf16[224,4096]{1,0:T(8,128)(2,1)S(1)} %bitcast.18), channel_id=1, source_target_pairs={{0,1},{1,0},{2,3},{3,2},{4,5},{5,4},{6,7},{7,6},{8,9},{9,8},{10,11... | collective-permute-start | bytes 5505032 | tf_op jit(solution)/shard_map/weights/ppermute | solution.py:310
  18.3 43.2 %all-to-all-start.1 = ((bf16[8,480,128]{2,1,0:T(8,128)(2,1)}), bf16[8,480,128]{2,1,0:T(8,128)(2,1)S(1)}, u32[]{:S(2)}, u32[]{:S(2)}) async-start(bf16[8,480,128]{2,1,0:T(8,128)(2,1)} %get-tuple-element.50), calls=%async_computation.1 | async-start | bytes 1966080 | tf_op jit(solution)/shard_map/gather/all_to_all | solution.py:345
  28.6 6.4 %collective-permute-start.2 = (bf16[496,128]{1,0:T(8,128)(2,1)S(1)}, bf16[496,128]{1,0:T(8,128)(2,1)S(1)}, u32[]{:S(2)}, u32[]{:S(2)}) collective-permute-start(bf16[496,128]{1,0:T(8,128)(2,1)S(1)} %get-tuple-element.49), channel_id=1, source_target_pairs={{0,16},{16,32},{32,48},{48,0},{1,17},{17,33},{33,49},{49,1},{2,18}... | collective-permute-start | bytes 380936 | tf_op jit(solution)/shard_map/gather/ppermute | solution.py:310
  35.1 25.7 %collective-permute-start.3 = (bf16[4,496,128]{2,1,0:T(8,128)(2,1)S(1)}, bf16[4,496,128]{2,1,0:T(8,128)(2,1)S(1)}, u32[]{:S(2)}, u32[]{:S(2)}) collective-permute-start(bf16[4,496,128]{2,1,0:T(8,128)(2,1)S(1)} %pad_maximum_fusion.b0), channel_id=1, source_target_pairs={{0,2},{2,4},{4,6},{6,8},{8,10},{10,12},{12,14},{14,0},{1,3},{3,5},... | collective-permute-start | bytes 1523720 | tf_op jit(solution)/shard_map/gather/ppermute | solution.py:310
  36.7 24.8 %collective-permute-start.4 = (bf16[4,496,128]{2,1,0:T(8,128)(2,1)S(1)}, bf16[4,496,128]{2,1,0:T(8,128)(2,1)}, u32[]{:S(2)}, u32[]{:S(2)}) collective-permute-start(bf16[4,496,128]{2,1,0:T(8,128)(2,1)S(1)} %pad_maximum_fusion.b0), channel_id=1, source_target_pairs={{0,14},{2,0},{4,2},{6,4},{8,6},{10,8},{12,10},{14,12},{1,15},{3,1}... | collective-permute-start | bytes 1523720 | tf_op jit(solution)/shard_map/gather/ppermute | solution.py:310
  61.5 16.9 %collective-permute-start.6 = (bf16[4,496,128]{2,1,0:T(8,128)(2,1)}, bf16[4,496,128]{2,1,0:T(8,128)(2,1)S(1)}, u32[]{:S(2)}, u32[]{:S(2)}) collective-permute-start(bf16[4,496,128]{2,1,0:T(8,128)(2,1)} %copy-done.3), channel_id=1, source_target_pairs={{0,2},{2,4},{4,6},{6,8},{8,10},{10,12},{12,14},{14,0},{1,3},{3,5},... | collective-permute-start | bytes 1523720 | tf_op jit(solution)/shard_map/gather/ppermute | solution.py:310
  61.6 16.8 %collective-permute-start.7 = (bf16[4,496,128]{2,1,0:T(8,128)(2,1)}, bf16[4,496,128]{2,1,0:T(8,128)(2,1)S(1)}, u32[]{:S(2)}, u32[]{:S(2)}) collective-permute-start(bf16[4,496,128]{2,1,0:T(8,128)(2,1)} %collective-permute-done.4.b1), channel_id=1, source_target_pairs={{0,14},{2,0},{4,2},{6,4},{8,6},{10,8},{12,10},{14,12},{1,15},{3,1}... | collective-permute-start | bytes 1523720 | tf_op jit(solution)/shard_map/gather/ppermute | solution.py:310
  64.3 41.2 %collective-permute-start.16 = (bf16[224,4096]{1,0:T(8,128)(2,1)}, bf16[224,4096]{1,0:T(8,128)(2,1)S(1)}, u32[]{:S(2)}, u32[]{:S(2)}) collective-permute-start(bf16[224,4096]{1,0:T(8,128)(2,1)} %bitcast.21), channel_id=1, source_target_pairs={{0,1},{1,0},{2,3},{3,2},{4,5},{5,4},{6,7},{7,6},{8,9},{9,8},{10,11... | collective-permute-start | bytes 5505032 | tf_op jit(solution)/shard_map/weights/ppermute | solution.py:310
  66.5 11.9 %collective-permute-start.8 = (bf16[4,480,128]{2,1,0:T(8,128)(2,1)S(1)}, bf16[4,480,128]{2,1,0:T(8,128)(2,1)S(1)}, u32[]{:S(2)}, u32[]{:S(2)}) collective-permute-start(bf16[4,480,128]{2,1,0:T(8,128)(2,1)S(1)} %get-tuple-element.92), channel_id=1, source_target_pairs={{0,16},{16,32},{32,48},{48,0},{1,17},{17,33},{33,49},{49,1},{2,18}... | collective-permute-start | bytes 1474568 | tf_op jit(solution)/shard_map/gather/ppermute | solution.py:310
  67.9 10.5 %collective-permute-start.9 = (bf16[4,480,128]{2,1,0:T(8,128)(2,1)S(1)}, bf16[4,480,128]{2,1,0:T(8,128)(2,1)S(1)}, u32[]{:S(2)}, u32[]{:S(2)}) collective-permute-start(bf16[4,480,128]{2,1,0:T(8,128)(2,1)S(1)} %get-tuple-element.92), channel_id=1, source_target_pairs={{0,48},{16,0},{32,16},{48,32},{1,49},{17,1},{33,17},{49,33},{2,50}... | collective-permute-start | bytes 1474568 | tf_op jit(solution)/shard_map/gather/ppermute | solution.py:310
  78.4 13.0 %collective-permute-start.10 = (bf16[4,496,128]{2,1,0:T(8,128)(2,1)S(1)}, bf16[4,496,128]{2,1,0:T(8,128)(2,1)S(1)}, u32[]{:S(2)}, u32[]{:S(2)}) collective-permute-start(bf16[4,496,128]{2,1,0:T(8,128)(2,1)S(1)} %collective-permute-done.6.b6), channel_id=1, source_target_pairs={{0,2},{2,4},{4,6},{6,8},{8,10},{10,12},{12,14},{14,0},{1,3},{3,5},... | collective-permute-start | bytes 1523720 | tf_op jit(solution)/shard_map/gather/ppermute | solution.py:310
  78.5 12.9 %collective-permute-start.11 = (bf16[4,496,128]{2,1,0:T(8,128)(2,1)S(1)}, bf16[4,496,128]{2,1,0:T(8,128)(2,1)S(1)}, u32[]{:S(2)}, u32[]{:S(2)}) collective-permute-start(bf16[4,496,128]{2,1,0:T(8,128)(2,1)S(1)} %collective-permute-done.7.b2), channel_id=1, source_target_pairs={{0,14},{2,0},{4,2},{6,4},{8,6},{10,8},{12,10},{14,12},{1,15},{3,1}... | collective-permute-start | bytes 1523720 | tf_op jit(solution)/shard_map/gather/ppermute | solution.py:310
  81.1 10.2 %collective-permute-start.12 = (bf16[4,480,128]{2,1,0:T(8,128)(2,1)S(1)}, bf16[4,480,128]{2,1,0:T(8,128)(2,1)S(1)}, u32[]{:S(2)}, u32[]{:S(2)}) collective-permute-start(bf16[4,480,128]{2,1,0:T(8,128)(2,1)S(1)} %get-tuple-element.91), channel_id=1, source_target_pairs={{0,16},{16,32},{32,48},{48,0},{1,17},{17,33},{33,49},{49,1},{2,18}... | collective-permute-start | bytes 1474568 | tf_op jit(solution)/shard_map/gather/ppermute | solution.py:310
  82.0 9.3 %collective-permute-start.13 = (bf16[4,480,128]{2,1,0:T(8,128)(2,1)S(1)}, bf16[4,480,128]{2,1,0:T(8,128)(2,1)S(1)}, u32[]{:S(2)}, u32[]{:S(2)}) collective-permute-start(bf16[4,480,128]{2,1,0:T(8,128)(2,1)S(1)} %get-tuple-element.91), channel_id=1, source_target_pairs={{0,48},{16,0},{32,16},{48,32},{1,49},{17,1},{33,17},{49,33},{2,50}... | collective-permute-start | bytes 1474568 | tf_op jit(solution)/shard_map/gather/ppermute | solution.py:310
  91.4 9.7 %collective-permute-start.14 = (bf16[4,480,128]{2,1,0:T(8,128)(2,1)S(1)}, bf16[4,480,128]{2,1,0:T(8,128)(2,1)S(1)}, u32[]{:S(2)}, u32[]{:S(2)}) collective-permute-start(bf16[4,480,128]{2,1,0:T(8,128)(2,1)S(1)} %collective-permute-done.8.near3_ref), channel_id=1, source_target_pairs={{0,16},{16,32},{32,48},{48,0},{1,17},{17,33},{33,49},{49,1},{2,18}... | collective-permute-start | bytes 1474568 | tf_op jit(solution)/shard_map/gather/ppermute | solution.py:310
  91.4 9.7 %collective-permute-start.15 = (bf16[4,480,128]{2,1,0:T(8,128)(2,1)S(1)}, bf16[4,480,128]{2,1,0:T(8,128)(2,1)S(1)}, u32[]{:S(2)}, u32[]{:S(2)}) collective-permute-start(bf16[4,480,128]{2,1,0:T(8,128)(2,1)S(1)} %collective-permute-done.13.far1_ref), channel_id=1, source_target_pairs={{0,48},{16,0},{32,16},{48,32},{1,49},{17,1},{33,17},{49,33},{2,50}... | collective-permute-start | bytes 1474568 | tf_op jit(solution)/shard_map/gather/ppermute | solution.py:310
  94.2 6.9 %collective-permute-start.17 = (bf16[2,496,128]{2,1,0:T(8,128)(2,1)S(1)}, bf16[2,496,128]{2,1,0:T(8,128)(2,1)S(1)}, u32[]{:S(2)}, u32[]{:S(2)}) collective-permute-start(bf16[2,496,128]{2,1,0:T(8,128)(2,1)S(1)} %slice.16), channel_id=1, source_target_pairs={{0,2},{2,4},{4,6},{6,8},{8,10},{10,12},{12,14},{14,0},{1,3},{3,5},... | collective-permute-start | bytes 761864 | tf_op jit(solution)/shard_map/gather/ppermute | solution.py:310
  94.3 6.8 %collective-permute-start.18 = (bf16[2,496,128]{2,1,0:T(8,128)(2,1)S(1)}, bf16[2,496,128]{2,1,0:T(8,128)(2,1)S(1)}, u32[]{:S(2)}, u32[]{:S(2)}) collective-permute-start(bf16[2,496,128]{2,1,0:T(8,128)(2,1)S(1)} %slice.17), channel_id=1, source_target_pairs={{0,14},{2,0},{4,2},{6,4},{8,6},{10,8},{12,10},{14,12},{1,15},{3,1}... | collective-permute-start | bytes 761864 | tf_op jit(solution)/shard_map/gather/ppermute | solution.py:310
  103.1 7.1 %collective-permute-start.19 = (bf16[320,224]{1,0:T(8,128)(2,1)S(1)}, bf16[320,224]{1,0:T(8,128)(2,1)S(1)}, u32[]{:S(2)}, u32[]{:S(2)}) collective-permute-start(bf16[320,224]{1,0:T(8,128)(2,1)S(1)} %get-tuple-element.78), channel_id=1, source_target_pairs={{0,1},{1,0},{2,3},{3,2},{4,5},{5,4},{6,7},{7,6},{8,9},{9,8},{10,11... | collective-permute-start | bytes 430088 | tf_op jit(solution)/shard_map/act/ppermute | solution.py:310
  116.5 28.7 %all-to-all-start.2 = ((bf16[8,4,112,128]{3,2,1,0:T(8,128)(2,1)}), bf16[8,4,112,128]{3,2,1,0:T(8,128)(2,1)S(1)}, u32[]{:S(2)}, u32[]{:S(2)}) async-start(bf16[8,4,112,128]{3,2,1,0:T(8,128)(2,1)} %get-tuple-element.79), calls=%async_computation.2 | async-start | bytes 1835008 | tf_op jit(solution)/shard_map/scatter/all_to_all | solution.py:400
  121.7 8.9 %collective-permute-start.20 = (bf16[8,224,128]{2,1,0:T(8,128)(2,1)S(1)}, bf16[8,224,128]{2,1,0:T(8,128)(2,1)S(1)}, u32[]{:S(2)}, u32[]{:S(2)}) collective-permute-start(bf16[8,224,128]{2,1,0:T(8,128)(2,1)S(1)} %get-tuple-element.81), channel_id=1, source_target_pairs={{0,32},{16,48},{32,0},{48,16},{1,33},{17,49},{33,1},{49,17},{2,34}... | collective-permute-start | bytes 1376264 | tf_op jit(solution)/shard_map/scatter/ppermute | solution.py:310
  124.6 18.6 %collective-permute-start.21 = (bf16[8,224,128]{2,1,0:T(8,128)(2,1)S(1)}, bf16[8,224,128]{2,1,0:T(8,128)(2,1)S(1)}, u32[]{:S(2)}, u32[]{:S(2)}) collective-permute-start(bf16[8,224,128]{2,1,0:T(8,128)(2,1)S(1)} %get-tuple-element.82), channel_id=1, source_target_pairs={{0,16},{16,32},{32,48},{48,0},{1,17},{17,33},{33,49},{49,1},{2,18}... | collective-permute-start | bytes 1376264 | tf_op jit(solution)/shard_map/scatter/ppermute | solution.py:310
  125.0 18.2 %collective-permute-start.22 = (bf16[8,224,128]{2,1,0:T(8,128)(2,1)S(1)}, bf16[8,224,128]{2,1,0:T(8,128)(2,1)S(1)}, u32[]{:S(2)}, u32[]{:S(2)}) collective-permute-start(bf16[8,224,128]{2,1,0:T(8,128)(2,1)S(1)} %get-tuple-element.83), channel_id=1, source_target_pairs={{0,48},{16,0},{32,16},{48,32},{1,49},{17,1},{33,17},{49,33},{2,50}... | collective-permute-start | bytes 1376264 | tf_op jit(solution)/shard_map/scatter/ppermute | solution.py:310
  145.2 17.4 %all-to-all-start.3 = ((bf16[8,224,128]{2,1,0:T(8,128)(2,1)}), bf16[8,224,128]{2,1,0:T(8,128)(2,1)S(1)}, u32[]{:S(2)}, u32[]{:S(2)}) async-start(bf16[8,224,128]{2,1,0:T(8,128)(2,1)} %scatter.2), calls=%async_computation.3 | async-start | bytes 917504 | tf_op jit(solution)/shard_map/scatter/all_to_all | solution.py:405
  (15 other events, 101.4 us)

commit v5 on v4

--- a/solution.py
+++ b/solution.py
@@ -18,7 +18,7 @@
 GAIN_ROWS = 16
 MINE = CAP // 2
 XROWS = HALF + GAIN_ROWS
-SPLIT = 144
+SPLIT = 192
 PADDED = 384
 ZFIRST = 112
 YFIRST = HALF - ZFIRST
@@ -91,8 +91,7 @@
             out_ref[e, k, pl.ds(MINE, MINE), :] = jnp.where(low, second, gain).astype(BF16)
 
 
-def assemble_kernel(got_ref, copies_ref, b_ref):
-    a_ref = copies_ref.at[0]
+def assemble_kernel(got_ref, a_ref, b_ref):
     grads = []
     for g in range(GROUPS):
         low, high = got_ref[g, 0].astype(F32), got_ref[g, 1].astype(F32)
@@ -101,12 +100,9 @@
         a_ref[pl.ds(g * MINE, MINE), :] = x[:MINE]
         if g == 0:
             a_ref[pl.ds(HALF, GAIN_ROWS), :] = x[MINE : MINE + GAIN_ROWS]
-    a_ref[pl.ds(XROWS, SPLIT), :] = grads[0][:SPLIT]
-    b_ref[pl.ds(0, CAP - SPLIT), :] = grads[0][SPLIT:]
-    for g in range(1, GROUPS):
-        b_ref[pl.ds(g * CAP - SPLIT, CAP), :] = grads[g]
-    for z in range(1, NZ):
-        copies_ref[z] = copies_ref[0]
+    grads = jnp.concatenate(grads, axis=0)
+    a_ref[pl.ds(XROWS, SPLIT), :] = grads[:SPLIT]
+    b_ref[...] = grads[SPLIT:]
 
 
 def block(y, z):
@@ -334,15 +330,16 @@
             ids, probs, x_t, grad_t, gain_row
         )
         got = lax.all_to_all(routed.reshape(2 * GROUPS, CAP, LANES), LINE, 0, 0, tiled=True)
-        got, own_wg = lax.optimization_barrier((got, wg))
-        copies, piece_b = call(
-            assemble_kernel, [((NZ, XROWS + SPLIT, LANES), BF16), ((ROWS - SPLIT, LANES), BF16)], 2
+        piece_a, piece_b = call(
+            assemble_kernel, [((XROWS + SPLIT, LANES), BF16), ((ROWS - SPLIT, LANES), BF16)], 2
         )(got.reshape(GROUPS, 2, CAP, LANES))
+
+        piece_a, own_wg = lax.optimization_barrier((piece_a, wg))
 
     with jax.named_scope("weights"):
         wgp = shift(own_wg, "kv", 1)
     with jax.named_scope("gather"):
-        line_a = lax.all_to_all(copies, "tensor_1", 0, 0, tiled=True)
+        line_a = lax.all_gather(piece_a, "tensor_1", axis=0)
         line_b = jnp.stack([piece_b] + [shift(piece_b, "tensor_0", -a) for a in (1, 2, 3)])
 
         near, far, state = [], [], None
@@ -351,11 +348,11 @@
         def meet(step, right, left, got):
             nonlocal line_a, wgp, state
             if step == 2:
-                right, left, line_a, wgp = lax.optimization_barrier((right, left, line_a, wgp))
+                right, left, line_a = lax.optimization_barrier((right, left, line_a))
                 near[:] = [shift(line_a[: NZ // 2], "tensor_0", by) for by in (1, -1)]
                 far[:] = [shift(line_a[NZ // 2 :], "tensor_0", by) for by in (1, -1)]
             if step == 3:
-                right, left, *near[:] = lax.optimization_barrier((right, left, *near))
+                right, left, wgp, *near[:] = lax.optimization_barrier((right, left, wgp, *near))
                 early = [got[b] for b in (0, 1, 2, 6, 7)]
                 state = [*call(place_first_kernel, placed, 5)(line_a, near[1], near[0], *early)]
             if step == 4:

time: 181 us -> 194 us (1.072)
  between operations: 0.17 us -> 13.5 us
  waiting for transfers between devices: 65 us -> 76.7 us
  starting transfers between devices: 59.9 us -> 49.5 us
    all_to_all x1 -> x0, starting transfers between devices: 7.41 us -> none  [shards(): line_a = lax.all_to_all(copies, 'tensor_1', 0, 0, tiled=True)]
    all_gather x0 -> x1, waiting for transfers between devices: none -> 6.11 us  [shards(): line_a = lax.all_gather(piece_a, 'tensor_1', axis=0)]
    ppermute x26, waiting for transfers between devices: 61.6 us -> 65.5 us  [shift(): return lax.ppermute(value, axis, [(i, (i + by) % n) for i in range(n)])]
    ppermute x26, starting transfers between devices: 40.9 us -> 37.8 us  [shift(): return lax.ppermute(value, axis, [(i, (i + by) % n) for i in range(n)])]
  transfers between devices with their start and end apart: 29 -> 29, of which waited for: 11 -> 14; matrix products, arithmetic and copies ran while one was open for 0% -> 1% of each run, Pallas kernels for 7% -> 5%
where the time goes in v5:
time: 194 us; the launch traced here: 193 us
  waiting for transfers between devices  76.7 us (40%)
  starting transfers between devices  49.5 us (26%)
  blocking collectives  30.1 us (16%)
  Pallas kernels  19.3 us (10%)
  between operations  13.5 us (7%)
  local copies, waits for them, and re-layouts  3.76 us (2%)
    ppermute x26, waiting for transfers between devices, shift(): return lax.ppermute(value, axis, [(i, (i + by) % n) for i in range(n)])  65.5 us
    ppermute x26, starting transfers between devices, shift(): return lax.ppermute(value, axis, [(i, (i + by) % n) for i in range(n)])  37.8 us
    pallas_call x11, Pallas kernels, run(): pl.pallas_call(kernel, in_specs=[here] * len(arrays), out_specs=[here] *...  19.3 us
    all_to_all x1, blocking collectives, shards(): got = lax.all_to_all(pieces, LINE, 0, 0, tiled=True)  16 us
    all_to_all x1, blocking collectives, shards(): lax.all_to_all(routed.reshape(2 * GROUPS, CAP, LANES), LINE, 0, 0, tiled=...  14.1 us
    all_to_all x1, starting transfers between devices, shards(): low = lax.all_to_all(low, 'tensor_1', 0, 0, tiled=True)  6.28 us
    all_gather x1, waiting for transfers between devices, shards(): line_a = lax.all_gather(piece_a, 'tensor_1', axis=0)  6.11 us
    all_to_all x1, starting transfers between devices, shards(): top = lax.all_to_all(top, 'tensor_1', 0, 0, tiled=True)  5.37 us
  transfers between devices with their start and end apart: 29, of which 14 were waited for; matrix products, arithmetic and copies ran while one was open for 1% of the time, Pallas kernels for 5%

profile of v5, /device:TPU:1, one launch (start us, length us, event | category | flops | bytes accessed | tf_op | source)
XLA Modules:
  0.0 193.0 jit_solution(8501931257703894380)
XLA Ops:
  8.5 14.1 %all_to_all.20 = bf16[8,160,128]{2,1,0:T(8,128)(2,1)S(1)} all-to-all(bf16[8,160,128]{2,1,0:T(8,128)(2,1)} %bitcast.33), channel_id=1, replica_groups=mesh['expert'=4,'tensor_0'=4,'tensor_1'=8,'kv'=2] {'expert','kv'}, dimensions={0} | all-to-all | bytes 655360 | tf_op jit(solution)/shard_map/dispatch/all_to_all | solution.py:332
  25.6 2.2 %collective-permute-start = (bf16[448,128]{1,0:T(8,128)(2,1)S(1)}, bf16[448,128]{1,0:T(8,128)(2,1)S(1)}, u32[]{:S(2)}, u32[]{:S(2)}) collective-permute-start(bf16[448,128]{1,0:T(8,128)(2,1)S(1)} %get-tuple-element.48), channel_id=1, source_target_pairs={{0,48},{16,0},{32,16},{48,32},{1,49},{17,1},{33,17},{49,33},{2,50}... | collective-permute-start | bytes 344072 | tf_op jit(solution)/shard_map/gather/ppermute | solution.py:306
  30.3 3.2 %collective-permute-done.1 = bf16[448,128]{1,0:T(8,128)(2,1)S(1)} collective-permute-done((bf16[448,128]{1,0:T(8,128)(2,1)S(1)}, bf16[448,128]{1,0:T(8,128)(2,1)S(1)}, u32[]{:S(2)}, u32[]{:S(2)}) %collective-permute-start.1) | collective-permute-done | bytes 114720 | tf_op jit(solution)/shard_map/gather/ppermute | solution.py:306
  35.4 4.0 %collective-permute-start.4 = (bf16[4,448,128]{2,1,0:T(8,128)(2,1)S(1)}, bf16[4,448,128]{2,1,0:T(8,128)(2,1)S(1)}, u32[]{:S(2)}, u32[]{:S(2)}) collective-permute-start(bf16[4,448,128]{2,1,0:T(8,128)(2,1)S(1)} %pad_maximum_fusion.b0), channel_id=1, source_target_pairs={{0,14},{2,0},{4,2},{6,4},{8,6},{10,8},{12,10},{14,12},{1,15},{3,1}... | collective-permute-start | bytes 1376264 | tf_op jit(solution)/shard_map/gather/ppermute | solution.py:306
  39.4 14.5 %collective-permute-done.3.b7 = bf16[4,448,128]{2,1,0:T(8,128)(2,1)S(1)} collective-permute-done((bf16[4,448,128]{2,1,0:T(8,128)(2,1)S(1)}, bf16[4,448,128]{2,1,0:T(8,128)(2,1)S(1)}, u32[]{:S(2)}, u32[]{:S(2)}) %collective-permute-start.3) | collective-permute-done | bytes 458784 | tf_op jit(solution)/shard_map/gather/ppermute | solution.py:306
  55.1 6.1 %all-gather.3.cloned.1.call-done = bf16[4224,128]{1,0:T(8,128)(2,1)} async-done(((bf16[528,128]{1,0:T(8,128)(2,1)}), bf16[4224,128]{1,0:T(8,128)(2,1)}) %all-gather.3.cloned.1.call-update) | async-done | bytes 1081360 | tf_op jit(solution)/shard_map/gather/all_gather | solution.py:342
  68.0 6.5 %collective-permute-done.5.b6 = bf16[4,448,128]{2,1,0:T(8,128)(2,1)S(1)} collective-permute-done((bf16[4,448,128]{2,1,0:T(8,128)(2,1)S(1)}, bf16[4,448,128]{2,1,0:T(8,128)(2,1)S(1)}, u32[]{:S(2)}, u32[]{:S(2)}) %collective-permute-start.5) | collective-permute-done | bytes 458784 | tf_op jit(solution)/shard_map/gather/ppermute | solution.py:306
  74.6 3.0 %collective-permute-start.16 = (bf16[224,4096]{1,0:T(8,128)(2,1)}, bf16[224,4096]{1,0:T(8,128)(2,1)S(1)}, u32[]{:S(2)}, u32[]{:S(2)}) collective-permute-start(bf16[224,4096]{1,0:T(8,128)(2,1)} %bitcast.24), channel_id=1, source_target_pairs={{0,1},{1,0},{2,3},{3,2},{4,5},{5,4},{6,7},{7,6},{8,9},{9,8},{10,11... | collective-permute-start | bytes 5505032 | tf_op jit(solution)/shard_map/weights/ppermute | solution.py:306
  80.3 2.6 %collective-permute-start.11 = (bf16[4,448,128]{2,1,0:T(8,128)(2,1)S(1)}, bf16[4,448,128]{2,1,0:T(8,128)(2,1)S(1)}, u32[]{:S(2)}, u32[]{:S(2)}) collective-permute-start(bf16[4,448,128]{2,1,0:T(8,128)(2,1)S(1)} %collective-permute-done.6.b2), channel_id=1, source_target_pairs={{0,14},{2,0},{4,2},{6,4},{8,6},{10,8},{12,10},{14,12},{1,15},{3,1}... | collective-permute-start | bytes 1376264 | tf_op jit(solution)/shard_map/gather/ppermute | solution.py:306
  84.2 3.2 %collective-permute-done.12.far3_ref = bf16[4,528,128]{2,1,0:T(8,128)(2,1)S(1)} collective-permute-done((bf16[4,528,128]{2,1,0:T(8,128)(2,1)S(1)}, bf16[4,528,128]{2,1,0:T(8,128)(2,1)S(1)}, u32[]{:S(2)}, u32[]{:S(2)}) %collective-permute-start.12) | collective-permute-done | bytes 540704 | tf_op jit(solution)/shard_map/gather/ppermute | solution.py:306
  90.3 2.7 %collective-permute-start.18 = (bf16[2,448,128]{2,1,0:T(8,128)(2,1)S(1)}, bf16[2,448,128]{2,1,0:T(8,128)(2,1)S(1)}, u32[]{:S(2)}, u32[]{:S(2)}) collective-permute-start(bf16[2,448,128]{2,1,0:T(8,128)(2,1)S(1)} %slice.17), channel_id=1, source_target_pairs={{0,14},{2,0},{4,2},{6,4},{8,6},{10,8},{12,10},{14,12},{1,15},{3,1}... | collective-permute-start | bytes 688136 | tf_op jit(solution)/shard_map/gather/ppermute | solution.py:306
  93.7 5.2 %collective-permute-done.14.refs_2_.lo_ref = bf16[4,528,128]{2,1,0:T(8,128)(2,1)S(1)} collective-permute-done((bf16[4,528,128]{2,1,0:T(8,128)(2,1)S(1)}, bf16[4,528,128]{2,1,0:T(8,128)(2,1)S(1)}, u32[]{:S(2)}, u32[]{:S(2)}) %collective-permute-start.14) | collective-permute-done | bytes 540704 | tf_op jit(solution)/shard_map/gather/ppermute | solution.py:306
  98.9 2.0 %act.1 = (bf16[640,4096]{1,0:T(8,128)(2,1)S(1)}, f32[320,224]{1,0:T(8,128)S(1)}, bf16[320,224]{1,0:T(8,128)(2,1)S(1)}) custom-call(bf16[640,4096]{1,0:T(8,128)(2,1)S(1)} %get-tuple-element.74._ds, bf16[4,528,128]{2,1,0:T(8,128)(2,1)S(1)} %collective-permute-done.14.refs_2_.lo_ref, ...), custom_call_target="tpu_custom_call", output_to_operand_aliasing={{0}: (0, {})} | custom-call | flops 3000000000 | tf_op jit(solution)/shard_map/act/pallas_call | solution.py:38
  101.0 11.8 %collective-permute-done.16.refs_7_.refs_9_ = bf16[224,4096]{1,0:T(8,128)(2,1)S(1)} collective-permute-done((bf16[224,4096]{1,0:T(8,128)(2,1)}, bf16[224,4096]{1,0:T(8,128)(2,1)S(1)}, u32[]{:S(2)}, u32[]{:S(2)}) %collective-permute-start.16) | collective-permute-done | bytes 1835040 | tf_op jit(solution)/shard_map/weights/ppermute | solution.py:306
  112.8 4.7 %forward.1 = (bf16[320,4096]{1,0:T(8,128)(2,1)S(1)}, f32[320,128]{1,0:T(8,128)S(1)}, f32[320,224]{1,0:T(8,128)S(1)}, f32[320,224]{1,0:T(8,128)S(1)}, f32[320,224...) custom-call(bf16[320,4096]{1,0:T(8,128)(2,1)S(1)} %get-tuple-element, ...), custom_call_target="tpu_custom_call", output_to_operand_aliasing={{0}: (0, {}), {1}: (1, {})} | custom-call | flops 5000000000 | tf_op jit(solution)/shard_map/forward/pallas_call | solution.py:38
  117.6 5.5 %back.1 = (bf16[8,4,112,128]{3,2,1,0:T(8,128)(2,1)}, bf16[8,224,128]{2,1,0:T(8,128)(2,1)S(1)}, bf16[8,224,128]{2,1,0:T(8,128)(2,1)S(1)}, bf16[8,224,128]{2,1,0:T(8,128)(2,1)S(1)}, bf16[8,224,128]{2,1,0:T(8,128)(2,1)S(1)}) custom-call(f32[320,224]{1,0:T(8,128)S(1)} %get-tuple-element.70.refs_0_, f32[320,224]{1,0:T(8,128)S(1)} %get-tuple-element.71.refs_1_, ...), custom_call_target="tpu_custom_call" | custom-call | flops 8000000000 | tf_op jit(solution)/shard_map/back/pallas_call | solution.py:38
  124.7 5.4 %all-to-all-start.1 = ((bf16[8,4,112,128]{3,2,1,0:T(8,128)(2,1)}), bf16[8,4,112,128]{3,2,1,0:T(8,128)(2,1)S(1)}, u32[]{:S(2)}, u32[]{:S(2)}) async-start(bf16[8,4,112,128]{3,2,1,0:T(8,128)(2,1)} %get-tuple-element.79), calls=%async_computation.1 | async-start | bytes 1835008 | tf_op jit(solution)/shard_map/scatter/all_to_all | solution.py:397
  134.6 4.4 %collective-permute-done.20.refs_1_ = bf16[8,224,128]{2,1,0:T(8,128)(2,1)S(1)} collective-permute-done((bf16[8,224,128]{2,1,0:T(8,128)(2,1)S(1)}, bf16[8,224,128]{2,1,0:T(8,128)(2,1)S(1)}, u32[]{:S(2)}, u32[]{:S(2)}) %collective-permute-start.20) | collective-permute-done | bytes 458784 | tf_op jit(solution)/shard_map/scatter/ppermute | solution.py:306
  139.1 11.0 %collective-permute-done.21.refs_2_ = bf16[8,224,128]{2,1,0:T(8,128)(2,1)S(1)} collective-permute-done((bf16[8,224,128]{2,1,0:T(8,128)(2,1)S(1)}, bf16[8,224,128]{2,1,0:T(8,128)(2,1)S(1)}, u32[]{:S(2)}, u32[]{:S(2)}) %collective-permute-start.21) | collective-permute-done | bytes 458784 | tf_op jit(solution)/shard_map/scatter/ppermute | solution.py:306
  151.1 6.3 %all-to-all-start.2 = ((bf16[8,224,128]{2,1,0:T(8,128)(2,1)}), bf16[8,224,128]{2,1,0:T(8,128)(2,1)S(1)}, u32[]{:S(2)}, u32[]{:S(2)}) async-start(bf16[8,224,128]{2,1,0:T(8,128)(2,1)} %scatter.2), calls=%async_computation.2 | async-start | bytes 917504 | tf_op jit(solution)/shard_map/scatter/all_to_all | solution.py:402
  157.5 2.4 %collective-permute-start.23 = (bf16[112,128]{1,0:T(8,128)(2,1)S(1)}, bf16[112,128]{1,0:T(8,128)(2,1)S(1)}, u32[]{:S(2)}, u32[]{:S(2)}) collective-permute-start(bf16[112,128]{1,0:T(8,128)(2,1)S(1)} %get-tuple-element.86), channel_id=1, source_target_pairs={{0,32},{16,48},{32,0},{48,16},{1,33},{17,49},{33,1},{49,17},{2,34}... | collective-permute-start | bytes 86024 | tf_op jit(solution)/shard_map/scatter/ppermute | solution.py:306
  160.1 2.5 %collective-permute-start.25 = (bf16[112,128]{1,0:T(8,128)(2,1)S(1)}, bf16[112,128]{1,0:T(8,128)(2,1)S(1)}, u32[]{:S(2)}, u32[]{:S(2)}) collective-permute-start(bf16[112,128]{1,0:T(8,128)(2,1)S(1)} %get-tuple-element.88), channel_id=1, source_target_pairs={{0,48},{16,0},{32,16},{48,32},{1,49},{17,1},{33,17},{49,33},{2,50}... | collective-permute-start | bytes 86024 | tf_op jit(solution)/shard_map/scatter/ppermute | solution.py:306
  163.9 5.0 %all-to-all-done.2.refs_4_ = bf16[8,224,128]{2,1,0:T(8,128)(2,1)S(1)} async-done(((bf16[8,224,128]{2,1,0:T(8,128)(2,1)}), bf16[8,224,128]{2,1,0:T(8,128)(2,1)S(1)}, u32[]{:S(2)}, u32[]{:S(2)}) %all-to-all-start.2) | async-done | bytes 458784 | tf_op jit(solution)/shard_map/scatter/all_to_all | solution.py:402
  169.0 16.0 %all_to_all.21.got_ref = bf16[8,96,128]{2,1,0:T(8,128)(2,1)S(1)} all-to-all(bf16[8,96,128]{2,1,0:T(8,128)(2,1)S(1)} %combine.2), channel_id=1, replica_groups=mesh['expert'=4,'tensor_0'=4,'tensor_1'=8,'kv'=2] {'expert','kv'}, dimensions={0} | all-to-all | bytes 393216 | tf_op jit(solution)/shard_map/combine/all_to_all | solution.py:407
  (74 shorter events, 35.0 us)
Async XLA Ops:
  6.5 54.7 %all-gather.3.cloned.1.call-start = ((), (), s32[]{:S(2)}) async-start(), calls=%async_computation.4 | async-start | bytes 1216512 | tf_op jit(solution)/shard_map/gather/all_gather | solution.py:342
  24.2 43.8 %collective-permute-start.7 = (bf16[224,4096]{1,0:T(8,128)(2,1)S(1)}, bf16[224,4096]{1,0:T(8,128)(2,1)}, u32[]{:S(2)}, u32[]{:S(2)}) collective-permute-start(bf16[224,4096]{1,0:T(8,128)(2,1)S(1)} %bitcast.21), channel_id=1, source_target_pairs={{0,1},{1,0},{2,3},{3,2},{4,5},{5,4},{6,7},{7,6},{8,9},{9,8},{10,11... | collective-permute-start | bytes 5505032 | tf_op jit(solution)/shard_map/weights/ppermute | solution.py:306
  27.8 5.7 %collective-permute-start.1 = (bf16[448,128]{1,0:T(8,128)(2,1)S(1)}, bf16[448,128]{1,0:T(8,128)(2,1)S(1)}, u32[]{:S(2)}, u32[]{:S(2)}) collective-permute-start(bf16[448,128]{1,0:T(8,128)(2,1)S(1)} %get-tuple-element.48), channel_id=1, source_target_pairs={{0,32},{16,48},{32,0},{48,16},{1,33},{17,49},{33,1},{49,17},{2,34}... | collective-permute-start | bytes 344072 | tf_op jit(solution)/shard_map/gather/ppermute | solution.py:306
  33.6 20.4 %collective-permute-start.3 = (bf16[4,448,128]{2,1,0:T(8,128)(2,1)S(1)}, bf16[4,448,128]{2,1,0:T(8,128)(2,1)S(1)}, u32[]{:S(2)}, u32[]{:S(2)}) collective-permute-start(bf16[4,448,128]{2,1,0:T(8,128)(2,1)S(1)} %pad_maximum_fusion.b0), channel_id=1, source_target_pairs={{0,2},{2,4},{4,6},{6,8},{8,10},{10,12},{12,14},{14,0},{1,3},{3,5},... | collective-permute-start | bytes 1376264 | tf_op jit(solution)/shard_map/gather/ppermute | solution.py:306
  35.4 19.7 %collective-permute-start.4 = (bf16[4,448,128]{2,1,0:T(8,128)(2,1)S(1)}, bf16[4,448,128]{2,1,0:T(8,128)(2,1)S(1)}, u32[]{:S(2)}, u32[]{:S(2)}) collective-permute-start(bf16[4,448,128]{2,1,0:T(8,128)(2,1)S(1)} %pad_maximum_fusion.b0), channel_id=1, source_target_pairs={{0,14},{2,0},{4,2},{6,4},{8,6},{10,8},{12,10},{14,12},{1,15},{3,1}... | collective-permute-start | bytes 1376264 | tf_op jit(solution)/shard_map/gather/ppermute | solution.py:306
  62.6 12.0 %collective-permute-start.8 = (bf16[4,528,128]{2,1,0:T(8,128)(2,1)S(1)}, bf16[4,528,128]{2,1,0:T(8,128)(2,1)S(1)}, u32[]{:S(2)}, u32[]{:S(2)}) collective-permute-start(bf16[4,528,128]{2,1,0:T(8,128)(2,1)S(1)} %get-tuple-element.92), channel_id=1, source_target_pairs={{0,16},{16,32},{32,48},{48,0},{1,17},{17,33},{33,49},{49,1},{2,18}... | collective-permute-start | bytes 1622024 | tf_op jit(solution)/shard_map/gather/ppermute | solution.py:306
  64.2 10.3 %collective-permute-start.9 = (bf16[4,528,128]{2,1,0:T(8,128)(2,1)S(1)}, bf16[4,528,128]{2,1,0:T(8,128)(2,1)S(1)}, u32[]{:S(2)}, u32[]{:S(2)}) collective-permute-start(bf16[4,528,128]{2,1,0:T(8,128)(2,1)S(1)} %get-tuple-element.92), channel_id=1, source_target_pairs={{0,48},{16,0},{32,16},{48,32},{1,49},{17,1},{33,17},{49,33},{2,50}... | collective-permute-start | bytes 1622024 | tf_op jit(solution)/shard_map/gather/ppermute | solution.py:306
  65.4 9.2 %collective-permute-start.5 = (bf16[4,448,128]{2,1,0:T(8,128)(2,1)S(1)}, bf16[4,448,128]{2,1,0:T(8,128)(2,1)S(1)}, u32[]{:S(2)}, u32[]{:S(2)}) collective-permute-start(bf16[4,448,128]{2,1,0:T(8,128)(2,1)S(1)} %collective-permute-done.3.b7), channel_id=1, source_target_pairs={{0,2},{2,4},{4,6},{6,8},{8,10},{10,12},{12,14},{14,0},{1,3},{3,5},... | collective-permute-start | bytes 1376264 | tf_op jit(solution)/shard_map/gather/ppermute | solution.py:306
  66.7 7.9 %collective-permute-start.6 = (bf16[4,448,128]{2,1,0:T(8,128)(2,1)S(1)}, bf16[4,448,128]{2,1,0:T(8,128)(2,1)S(1)}, u32[]{:S(2)}, u32[]{:S(2)}) collective-permute-start(bf16[4,448,128]{2,1,0:T(8,128)(2,1)S(1)} %collective-permute-done.4.b1), channel_id=1, source_target_pairs={{0,14},{2,0},{4,2},{6,4},{8,6},{10,8},{12,10},{14,12},{1,15},{3,1}... | collective-permute-start | bytes 1376264 | tf_op jit(solution)/shard_map/gather/ppermute | solution.py:306
  74.6 38.3 %collective-permute-start.16 = (bf16[224,4096]{1,0:T(8,128)(2,1)}, bf16[224,4096]{1,0:T(8,128)(2,1)S(1)}, u32[]{:S(2)}, u32[]{:S(2)}) collective-permute-start(bf16[224,4096]{1,0:T(8,128)(2,1)} %bitcast.24), channel_id=1, source_target_pairs={{0,1},{1,0},{2,3},{3,2},{4,5},{5,4},{6,7},{7,6},{8,9},{9,8},{10,11... | collective-permute-start | bytes 5505032 | tf_op jit(solution)/shard_map/weights/ppermute | solution.py:306
  77.6 9.8 %collective-permute-start.12 = (bf16[4,528,128]{2,1,0:T(8,128)(2,1)S(1)}, bf16[4,528,128]{2,1,0:T(8,128)(2,1)S(1)}, u32[]{:S(2)}, u32[]{:S(2)}) collective-permute-start(bf16[4,528,128]{2,1,0:T(8,128)(2,1)S(1)} %get-tuple-element.91), channel_id=1, source_target_pairs={{0,16},{16,32},{32,48},{48,0},{1,17},{17,33},{33,49},{49,1},{2,18}... | collective-permute-start | bytes 1622024 | tf_op jit(solution)/shard_map/gather/ppermute | solution.py:306
  78.5 9.0 %collective-permute-start.13 = (bf16[4,528,128]{2,1,0:T(8,128)(2,1)S(1)}, bf16[4,528,128]{2,1,0:T(8,128)(2,1)S(1)}, u32[]{:S(2)}, u32[]{:S(2)}) collective-permute-start(bf16[4,528,128]{2,1,0:T(8,128)(2,1)S(1)} %get-tuple-element.91), channel_id=1, source_target_pairs={{0,48},{16,0},{32,16},{48,32},{1,49},{17,1},{33,17},{49,33},{2,50}... | collective-permute-start | bytes 1622024 | tf_op jit(solution)/shard_map/gather/ppermute | solution.py:306
  80.2 8.8 %collective-permute-start.10 = (bf16[4,448,128]{2,1,0:T(8,128)(2,1)S(1)}, bf16[4,448,128]{2,1,0:T(8,128)(2,1)S(1)}, u32[]{:S(2)}, u32[]{:S(2)}) collective-permute-start(bf16[4,448,128]{2,1,0:T(8,128)(2,1)S(1)} %collective-permute-done.5.b6), channel_id=1, source_target_pairs={{0,2},{2,4},{4,6},{6,8},{8,10},{10,12},{12,14},{14,0},{1,3},{3,5},... | collective-permute-start | bytes 1376264 | tf_op jit(solution)/shard_map/gather/ppermute | solution.py:306
  80.3 8.8 %collective-permute-start.11 = (bf16[4,448,128]{2,1,0:T(8,128)(2,1)S(1)}, bf16[4,448,128]{2,1,0:T(8,128)(2,1)S(1)}, u32[]{:S(2)}, u32[]{:S(2)}) collective-permute-start(bf16[4,448,128]{2,1,0:T(8,128)(2,1)S(1)} %collective-permute-done.6.b2), channel_id=1, source_target_pairs={{0,14},{2,0},{4,2},{6,4},{8,6},{10,8},{12,10},{14,12},{1,15},{3,1}... | collective-permute-start | bytes 1376264 | tf_op jit(solution)/shard_map/gather/ppermute | solution.py:306
  87.4 11.5 %collective-permute-start.14 = (bf16[4,528,128]{2,1,0:T(8,128)(2,1)S(1)}, bf16[4,528,128]{2,1,0:T(8,128)(2,1)S(1)}, u32[]{:S(2)}, u32[]{:S(2)}) collective-permute-start(bf16[4,528,128]{2,1,0:T(8,128)(2,1)S(1)} %collective-permute-done.8.near3_ref), channel_id=1, source_target_pairs={{0,16},{16,32},{32,48},{48,0},{1,17},{17,33},{33,49},{49,1},{2,18}... | collective-permute-start | bytes 1622024 | tf_op jit(solution)/shard_map/gather/ppermute | solution.py:306
  89.1 9.8 %collective-permute-start.15 = (bf16[4,528,128]{2,1,0:T(8,128)(2,1)S(1)}, bf16[4,528,128]{2,1,0:T(8,128)(2,1)S(1)}, u32[]{:S(2)}, u32[]{:S(2)}) collective-permute-start(bf16[4,528,128]{2,1,0:T(8,128)(2,1)S(1)} %collective-permute-done.13.far1_ref), channel_id=1, source_target_pairs={{0,48},{16,0},{32,16},{48,32},{1,49},{17,1},{33,17},{49,33},{2,50}... | collective-permute-start | bytes 1622024 | tf_op jit(solution)/shard_map/gather/ppermute | solution.py:306
  90.2 8.7 %collective-permute-start.17 = (bf16[2,448,128]{2,1,0:T(8,128)(2,1)S(1)}, bf16[2,448,128]{2,1,0:T(8,128)(2,1)S(1)}, u32[]{:S(2)}, u32[]{:S(2)}) collective-permute-start(bf16[2,448,128]{2,1,0:T(8,128)(2,1)S(1)} %slice.16), channel_id=1, source_target_pairs={{0,2},{2,4},{4,6},{6,8},{8,10},{10,12},{12,14},{14,0},{1,3},{3,5},... | collective-permute-start | bytes 688136 | tf_op jit(solution)/shard_map/gather/ppermute | solution.py:306
  90.3 8.6 %collective-permute-start.18 = (bf16[2,448,128]{2,1,0:T(8,128)(2,1)S(1)}, bf16[2,448,128]{2,1,0:T(8,128)(2,1)S(1)}, u32[]{:S(2)}, u32[]{:S(2)}) collective-permute-start(bf16[2,448,128]{2,1,0:T(8,128)(2,1)S(1)} %slice.17), channel_id=1, source_target_pairs={{0,14},{2,0},{4,2},{6,4},{8,6},{10,8},{12,10},{14,12},{1,15},{3,1}... | collective-permute-start | bytes 688136 | tf_op jit(solution)/shard_map/gather/ppermute | solution.py:306
  100.9 16.7 %collective-permute-start.19 = (bf16[320,224]{1,0:T(8,128)(2,1)S(1)}, bf16[320,224]{1,0:T(8,128)(2,1)S(1)}, u32[]{:S(2)}, u32[]{:S(2)}) collective-permute-start(bf16[320,224]{1,0:T(8,128)(2,1)S(1)} %get-tuple-element.78), channel_id=1, source_target_pairs={{0,1},{1,0},{2,3},{3,2},{4,5},{5,4},{6,7},{7,6},{8,9},{9,8},{10,11... | collective-permute-start | bytes 430088 | tf_op jit(solution)/shard_map/act/ppermute | solution.py:306
  124.7 26.4 %all-to-all-start.1 = ((bf16[8,4,112,128]{3,2,1,0:T(8,128)(2,1)}), bf16[8,4,112,128]{3,2,1,0:T(8,128)(2,1)S(1)}, u32[]{:S(2)}, u32[]{:S(2)}) async-start(bf16[8,4,112,128]{3,2,1,0:T(8,128)(2,1)} %get-tuple-element.79), calls=%async_computation.1 | async-start | bytes 1835008 | tf_op jit(solution)/shard_map/scatter/all_to_all | solution.py:397
  130.0 9.0 %collective-permute-start.20 = (bf16[8,224,128]{2,1,0:T(8,128)(2,1)S(1)}, bf16[8,224,128]{2,1,0:T(8,128)(2,1)S(1)}, u32[]{:S(2)}, u32[]{:S(2)}) collective-permute-start(bf16[8,224,128]{2,1,0:T(8,128)(2,1)S(1)} %copy-done.5), channel_id=1, source_target_pairs={{0,32},{16,48},{32,0},{48,16},{1,33},{17,49},{33,1},{49,17},{2,34}... | collective-permute-start | bytes 1376264 | tf_op jit(solution)/shard_map/scatter/ppermute | solution.py:306
  132.0 18.1 %collective-permute-start.21 = (bf16[8,224,128]{2,1,0:T(8,128)(2,1)S(1)}, bf16[8,224,128]{2,1,0:T(8,128)(2,1)S(1)}, u32[]{:S(2)}, u32[]{:S(2)}) collective-permute-start(bf16[8,224,128]{2,1,0:T(8,128)(2,1)S(1)} %get-tuple-element.82), channel_id=1, source_target_pairs={{0,16},{16,32},{32,48},{48,0},{1,17},{17,33},{33,49},{49,1},{2,18}... | collective-permute-start | bytes 1376264 | tf_op jit(solution)/shard_map/scatter/ppermute | solution.py:306
  132.9 17.2 %collective-permute-start.22 = (bf16[8,224,128]{2,1,0:T(8,128)(2,1)S(1)}, bf16[8,224,128]{2,1,0:T(8,128)(2,1)S(1)}, u32[]{:S(2)}, u32[]{:S(2)}) collective-permute-start(bf16[8,224,128]{2,1,0:T(8,128)(2,1)S(1)} %get-tuple-element.83), channel_id=1, source_target_pairs={{0,48},{16,0},{32,16},{48,32},{1,49},{17,1},{33,17},{49,33},{2,50}... | collective-permute-start | bytes 1376264 | tf_op jit(solution)/shard_map/scatter/ppermute | solution.py:306
  151.1 17.8 %all-to-all-start.2 = ((bf16[8,224,128]{2,1,0:T(8,128)(2,1)}), bf16[8,224,128]{2,1,0:T(8,128)(2,1)S(1)}, u32[]{:S(2)}, u32[]{:S(2)}) async-start(bf16[8,224,128]{2,1,0:T(8,128)(2,1)} %scatter.2), calls=%async_computation.2 | async-start | bytes 917504 | tf_op jit(solution)/shard_map/scatter/all_to_all | solution.py:402
  (16 other events, 146.6 us)
Sparse Core Ops, SparseCore 0:
  23.6 37.5 all-gather.2

commit v6 on v4

--- a/solution.py
+++ b/solution.py
@@ -31,7 +31,7 @@
 TN = (((0,), (0,)), ((), ()))
 
 
-def call(kernel, outs, us, scratch=(), limit=6, aliases=None):
+def call(kernel, outs, us, scratch=(), limit=10, aliases=None):
     here = pl.BlockSpec(memory_space=pltpu.VMEM) if limit < 32 else pl.BlockSpec()
 
     def run(*arrays):
@@ -334,10 +334,11 @@
             ids, probs, x_t, grad_t, gain_row
         )
         got = lax.all_to_all(routed.reshape(2 * GROUPS, CAP, LANES), LINE, 0, 0, tiled=True)
-        got, own_wg = lax.optimization_barrier((got, wg))
         copies, piece_b = call(
             assemble_kernel, [((NZ, XROWS + SPLIT, LANES), BF16), ((ROWS - SPLIT, LANES), BF16)], 2
         )(got.reshape(GROUPS, 2, CAP, LANES))
+
+        piece_b, own_wg = lax.optimization_barrier((piece_b, wg))
 
     with jax.named_scope("weights"):
         wgp = shift(own_wg, "kv", 1)
@@ -345,17 +346,19 @@
         line_a = lax.all_to_all(copies, "tensor_1", 0, 0, tiled=True)
         line_b = jnp.stack([piece_b] + [shift(piece_b, "tensor_0", -a) for a in (1, 2, 3)])
 
+        line_b, own_wu = lax.optimization_barrier((line_b, wu))
+        wup = shift(own_wu, "kv", 1)
         near, far, state = [], [], None
         placed = [((HALF, D), BF16), ((ROWS, D), BF16), ((HALF, LANES), F32)]
 
         def meet(step, right, left, got):
             nonlocal line_a, wgp, state
             if step == 2:
-                right, left, line_a, wgp = lax.optimization_barrier((right, left, line_a, wgp))
+                right, left, line_a = lax.optimization_barrier((right, left, line_a))
                 near[:] = [shift(line_a[: NZ // 2], "tensor_0", by) for by in (1, -1)]
                 far[:] = [shift(line_a[NZ // 2 :], "tensor_0", by) for by in (1, -1)]
             if step == 3:
-                right, left, *near[:] = lax.optimization_barrier((right, left, *near))
+                right, left, wgp, *near[:] = lax.optimization_barrier((right, left, wgp, *near))
                 early = [got[b] for b in (0, 1, 2, 6, 7)]
                 state = [*call(place_first_kernel, placed, 5)(line_a, near[1], near[0], *early)]
             if step == 4:
@@ -368,10 +371,6 @@
         xs, ds, sq = call(place_second_kernel, placed, 3, aliases={0: 0, 1: 1, 2: 2})(
             *state, far[1], far[0], b_got[3], b_got[5]
         )
-    with jax.named_scope("weights"):
-        wgp, own_wu = lax.optimization_barrier((wgp, wu))
-        wup = shift(own_wu, "kv", 1)
-
     with jax.named_scope("act"):
         _, act, theirs = call(
             act_kernel,

time: 181 us -> 183 us (1.011)
  blocking collectives: 29.9 us -> 27.1 us
  waiting for transfers between devices: 65 us -> 67.5 us
    all_to_all x1, blocking collectives: 15.7 us -> 13 us  [shards(): got = lax.all_to_all(pieces, LINE, 0, 0, tiled=True)]
  transfers between devices with their start and end apart: 29 -> 29, of which waited for: 11 -> 13; matrix products, arithmetic and copies ran while one was open for 0% -> 0% of each run, Pallas kernels for 7% -> 6%
where the time goes in v6:
time: 183 us; the launch traced here: 182 us
  waiting for transfers between devices  67.5 us (37%)
  starting transfers between devices  61.6 us (34%)
  blocking collectives  27.1 us (15%)
  Pallas kernels  21.8 us (12%)
  local copies, waits for them, and re-layouts  3.73 us (2%)
    ppermute x26, waiting for transfers between devices, shift(): return lax.ppermute(value, axis, [(i, (i + by) % n) for i in range(n)])  62.6 us
    ppermute x26, starting transfers between devices, shift(): return lax.ppermute(value, axis, [(i, (i + by) % n) for i in range(n)])  41.6 us
    pallas_call x11, Pallas kernels, run(): pl.pallas_call(kernel, in_specs=[here] * len(arrays), out_specs=[here] *...  21.8 us
    all_to_all x1, blocking collectives, shards(): lax.all_to_all(routed.reshape(2 * GROUPS, CAP, LANES), LINE, 0, 0, tiled=...  14.1 us
    all_to_all x1, blocking collectives, shards(): got = lax.all_to_all(pieces, LINE, 0, 0, tiled=True)  13 us
    all_to_all x1, starting transfers between devices, shards(): line_a = lax.all_to_all(copies, 'tensor_1', 0, 0, tiled=True)  7.42 us
    all_to_all x1, starting transfers between devices, shards(): low = lax.all_to_all(low, 'tensor_1', 0, 0, tiled=True)  6.37 us
    all_to_all x1, starting transfers between devices, shards(): top = lax.all_to_all(top, 'tensor_1', 0, 0, tiled=True)  6.24 us
  transfers between devices with their start and end apart: 29, of which 13 were waited for; matrix products, arithmetic and copies ran while one was open for 0% of the time, Pallas kernels for 6%

profile of v6, /device:TPU:1, one launch (start us, length us, event | category | flops | bytes accessed | tf_op | source)
XLA Modules:
  0.0 182.0 jit_solution(10798885905924277162)
XLA Ops:
  2.0 14.1 %all_to_all.25 = bf16[8,160,128]{2,1,0:T(8,128)(2,1)S(1)} all-to-all(bf16[8,160,128]{2,1,0:T(8,128)(2,1)} %bitcast.30), channel_id=1, replica_groups=mesh['expert'=4,'tensor_0'=4,'tensor_1'=8,'kv'=2] {'expert','kv'}, dimensions={0} | all-to-all | bytes 655360 | tf_op jit(solution)/shard_map/dispatch/all_to_all | solution.py:336
  17.3 7.4 %all-to-all-start.1 = ((bf16[8,480,128]{2,1,0:T(8,128)(2,1)}), bf16[8,480,128]{2,1,0:T(8,128)(2,1)S(1)}, u32[]{:S(2)}, u32[]{:S(2)}) async-start(bf16[8,480,128]{2,1,0:T(8,128)(2,1)} %get-tuple-element.51), calls=%async_computation.1 | async-start | bytes 1966080 | tf_op jit(solution)/shard_map/gather/all_to_all | solution.py:346
  25.7 2.9 %collective-permute-start.1 = (bf16[496,128]{1,0:T(8,128)(2,1)S(1)}, bf16[496,128]{1,0:T(8,128)(2,1)S(1)}, u32[]{:S(2)}, u32[]{:S(2)}) collective-permute-start(bf16[496,128]{1,0:T(8,128)(2,1)S(1)} %get-tuple-element.49), channel_id=1, source_target_pairs={{0,32},{16,48},{32,0},{48,16},{1,33},{17,49},{33,1},{49,17},{2,34}... | collective-permute-start | bytes 380936 | tf_op jit(solution)/shard_map/gather/ppermute | solution.py:310
  31.3 3.6 %collective-permute-done.2 = bf16[496,128]{1,0:T(8,128)(2,1)S(1)} collective-permute-done((bf16[496,128]{1,0:T(8,128)(2,1)S(1)}, bf16[496,128]{1,0:T(8,128)(2,1)S(1)}, u32[]{:S(2)}, u32[]{:S(2)}) %collective-permute-start.2) | collective-permute-done | bytes 127008 | tf_op jit(solution)/shard_map/gather/ppermute | solution.py:310
  39.7 20.2 %collective-permute-done.3.b7 = bf16[4,496,128]{2,1,0:T(8,128)(2,1)S(1)} collective-permute-done((bf16[4,496,128]{2,1,0:T(8,128)(2,1)S(1)}, bf16[4,496,128]{2,1,0:T(8,128)(2,1)S(1)}, u32[]{:S(2)}, u32[]{:S(2)}) %collective-permute-start.3) | collective-permute-done | bytes 507936 | tf_op jit(solution)/shard_map/gather/ppermute | solution.py:310
  60.7 2.7 %collective-permute-start.6 = (bf16[4,496,128]{2,1,0:T(8,128)(2,1)}, bf16[4,496,128]{2,1,0:T(8,128)(2,1)S(1)}, u32[]{:S(2)}, u32[]{:S(2)}) collective-permute-start(bf16[4,496,128]{2,1,0:T(8,128)(2,1)} %collective-permute-done.4.b1), channel_id=1, source_target_pairs={{0,14},{2,0},{4,2},{6,4},{8,6},{10,8},{12,10},{14,12},{1,15},{3,1}... | collective-permute-start | bytes 1523720 | tf_op jit(solution)/shard_map/gather/ppermute | solution.py:310
  67.3 2.7 %collective-permute-start.9 = (bf16[4,480,128]{2,1,0:T(8,128)(2,1)S(1)}, bf16[4,480,128]{2,1,0:T(8,128)(2,1)S(1)}, u32[]{:S(2)}, u32[]{:S(2)}) collective-permute-start(bf16[4,480,128]{2,1,0:T(8,128)(2,1)S(1)} %get-tuple-element.92), channel_id=1, source_target_pairs={{0,48},{16,0},{32,16},{48,32},{1,49},{17,1},{33,17},{49,33},{2,50}... | collective-permute-start | bytes 1474568 | tf_op jit(solution)/shard_map/gather/ppermute | solution.py:310
  70.1 5.7 %collective-permute-done.8.near3_ref = bf16[4,480,128]{2,1,0:T(8,128)(2,1)S(1)} collective-permute-done((bf16[4,480,128]{2,1,0:T(8,128)(2,1)S(1)}, bf16[4,480,128]{2,1,0:T(8,128)(2,1)S(1)}, u32[]{:S(2)}, u32[]{:S(2)}) %collective-permute-start.8) | collective-permute-done | bytes 491552 | tf_op jit(solution)/shard_map/gather/ppermute | solution.py:310
  81.5 2.6 %collective-permute-start.13 = (bf16[4,480,128]{2,1,0:T(8,128)(2,1)S(1)}, bf16[4,480,128]{2,1,0:T(8,128)(2,1)S(1)}, u32[]{:S(2)}, u32[]{:S(2)}) collective-permute-start(bf16[4,480,128]{2,1,0:T(8,128)(2,1)S(1)} %get-tuple-element.91), channel_id=1, source_target_pairs={{0,48},{16,0},{32,16},{48,32},{1,49},{17,1},{33,17},{49,33},{2,50}... | collective-permute-start | bytes 1474568 | tf_op jit(solution)/shard_map/gather/ppermute | solution.py:310
  87.4 4.2 %collective-permute-done.12.far3_ref = bf16[4,480,128]{2,1,0:T(8,128)(2,1)S(1)} collective-permute-done((bf16[4,480,128]{2,1,0:T(8,128)(2,1)S(1)}, bf16[4,480,128]{2,1,0:T(8,128)(2,1)S(1)}, u32[]{:S(2)}, u32[]{:S(2)}) %collective-permute-start.12) | collective-permute-done | bytes 491552 | tf_op jit(solution)/shard_map/gather/ppermute | solution.py:310
  91.7 2.7 %collective-permute-start.15 = (bf16[4,480,128]{2,1,0:T(8,128)(2,1)S(1)}, bf16[4,480,128]{2,1,0:T(8,128)(2,1)S(1)}, u32[]{:S(2)}, u32[]{:S(2)}) collective-permute-start(bf16[4,480,128]{2,1,0:T(8,128)(2,1)S(1)} %collective-permute-done.13.far1_ref), channel_id=1, source_target_pairs={{0,48},{16,0},{32,16},{48,32},{1,49},{17,1},{33,17},{49,33},{2,50}... | collective-permute-start | bytes 1474568 | tf_op jit(solution)/shard_map/gather/ppermute | solution.py:310
  94.6 2.7 %collective-permute-start.18 = (bf16[2,496,128]{2,1,0:T(8,128)(2,1)S(1)}, bf16[2,496,128]{2,1,0:T(8,128)(2,1)S(1)}, u32[]{:S(2)}, u32[]{:S(2)}) collective-permute-start(bf16[2,496,128]{2,1,0:T(8,128)(2,1)S(1)} %slice.17), channel_id=1, source_target_pairs={{0,14},{2,0},{4,2},{6,4},{8,6},{10,8},{12,10},{14,12},{1,15},{3,1}... | collective-permute-start | bytes 761864 | tf_op jit(solution)/shard_map/gather/ppermute | solution.py:310
  98.0 3.4 %collective-permute-done.14.refs_2_.lo_ref = bf16[4,480,128]{2,1,0:T(8,128)(2,1)S(1)} collective-permute-done((bf16[4,480,128]{2,1,0:T(8,128)(2,1)S(1)}, bf16[4,480,128]{2,1,0:T(8,128)(2,1)S(1)}, u32[]{:S(2)}, u32[]{:S(2)}) %collective-permute-start.14) | collective-permute-done | bytes 491552 | tf_op jit(solution)/shard_map/gather/ppermute | solution.py:310
  103.6 3.1 %collective-permute-done.16.refs_7_.refs_9_ = bf16[224,4096]{1,0:T(8,128)(2,1)} collective-permute-done((bf16[224,4096]{1,0:T(8,128)(2,1)}, bf16[224,4096]{1,0:T(8,128)(2,1)}, u32[]{:S(2)}, u32[]{:S(2)}) %collective-permute-start.16) | collective-permute-done | bytes 1835040 | tf_op jit(solution)/shard_map/gather/ppermute | solution.py:310
  106.7 5.2 %forward.1 = (bf16[320,4096]{1,0:T(8,128)(2,1)S(1)}, f32[320,128]{1,0:T(8,128)S(1)}, f32[320,224]{1,0:T(8,128)S(1)}, f32[320,224]{1,0:T(8,128)S(1)}, f32[320,224...) custom-call(bf16[320,4096]{1,0:T(8,128)(2,1)S(1)} %get-tuple-element, ...), custom_call_target="tpu_custom_call", output_to_operand_aliasing={{0}: (0, {}), {1}: (1, {})} | custom-call | flops 5000000000 | tf_op jit(solution)/shard_map/forward/pallas_call | solution.py:38
  111.9 6.1 %back.1 = (bf16[8,4,112,128]{3,2,1,0:T(8,128)(2,1)}, bf16[8,224,128]{2,1,0:T(8,128)(2,1)S(1)}, bf16[8,224,128]{2,1,0:T(8,128)(2,1)S(1)}, bf16[8,224,128]{2,1,0:T(8,128)(2,1)S(1)}, bf16[8,224,128]{2,1,0:T(8,128)(2,1)S(1)}) custom-call(f32[320,224]{1,0:T(8,128)S(1)} %get-tuple-element.70.refs_0_, f32[320,224]{1,0:T(8,128)S(1)} %get-tuple-element.71.refs_1_, ...), custom_call_target="tpu_custom_call" | custom-call | flops 8000000000 | tf_op jit(solution)/shard_map/back/pallas_call | solution.py:38
  118.8 6.2 %all-to-all-start.2 = ((bf16[8,4,112,128]{3,2,1,0:T(8,128)(2,1)}), bf16[8,4,112,128]{3,2,1,0:T(8,128)(2,1)S(1)}, u32[]{:S(2)}, u32[]{:S(2)}) async-start(bf16[8,4,112,128]{3,2,1,0:T(8,128)(2,1)} %get-tuple-element.79), calls=%async_computation.2 | async-start | bytes 1835008 | tf_op jit(solution)/shard_map/scatter/all_to_all | solution.py:399
  125.0 2.9 %collective-permute-start.20 = (bf16[8,224,128]{2,1,0:T(8,128)(2,1)S(1)}, bf16[8,224,128]{2,1,0:T(8,128)(2,1)S(1)}, u32[]{:S(2)}, u32[]{:S(2)}) collective-permute-start(bf16[8,224,128]{2,1,0:T(8,128)(2,1)S(1)} %get-tuple-element.81), channel_id=1, source_target_pairs={{0,32},{16,48},{32,0},{48,16},{1,33},{17,49},{33,1},{49,17},{2,34}... | collective-permute-start | bytes 1376264 | tf_op jit(solution)/shard_map/scatter/ppermute | solution.py:310
  130.6 3.3 %collective-permute-done.20.refs_1_ = bf16[8,224,128]{2,1,0:T(8,128)(2,1)S(1)} collective-permute-done((bf16[8,224,128]{2,1,0:T(8,128)(2,1)S(1)}, bf16[8,224,128]{2,1,0:T(8,128)(2,1)S(1)}, u32[]{:S(2)}, u32[]{:S(2)}) %collective-permute-start.20) | collective-permute-done | bytes 458784 | tf_op jit(solution)/shard_map/scatter/ppermute | solution.py:310
  134.0 13.1 %collective-permute-done.21.refs_2_ = bf16[8,224,128]{2,1,0:T(8,128)(2,1)S(1)} collective-permute-done((bf16[8,224,128]{2,1,0:T(8,128)(2,1)S(1)}, bf16[8,224,128]{2,1,0:T(8,128)(2,1)S(1)}, u32[]{:S(2)}, u32[]{:S(2)}) %collective-permute-start.21) | collective-permute-done | bytes 458784 | tf_op jit(solution)/shard_map/scatter/ppermute | solution.py:310
  149.1 6.4 %all-to-all-start.3 = ((bf16[8,224,128]{2,1,0:T(8,128)(2,1)}), bf16[8,224,128]{2,1,0:T(8,128)(2,1)S(1)}, u32[]{:S(2)}, u32[]{:S(2)}) async-start(bf16[8,224,128]{2,1,0:T(8,128)(2,1)} %scatter.2), calls=%async_computation.3 | async-start | bytes 917504 | tf_op jit(solution)/shard_map/scatter/all_to_all | solution.py:404
  155.5 3.4 %collective-permute-start.23 = (bf16[112,128]{1,0:T(8,128)(2,1)S(1)}, bf16[112,128]{1,0:T(8,128)(2,1)S(1)}, u32[]{:S(2)}, u32[]{:S(2)}) collective-permute-start(bf16[112,128]{1,0:T(8,128)(2,1)S(1)} %get-tuple-element.86), channel_id=1, source_target_pairs={{0,32},{16,48},{32,0},{48,16},{1,33},{17,49},{33,1},{49,17},{2,34}... | collective-permute-start | bytes 86024 | tf_op jit(solution)/shard_map/scatter/ppermute | solution.py:310
  162.9 4.9 %all-to-all-done.3.refs_4_ = bf16[8,224,128]{2,1,0:T(8,128)(2,1)S(1)} async-done(((bf16[8,224,128]{2,1,0:T(8,128)(2,1)}), bf16[8,224,128]{2,1,0:T(8,128)(2,1)S(1)}, u32[]{:S(2)}, u32[]{:S(2)}) %all-to-all-start.3) | async-done | bytes 458784 | tf_op jit(solution)/shard_map/scatter/all_to_all | solution.py:404
  167.9 13.0 %all_to_all.26.got_ref = bf16[8,96,128]{2,1,0:T(8,128)(2,1)S(1)} all-to-all(bf16[8,96,128]{2,1,0:T(8,128)(2,1)S(1)} %combine.2), channel_id=1, replica_groups=mesh['expert'=4,'tensor_0'=4,'tensor_1'=8,'kv'=2] {'expert','kv'}, dimensions={0} | all-to-all | bytes 393216 | tf_op jit(solution)/shard_map/combine/all_to_all | solution.py:409
  (71 shorter events, 39.0 us)
Async XLA Ops:
  17.3 43.4 %all-to-all-start.1 = ((bf16[8,480,128]{2,1,0:T(8,128)(2,1)}), bf16[8,480,128]{2,1,0:T(8,128)(2,1)S(1)}, u32[]{:S(2)}, u32[]{:S(2)}) async-start(bf16[8,480,128]{2,1,0:T(8,128)(2,1)} %get-tuple-element.51), calls=%async_computation.1 | async-start | bytes 1966080 | tf_op jit(solution)/shard_map/gather/all_to_all | solution.py:346
  24.8 42.6 %collective-permute-start.7 = (bf16[224,4096]{1,0:T(8,128)(2,1)S(1)}, bf16[224,4096]{1,0:T(8,128)(2,1)}, u32[]{:S(2)}, u32[]{:S(2)}) collective-permute-start(bf16[224,4096]{1,0:T(8,128)(2,1)S(1)} %bitcast.18), channel_id=1, source_target_pairs={{0,1},{1,0},{2,3},{3,2},{4,5},{5,4},{6,7},{7,6},{8,9},{9,8},{10,11... | collective-permute-start | bytes 5505032 | tf_op jit(solution)/shard_map/weights/ppermute | solution.py:310
  28.6 6.4 %collective-permute-start.2 = (bf16[496,128]{1,0:T(8,128)(2,1)S(1)}, bf16[496,128]{1,0:T(8,128)(2,1)S(1)}, u32[]{:S(2)}, u32[]{:S(2)}) collective-permute-start(bf16[496,128]{1,0:T(8,128)(2,1)S(1)} %get-tuple-element.49), channel_id=1, source_target_pairs={{0,16},{16,32},{32,48},{48,0},{1,17},{17,33},{33,49},{49,1},{2,18}... | collective-permute-start | bytes 380936 | tf_op jit(solution)/shard_map/gather/ppermute | solution.py:310
  35.0 24.9 %collective-permute-start.3 = (bf16[4,496,128]{2,1,0:T(8,128)(2,1)S(1)}, bf16[4,496,128]{2,1,0:T(8,128)(2,1)S(1)}, u32[]{:S(2)}, u32[]{:S(2)}) collective-permute-start(bf16[4,496,128]{2,1,0:T(8,128)(2,1)S(1)} %pad_maximum_fusion.b0), channel_id=1, source_target_pairs={{0,2},{2,4},{4,6},{6,8},{8,10},{10,12},{12,14},{14,0},{1,3},{3,5},... | collective-permute-start | bytes 1523720 | tf_op jit(solution)/shard_map/gather/ppermute | solution.py:310
  36.6 24.1 %collective-permute-start.4 = (bf16[4,496,128]{2,1,0:T(8,128)(2,1)S(1)}, bf16[4,496,128]{2,1,0:T(8,128)(2,1)}, u32[]{:S(2)}, u32[]{:S(2)}) collective-permute-start(bf16[4,496,128]{2,1,0:T(8,128)(2,1)S(1)} %pad_maximum_fusion.b0), channel_id=1, source_target_pairs={{0,14},{2,0},{4,2},{6,4},{8,6},{10,8},{12,10},{14,12},{1,15},{3,1}... | collective-permute-start | bytes 1523720 | tf_op jit(solution)/shard_map/gather/ppermute | solution.py:310
  37.9 68.8 %collective-permute-start.16 = (bf16[224,4096]{1,0:T(8,128)(2,1)}, bf16[224,4096]{1,0:T(8,128)(2,1)}, u32[]{:S(2)}, u32[]{:S(2)}) collective-permute-start(bf16[224,4096]{1,0:T(8,128)(2,1)} %bitcast.21), channel_id=1, source_target_pairs={{0,1},{1,0},{2,3},{3,2},{4,5},{5,4},{6,7},{7,6},{8,9},{9,8},{10,11... | collective-permute-start | bytes 5505032 | tf_op jit(solution)/shard_map/gather/ppermute | solution.py:310
  60.7 17.2 %collective-permute-start.5 = (bf16[4,496,128]{2,1,0:T(8,128)(2,1)}, bf16[4,496,128]{2,1,0:T(8,128)(2,1)S(1)}, u32[]{:S(2)}, u32[]{:S(2)}) collective-permute-start(bf16[4,496,128]{2,1,0:T(8,128)(2,1)} %copy-done.3), channel_id=1, source_target_pairs={{0,2},{2,4},{4,6},{6,8},{8,10},{10,12},{12,14},{14,0},{1,3},{3,5},... | collective-permute-start | bytes 1523720 | tf_op jit(solution)/shard_map/gather/ppermute | solution.py:310
  60.7 17.2 %collective-permute-start.6 = (bf16[4,496,128]{2,1,0:T(8,128)(2,1)}, bf16[4,496,128]{2,1,0:T(8,128)(2,1)S(1)}, u32[]{:S(2)}, u32[]{:S(2)}) collective-permute-start(bf16[4,496,128]{2,1,0:T(8,128)(2,1)} %collective-permute-done.4.b1), channel_id=1, source_target_pairs={{0,14},{2,0},{4,2},{6,4},{8,6},{10,8},{12,10},{14,12},{1,15},{3,1}... | collective-permute-start | bytes 1523720 | tf_op jit(solution)/shard_map/gather/ppermute | solution.py:310
  63.5 12.4 %collective-permute-start.8 = (bf16[4,480,128]{2,1,0:T(8,128)(2,1)S(1)}, bf16[4,480,128]{2,1,0:T(8,128)(2,1)S(1)}, u32[]{:S(2)}, u32[]{:S(2)}) collective-permute-start(bf16[4,480,128]{2,1,0:T(8,128)(2,1)S(1)} %get-tuple-element.92), channel_id=1, source_target_pairs={{0,16},{16,32},{32,48},{48,0},{1,17},{17,33},{33,49},{49,1},{2,18}... | collective-permute-start | bytes 1474568 | tf_op jit(solution)/shard_map/gather/ppermute | solution.py:310
  67.3 10.6 %collective-permute-start.9 = (bf16[4,480,128]{2,1,0:T(8,128)(2,1)S(1)}, bf16[4,480,128]{2,1,0:T(8,128)(2,1)S(1)}, u32[]{:S(2)}, u32[]{:S(2)}) collective-permute-start(bf16[4,480,128]{2,1,0:T(8,128)(2,1)S(1)} %get-tuple-element.92), channel_id=1, source_target_pairs={{0,48},{16,0},{32,16},{48,32},{1,49},{17,1},{33,17},{49,33},{2,50}... | collective-permute-start | bytes 1474568 | tf_op jit(solution)/shard_map/gather/ppermute | solution.py:310
  77.9 13.8 %collective-permute-start.10 = (bf16[4,496,128]{2,1,0:T(8,128)(2,1)S(1)}, bf16[4,496,128]{2,1,0:T(8,128)(2,1)S(1)}, u32[]{:S(2)}, u32[]{:S(2)}) collective-permute-start(bf16[4,496,128]{2,1,0:T(8,128)(2,1)S(1)} %collective-permute-done.5.b6), channel_id=1, source_target_pairs={{0,2},{2,4},{4,6},{6,8},{8,10},{10,12},{12,14},{14,0},{1,3},{3,5},... | collective-permute-start | bytes 1523720 | tf_op jit(solution)/shard_map/gather/ppermute | solution.py:310
  78.3 13.4 %collective-permute-start.11 = (bf16[4,496,128]{2,1,0:T(8,128)(2,1)S(1)}, bf16[4,496,128]{2,1,0:T(8,128)(2,1)S(1)}, u32[]{:S(2)}, u32[]{:S(2)}) collective-permute-start(bf16[4,496,128]{2,1,0:T(8,128)(2,1)S(1)} %collective-permute-done.6.b2), channel_id=1, source_target_pairs={{0,14},{2,0},{4,2},{6,4},{8,6},{10,8},{12,10},{14,12},{1,15},{3,1}... | collective-permute-start | bytes 1523720 | tf_op jit(solution)/shard_map/gather/ppermute | solution.py:310
  80.6 11.1 %collective-permute-start.12 = (bf16[4,480,128]{2,1,0:T(8,128)(2,1)S(1)}, bf16[4,480,128]{2,1,0:T(8,128)(2,1)S(1)}, u32[]{:S(2)}, u32[]{:S(2)}) collective-permute-start(bf16[4,480,128]{2,1,0:T(8,128)(2,1)S(1)} %get-tuple-element.91), channel_id=1, source_target_pairs={{0,16},{16,32},{32,48},{48,0},{1,17},{17,33},{33,49},{49,1},{2,18}... | collective-permute-start | bytes 1474568 | tf_op jit(solution)/shard_map/gather/ppermute | solution.py:310
  81.5 10.2 %collective-permute-start.13 = (bf16[4,480,128]{2,1,0:T(8,128)(2,1)S(1)}, bf16[4,480,128]{2,1,0:T(8,128)(2,1)S(1)}, u32[]{:S(2)}, u32[]{:S(2)}) collective-permute-start(bf16[4,480,128]{2,1,0:T(8,128)(2,1)S(1)} %get-tuple-element.91), channel_id=1, source_target_pairs={{0,48},{16,0},{32,16},{48,32},{1,49},{17,1},{33,17},{49,33},{2,50}... | collective-permute-start | bytes 1474568 | tf_op jit(solution)/shard_map/gather/ppermute | solution.py:310
  91.7 9.8 %collective-permute-start.14 = (bf16[4,480,128]{2,1,0:T(8,128)(2,1)S(1)}, bf16[4,480,128]{2,1,0:T(8,128)(2,1)S(1)}, u32[]{:S(2)}, u32[]{:S(2)}) collective-permute-start(bf16[4,480,128]{2,1,0:T(8,128)(2,1)S(1)} %collective-permute-done.8.near3_ref), channel_id=1, source_target_pairs={{0,16},{16,32},{32,48},{48,0},{1,17},{17,33},{33,49},{49,1},{2,18}... | collective-permute-start | bytes 1474568 | tf_op jit(solution)/shard_map/gather/ppermute | solution.py:310
  91.7 9.8 %collective-permute-start.15 = (bf16[4,480,128]{2,1,0:T(8,128)(2,1)S(1)}, bf16[4,480,128]{2,1,0:T(8,128)(2,1)S(1)}, u32[]{:S(2)}, u32[]{:S(2)}) collective-permute-start(bf16[4,480,128]{2,1,0:T(8,128)(2,1)S(1)} %collective-permute-done.13.far1_ref), channel_id=1, source_target_pairs={{0,48},{16,0},{32,16},{48,32},{1,49},{17,1},{33,17},{49,33},{2,50}... | collective-permute-start | bytes 1474568 | tf_op jit(solution)/shard_map/gather/ppermute | solution.py:310
  94.5 7.0 %collective-permute-start.17 = (bf16[2,496,128]{2,1,0:T(8,128)(2,1)S(1)}, bf16[2,496,128]{2,1,0:T(8,128)(2,1)S(1)}, u32[]{:S(2)}, u32[]{:S(2)}) collective-permute-start(bf16[2,496,128]{2,1,0:T(8,128)(2,1)S(1)} %slice.16), channel_id=1, source_target_pairs={{0,2},{2,4},{4,6},{6,8},{8,10},{10,12},{12,14},{14,0},{1,3},{3,5},... | collective-permute-start | bytes 761864 | tf_op jit(solution)/shard_map/gather/ppermute | solution.py:310
  94.6 6.9 %collective-permute-start.18 = (bf16[2,496,128]{2,1,0:T(8,128)(2,1)S(1)}, bf16[2,496,128]{2,1,0:T(8,128)(2,1)S(1)}, u32[]{:S(2)}, u32[]{:S(2)}) collective-permute-start(bf16[2,496,128]{2,1,0:T(8,128)(2,1)S(1)} %slice.17), channel_id=1, source_target_pairs={{0,14},{2,0},{4,2},{6,4},{8,6},{10,8},{12,10},{14,12},{1,15},{3,1}... | collective-permute-start | bytes 761864 | tf_op jit(solution)/shard_map/gather/ppermute | solution.py:310
  103.5 8.4 %collective-permute-start.19 = (bf16[320,224]{1,0:T(8,128)(2,1)S(1)}, bf16[320,224]{1,0:T(8,128)(2,1)S(1)}, u32[]{:S(2)}, u32[]{:S(2)}) collective-permute-start(bf16[320,224]{1,0:T(8,128)(2,1)S(1)} %get-tuple-element.78), channel_id=1, source_target_pairs={{0,1},{1,0},{2,3},{3,2},{4,5},{5,4},{6,7},{7,6},{8,9},{9,8},{10,11... | collective-permute-start | bytes 430088 | tf_op jit(solution)/shard_map/act/ppermute | solution.py:310
  118.8 30.3 %all-to-all-start.2 = ((bf16[8,4,112,128]{3,2,1,0:T(8,128)(2,1)}), bf16[8,4,112,128]{3,2,1,0:T(8,128)(2,1)S(1)}, u32[]{:S(2)}, u32[]{:S(2)}) async-start(bf16[8,4,112,128]{3,2,1,0:T(8,128)(2,1)} %get-tuple-element.79), calls=%async_computation.2 | async-start | bytes 1835008 | tf_op jit(solution)/shard_map/scatter/all_to_all | solution.py:399
  125.0 8.9 %collective-permute-start.20 = (bf16[8,224,128]{2,1,0:T(8,128)(2,1)S(1)}, bf16[8,224,128]{2,1,0:T(8,128)(2,1)S(1)}, u32[]{:S(2)}, u32[]{:S(2)}) collective-permute-start(bf16[8,224,128]{2,1,0:T(8,128)(2,1)S(1)} %get-tuple-element.81), channel_id=1, source_target_pairs={{0,32},{16,48},{32,0},{48,16},{1,33},{17,49},{33,1},{49,17},{2,34}... | collective-permute-start | bytes 1376264 | tf_op jit(solution)/shard_map/scatter/ppermute | solution.py:310
  127.9 19.1 %collective-permute-start.21 = (bf16[8,224,128]{2,1,0:T(8,128)(2,1)S(1)}, bf16[8,224,128]{2,1,0:T(8,128)(2,1)S(1)}, u32[]{:S(2)}, u32[]{:S(2)}) collective-permute-start(bf16[8,224,128]{2,1,0:T(8,128)(2,1)S(1)} %get-tuple-element.82), channel_id=1, source_target_pairs={{0,16},{16,32},{32,48},{48,0},{1,17},{17,33},{33,49},{49,1},{2,18}... | collective-permute-start | bytes 1376264 | tf_op jit(solution)/shard_map/scatter/ppermute | solution.py:310
  128.3 18.7 %collective-permute-start.22 = (bf16[8,224,128]{2,1,0:T(8,128)(2,1)S(1)}, bf16[8,224,128]{2,1,0:T(8,128)(2,1)S(1)}, u32[]{:S(2)}, u32[]{:S(2)}) collective-permute-start(bf16[8,224,128]{2,1,0:T(8,128)(2,1)S(1)} %get-tuple-element.83), channel_id=1, source_target_pairs={{0,48},{16,0},{32,16},{48,32},{1,49},{17,1},{33,17},{49,33},{2,50}... | collective-permute-start | bytes 1376264 | tf_op jit(solution)/shard_map/scatter/ppermute | solution.py:310
  149.1 18.7 %all-to-all-start.3 = ((bf16[8,224,128]{2,1,0:T(8,128)(2,1)}), bf16[8,224,128]{2,1,0:T(8,128)(2,1)S(1)}, u32[]{:S(2)}, u32[]{:S(2)}) async-start(bf16[8,224,128]{2,1,0:T(8,128)(2,1)} %scatter.2), calls=%async_computation.3 | async-start | bytes 917504 | tf_op jit(solution)/shard_map/scatter/all_to_all | solution.py:404
  (15 other events, 86.1 us)

commit v7 on v6

--- a/solution.py
+++ b/solution.py
@@ -18,7 +18,7 @@
 GAIN_ROWS = 16
 MINE = CAP // 2
 XROWS = HALF + GAIN_ROWS
-SPLIT = 144
+SPLIT = 96
 PADDED = 384
 ZFIRST = 112
 YFIRST = HALF - ZFIRST
@@ -334,11 +334,10 @@
             ids, probs, x_t, grad_t, gain_row
         )
         got = lax.all_to_all(routed.reshape(2 * GROUPS, CAP, LANES), LINE, 0, 0, tiled=True)
+        got, own_wg = lax.optimization_barrier((got, wg))
         copies, piece_b = call(
             assemble_kernel, [((NZ, XROWS + SPLIT, LANES), BF16), ((ROWS - SPLIT, LANES), BF16)], 2
         )(got.reshape(GROUPS, 2, CAP, LANES))
-
-        piece_b, own_wg = lax.optimization_barrier((piece_b, wg))
 
     with jax.named_scope("weights"):
         wgp = shift(own_wg, "kv", 1)
@@ -354,11 +353,11 @@
         def meet(step, right, left, got):
             nonlocal line_a, wgp, state
             if step == 2:
-                right, left, line_a = lax.optimization_barrier((right, left, line_a))
+                right, left, line_a, wgp = lax.optimization_barrier((right, left, line_a, wgp))
                 near[:] = [shift(line_a[: NZ // 2], "tensor_0", by) for by in (1, -1)]
                 far[:] = [shift(line_a[NZ // 2 :], "tensor_0", by) for by in (1, -1)]
             if step == 3:
-                right, left, wgp, *near[:] = lax.optimization_barrier((right, left, wgp, *near))
+                right, left, *near[:] = lax.optimization_barrier((right, left, *near))
                 early = [got[b] for b in (0, 1, 2, 6, 7)]
                 state = [*call(place_first_kernel, placed, 5)(line_a, near[1], near[0], *early)]
             if step == 4:
@@ -372,6 +371,7 @@
             *state, far[1], far[0], b_got[3], b_got[5]
         )
     with jax.named_scope("act"):
+        wd, wup = lax.optimization_barrier((wd, wup))
         _, act, theirs = call(
             act_kernel,
             [placed[1], ((HALF, hidden), F32), ((HALF, hidden), BF16)],

time: 183 us -> 190 us (1.038)
  waiting for transfers between devices: 67.5 us -> 74.2 us
    ppermute x26, waiting for transfers between devices: 62.6 us -> 67.3 us  [shift(): return lax.ppermute(value, axis, [(i, (i + by) % n) for i in range(n)])]
    all_to_all x1, waiting for transfers between devices: 4.87 us -> 6.91 us  [shards(): low = lax.all_to_all(low, 'tensor_1', 0, 0, tiled=True)]
  transfers between devices with their start and end apart: 29 -> 29, of which waited for: 13 -> 14; matrix products, arithmetic and copies ran while one was open for 0% -> 0% of each run, Pallas kernels for 6% -> 6%
where the time goes in v7:
time: 190 us; the launch traced here: 189 us
  waiting for transfers between devices  74.2 us (39%)
  starting transfers between devices  60.5 us (32%)
  blocking collectives  28.5 us (15%)
  Pallas kernels  22 us (12%)
  local copies, waits for them, and re-layouts  3.76 us (2%)
    ppermute x26, waiting for transfers between devices, shift(): return lax.ppermute(value, axis, [(i, (i + by) % n) for i in range(n)])  67.3 us
    ppermute x26, starting transfers between devices, shift(): return lax.ppermute(value, axis, [(i, (i + by) % n) for i in range(n)])  41.6 us
    pallas_call x11, Pallas kernels, run(): pl.pallas_call(kernel, in_specs=[here] * len(arrays), out_specs=[here] *...  22 us
    all_to_all x1, blocking collectives, shards(): got = lax.all_to_all(pieces, LINE, 0, 0, tiled=True)  14.3 us
    all_to_all x1, blocking collectives, shards(): lax.all_to_all(routed.reshape(2 * GROUPS, CAP, LANES), LINE, 0, 0, tiled=...  14.1 us
    all_to_all x1, starting transfers between devices, shards(): line_a = lax.all_to_all(copies, 'tensor_1', 0, 0, tiled=True)  7.41 us
    all_to_all x1, waiting for transfers between devices, shards(): low = lax.all_to_all(low, 'tensor_1', 0, 0, tiled=True)  6.91 us
    all_to_all x1, starting transfers between devices, shards(): low = lax.all_to_all(low, 'tensor_1', 0, 0, tiled=True)  6.38 us
  transfers between devices with their start and end apart: 29, of which 14 were waited for; matrix products, arithmetic and copies ran while one was open for 0% of the time, Pallas kernels for 6%

profile of v7, /device:TPU:1, one launch (start us, length us, event | category | flops | bytes accessed | tf_op | source)
XLA Modules:
  0.0 189.2 jit_solution(9755835121095889662)
XLA Ops:
  2.2 14.1 %all_to_all.25 = bf16[8,160,128]{2,1,0:T(8,128)(2,1)S(1)} all-to-all(bf16[8,160,128]{2,1,0:T(8,128)(2,1)} %bitcast.30), channel_id=1, replica_groups=mesh['expert'=4,'tensor_0'=4,'tensor_1'=8,'kv'=2] {'expert','kv'}, dimensions={0} | all-to-all | bytes 655360 | tf_op jit(solution)/shard_map/dispatch/all_to_all | solution.py:336
  18.2 7.4 %all-to-all-start.1 = ((bf16[8,432,128]{2,1,0:T(8,128)(2,1)}), bf16[8,432,128]{2,1,0:T(8,128)(2,1)S(1)}, u32[]{:S(2)}, u32[]{:S(2)}) async-start(bf16[8,432,128]{2,1,0:T(8,128)(2,1)} %get-tuple-element.53), calls=%async_computation.1 | async-start | bytes 1769472 | tf_op jit(solution)/shard_map/gather/all_to_all | solution.py:345
  25.7 2.9 %collective-permute-start.1 = (bf16[544,128]{1,0:T(8,128)(2,1)S(1)}, bf16[544,128]{1,0:T(8,128)(2,1)S(1)}, u32[]{:S(2)}, u32[]{:S(2)}) collective-permute-start(bf16[544,128]{1,0:T(8,128)(2,1)S(1)} %get-tuple-element.51), channel_id=1, source_target_pairs={{0,32},{16,48},{32,0},{48,16},{1,33},{17,49},{33,1},{49,17},{2,34}... | collective-permute-start | bytes 417800 | tf_op jit(solution)/shard_map/gather/ppermute | solution.py:310
  31.5 4.0 %collective-permute-done.2 = bf16[544,128]{1,0:T(8,128)(2,1)S(1)} collective-permute-done((bf16[544,128]{1,0:T(8,128)(2,1)S(1)}, bf16[544,128]{1,0:T(8,128)(2,1)S(1)}, u32[]{:S(2)}, u32[]{:S(2)}) %collective-permute-start.2) | collective-permute-done | bytes 139296 | tf_op jit(solution)/shard_map/gather/ppermute | solution.py:310
  40.4 19.3 %collective-permute-done.3.b7 = bf16[4,544,128]{2,1,0:T(8,128)(2,1)S(1)} collective-permute-done((bf16[4,544,128]{2,1,0:T(8,128)(2,1)S(1)}, bf16[4,544,128]{2,1,0:T(8,128)(2,1)S(1)}, u32[]{:S(2)}, u32[]{:S(2)}) %collective-permute-start.3) | collective-permute-done | bytes 557088 | tf_op jit(solution)/shard_map/gather/ppermute | solution.py:310
  60.6 3.3 %collective-permute-start.7 = (bf16[4,544,128]{2,1,0:T(8,128)(2,1)}, bf16[4,544,128]{2,1,0:T(8,128)(2,1)S(1)}, u32[]{:S(2)}, u32[]{:S(2)}) collective-permute-start(bf16[4,544,128]{2,1,0:T(8,128)(2,1)} %collective-permute-done.4.b1), channel_id=1, source_target_pairs={{0,14},{2,0},{4,2},{6,4},{8,6},{10,8},{12,10},{14,12},{1,15},{3,1}... | collective-permute-start | bytes 1671176 | tf_op jit(solution)/shard_map/gather/ppermute | solution.py:310
  66.9 7.9 %collective-permute-done.8.near3_ref = bf16[4,432,128]{2,1,0:T(8,128)(2,1)S(1)} collective-permute-done((bf16[4,432,128]{2,1,0:T(8,128)(2,1)S(1)}, bf16[4,432,128]{2,1,0:T(8,128)(2,1)S(1)}, u32[]{:S(2)}, u32[]{:S(2)}) %collective-permute-start.8) | collective-permute-done | bytes 442400 | tf_op jit(solution)/shard_map/gather/ppermute | solution.py:310
  75.1 2.7 %collective-permute-start.11 = (bf16[4,544,128]{2,1,0:T(8,128)(2,1)S(1)}, bf16[4,544,128]{2,1,0:T(8,128)(2,1)S(1)}, u32[]{:S(2)}, u32[]{:S(2)}) collective-permute-start(bf16[4,544,128]{2,1,0:T(8,128)(2,1)S(1)} %collective-permute-done.7.b2), channel_id=1, source_target_pairs={{0,14},{2,0},{4,2},{6,4},{8,6},{10,8},{12,10},{14,12},{1,15},{3,1}... | collective-permute-start | bytes 1671176 | tf_op jit(solution)/shard_map/gather/ppermute | solution.py:310
  81.6 2.3 %gather.1 = (bf16[320,4096]{1,0:T(8,128)(2,1)S(1)}, bf16[640,4096]{1,0:T(8,128)(2,1)S(1)}, f32[320,128]{1,0:T(8,128)S(1)}) custom-call(bf16[8,432,128]{2,1,0:T(8,128)(2,1)S(1)} %all-to-all-done.1.line_ref, bf16[4,432,128]{2,1,0:T(8,128)(2,1)S(1)} %collective-permute-done.9.near1_ref, bf16[4,432,128]{2,1,0:T(8,128)(2,1)S(1)} %collective-permute-done.8.near3_ref, ...), custom_call_target="tpu_custom_call" | custom-call | flops 5000000000 | tf_op jit(solution)/shard_map/gather/pallas_call | solution.py:38
  84.0 3.5 %collective-permute-done.12.far3_ref = bf16[4,432,128]{2,1,0:T(8,128)(2,1)S(1)} collective-permute-done((bf16[4,432,128]{2,1,0:T(8,128)(2,1)S(1)}, bf16[4,432,128]{2,1,0:T(8,128)(2,1)S(1)}, u32[]{:S(2)}, u32[]{:S(2)}) %collective-permute-start.12) | collective-permute-done | bytes 442400 | tf_op jit(solution)/shard_map/gather/ppermute | solution.py:310
  87.7 2.8 %collective-permute-start.15 = (bf16[4,432,128]{2,1,0:T(8,128)(2,1)S(1)}, bf16[4,432,128]{2,1,0:T(8,128)(2,1)S(1)}, u32[]{:S(2)}, u32[]{:S(2)}) collective-permute-start(bf16[4,432,128]{2,1,0:T(8,128)(2,1)S(1)} %collective-permute-done.13.far1_ref), channel_id=1, source_target_pairs={{0,48},{16,0},{32,16},{48,32},{1,49},{17,1},{33,17},{49,33},{2,50}... | collective-permute-start | bytes 1327112 | tf_op jit(solution)/shard_map/gather/ppermute | solution.py:310
  90.5 8.0 %collective-permute-done.16.refs_7_.refs_9_ = bf16[224,4096]{1,0:T(8,128)(2,1)} collective-permute-done((bf16[224,4096]{1,0:T(8,128)(2,1)}, bf16[224,4096]{1,0:T(8,128)(2,1)}, u32[]{:S(2)}, u32[]{:S(2)}) %collective-permute-start.16) | collective-permute-done | bytes 1835040 | tf_op jit(solution)/shard_map/gather/ppermute | solution.py:310
  99.4 4.0 %collective-permute-start.18 = (bf16[2,544,128]{2,1,0:T(8,128)(2,1)S(1)}, bf16[2,544,128]{2,1,0:T(8,128)(2,1)S(1)}, u32[]{:S(2)}, u32[]{:S(2)}) collective-permute-start(bf16[2,544,128]{2,1,0:T(8,128)(2,1)S(1)} %slice.17), channel_id=1, source_target_pairs={{0,14},{2,0},{4,2},{6,4},{8,6},{10,8},{12,10},{14,12},{1,15},{3,1}... | collective-permute-start | bytes 835592 | tf_op jit(solution)/shard_map/gather/ppermute | solution.py:310
  104.2 4.9 %collective-permute-done.17.b4lo_ref = bf16[2,544,128]{2,1,0:T(8,128)(2,1)S(1)} collective-permute-done((bf16[2,544,128]{2,1,0:T(8,128)(2,1)S(1)}, bf16[2,544,128]{2,1,0:T(8,128)(2,1)S(1)}, u32[]{:S(2)}, u32[]{:S(2)}) %collective-permute-start.17) | collective-permute-done | bytes 278560 | tf_op jit(solution)/shard_map/gather/ppermute | solution.py:310
  111.2 5.3 %forward.1 = (bf16[320,4096]{1,0:T(8,128)(2,1)S(1)}, f32[320,128]{1,0:T(8,128)S(1)}, f32[320,224]{1,0:T(8,128)S(1)}, f32[320,224]{1,0:T(8,128)S(1)}, f32[320,224...) custom-call(bf16[320,4096]{1,0:T(8,128)(2,1)S(1)} %get-tuple-element, ...), custom_call_target="tpu_custom_call", output_to_operand_aliasing={{0}: (0, {}), {1}: (1, {})} | custom-call | flops 5000000000 | tf_op jit(solution)/shard_map/forward/pallas_call | solution.py:38
  116.9 6.0 %back.1 = (bf16[8,4,112,128]{3,2,1,0:T(8,128)(2,1)}, bf16[8,224,128]{2,1,0:T(8,128)(2,1)S(1)}, bf16[8,224,128]{2,1,0:T(8,128)(2,1)S(1)}, bf16[8,224,128]{2,1,0:T(8,128)(2,1)S(1)}, bf16[8,224,128]{2,1,0:T(8,128)(2,1)S(1)}) custom-call(f32[320,224]{1,0:T(8,128)S(1)} %get-tuple-element.73.refs_0_, f32[320,224]{1,0:T(8,128)S(1)} %get-tuple-element.74.refs_1_, ...), custom_call_target="tpu_custom_call" | custom-call | flops 8000000000 | tf_op jit(solution)/shard_map/back/pallas_call | solution.py:38
  123.7 5.1 %all-to-all-start.2 = ((bf16[8,4,112,128]{3,2,1,0:T(8,128)(2,1)}), bf16[8,4,112,128]{3,2,1,0:T(8,128)(2,1)S(1)}, u32[]{:S(2)}, u32[]{:S(2)}) async-start(bf16[8,4,112,128]{3,2,1,0:T(8,128)(2,1)} %get-tuple-element.83), calls=%async_computation.2 | async-start | bytes 1835008 | tf_op jit(solution)/shard_map/scatter/all_to_all | solution.py:399
  128.8 2.9 %collective-permute-start.20 = (bf16[8,224,128]{2,1,0:T(8,128)(2,1)S(1)}, bf16[8,224,128]{2,1,0:T(8,128)(2,1)S(1)}, u32[]{:S(2)}, u32[]{:S(2)}) collective-permute-start(bf16[8,224,128]{2,1,0:T(8,128)(2,1)S(1)} %get-tuple-element.85), channel_id=1, source_target_pairs={{0,32},{16,48},{32,0},{48,16},{1,33},{17,49},{33,1},{49,17},{2,34}... | collective-permute-start | bytes 1376264 | tf_op jit(solution)/shard_map/scatter/ppermute | solution.py:310
  134.4 4.1 %collective-permute-done.20.refs_1_ = bf16[8,224,128]{2,1,0:T(8,128)(2,1)S(1)} collective-permute-done((bf16[8,224,128]{2,1,0:T(8,128)(2,1)S(1)}, bf16[8,224,128]{2,1,0:T(8,128)(2,1)S(1)}, u32[]{:S(2)}, u32[]{:S(2)}) %collective-permute-start.20) | collective-permute-done | bytes 458784 | tf_op jit(solution)/shard_map/scatter/ppermute | solution.py:310
  138.5 13.2 %collective-permute-done.21.refs_2_ = bf16[8,224,128]{2,1,0:T(8,128)(2,1)S(1)} collective-permute-done((bf16[8,224,128]{2,1,0:T(8,128)(2,1)S(1)}, bf16[8,224,128]{2,1,0:T(8,128)(2,1)S(1)}, u32[]{:S(2)}, u32[]{:S(2)}) %collective-permute-start.21) | collective-permute-done | bytes 458784 | tf_op jit(solution)/shard_map/scatter/ppermute | solution.py:310
  153.7 6.4 %all-to-all-start.3 = ((bf16[8,224,128]{2,1,0:T(8,128)(2,1)}), bf16[8,224,128]{2,1,0:T(8,128)(2,1)S(1)}, u32[]{:S(2)}, u32[]{:S(2)}) async-start(bf16[8,224,128]{2,1,0:T(8,128)(2,1)} %scatter.2), calls=%async_computation.3 | async-start | bytes 917504 | tf_op jit(solution)/shard_map/scatter/all_to_all | solution.py:404
  160.2 2.5 %collective-permute-start.23 = (bf16[112,128]{1,0:T(8,128)(2,1)S(1)}, bf16[112,128]{1,0:T(8,128)(2,1)S(1)}, u32[]{:S(2)}, u32[]{:S(2)}) collective-permute-start(bf16[112,128]{1,0:T(8,128)(2,1)S(1)} %get-tuple-element.90), channel_id=1, source_target_pairs={{0,32},{16,48},{32,0},{48,16},{1,33},{17,49},{33,1},{49,17},{2,34}... | collective-permute-start | bytes 86024 | tf_op jit(solution)/shard_map/scatter/ppermute | solution.py:310
  166.7 6.9 %all-to-all-done.3.refs_4_ = bf16[8,224,128]{2,1,0:T(8,128)(2,1)S(1)} async-done(((bf16[8,224,128]{2,1,0:T(8,128)(2,1)}), bf16[8,224,128]{2,1,0:T(8,128)(2,1)S(1)}, u32[]{:S(2)}, u32[]{:S(2)}) %all-to-all-start.3) | async-done | bytes 458784 | tf_op jit(solution)/shard_map/scatter/all_to_all | solution.py:404
  173.7 14.3 %all_to_all.26.got_ref = bf16[8,96,128]{2,1,0:T(8,128)(2,1)S(1)} all-to-all(bf16[8,96,128]{2,1,0:T(8,128)(2,1)S(1)} %combine.2), channel_id=1, replica_groups=mesh['expert'=4,'tensor_0'=4,'tensor_1'=8,'kv'=2] {'expert','kv'}, dimensions={0} | all-to-all | bytes 393216 | tf_op jit(solution)/shard_map/combine/all_to_all | solution.py:409
  (71 shorter events, 34.9 us)
Async XLA Ops:
  16.3 44.2 %collective-permute-start.5 = (bf16[224,4096]{1,0:T(8,128)(2,1)S(1)}, bf16[224,4096]{1,0:T(8,128)(2,1)}, u32[]{:S(2)}, u32[]{:S(2)}) collective-permute-start(bf16[224,4096]{1,0:T(8,128)(2,1)S(1)} %bitcast.18), channel_id=1, source_target_pairs={{0,1},{1,0},{2,3},{3,2},{4,5},{5,4},{6,7},{7,6},{8,9},{9,8},{10,11... | collective-permute-start | bytes 5505032 | tf_op jit(solution)/shard_map/weights/ppermute | solution.py:310
  18.2 42.3 %all-to-all-start.1 = ((bf16[8,432,128]{2,1,0:T(8,128)(2,1)}), bf16[8,432,128]{2,1,0:T(8,128)(2,1)S(1)}, u32[]{:S(2)}, u32[]{:S(2)}) async-start(bf16[8,432,128]{2,1,0:T(8,128)(2,1)} %get-tuple-element.53), calls=%async_computation.1 | async-start | bytes 1769472 | tf_op jit(solution)/shard_map/gather/all_to_all | solution.py:345
  28.6 6.9 %collective-permute-start.2 = (bf16[544,128]{1,0:T(8,128)(2,1)S(1)}, bf16[544,128]{1,0:T(8,128)(2,1)S(1)}, u32[]{:S(2)}, u32[]{:S(2)}) collective-permute-start(bf16[544,128]{1,0:T(8,128)(2,1)S(1)} %get-tuple-element.51), channel_id=1, source_target_pairs={{0,16},{16,32},{32,48},{48,0},{1,17},{17,33},{33,49},{49,1},{2,18}... | collective-permute-start | bytes 417800 | tf_op jit(solution)/shard_map/gather/ppermute | solution.py:310
  29.0 6.5 %collective-permute-start = (bf16[544,128]{1,0:T(8,128)(2,1)S(1)}, bf16[544,128]{1,0:T(8,128)(2,1)S(1)}, u32[]{:S(2)}, u32[]{:S(2)}) collective-permute-start(bf16[544,128]{1,0:T(8,128)(2,1)S(1)} %get-tuple-element.51), channel_id=1, source_target_pairs={{0,48},{16,0},{32,16},{48,32},{1,49},{17,1},{33,17},{49,33},{2,50}... | collective-permute-start | bytes 417800 | tf_op jit(solution)/shard_map/gather/ppermute | solution.py:310
  35.5 24.2 %collective-permute-start.3 = (bf16[4,544,128]{2,1,0:T(8,128)(2,1)S(1)}, bf16[4,544,128]{2,1,0:T(8,128)(2,1)S(1)}, u32[]{:S(2)}, u32[]{:S(2)}) collective-permute-start(bf16[4,544,128]{2,1,0:T(8,128)(2,1)S(1)} %pad_maximum_fusion.b0), channel_id=1, source_target_pairs={{0,2},{2,4},{4,6},{6,8},{8,10},{10,12},{12,14},{14,0},{1,3},{3,5},... | collective-permute-start | bytes 1671176 | tf_op jit(solution)/shard_map/gather/ppermute | solution.py:310
  37.2 23.3 %collective-permute-start.4 = (bf16[4,544,128]{2,1,0:T(8,128)(2,1)S(1)}, bf16[4,544,128]{2,1,0:T(8,128)(2,1)}, u32[]{:S(2)}, u32[]{:S(2)}) collective-permute-start(bf16[4,544,128]{2,1,0:T(8,128)(2,1)S(1)} %pad_maximum_fusion.b0), channel_id=1, source_target_pairs={{0,14},{2,0},{4,2},{6,4},{8,6},{10,8},{12,10},{14,12},{1,15},{3,1}... | collective-permute-start | bytes 1671176 | tf_op jit(solution)/shard_map/gather/ppermute | solution.py:310
  38.5 60.0 %collective-permute-start.16 = (bf16[224,4096]{1,0:T(8,128)(2,1)}, bf16[224,4096]{1,0:T(8,128)(2,1)}, u32[]{:S(2)}, u32[]{:S(2)}) collective-permute-start(bf16[224,4096]{1,0:T(8,128)(2,1)} %bitcast.21), channel_id=1, source_target_pairs={{0,1},{1,0},{2,3},{3,2},{4,5},{5,4},{6,7},{7,6},{8,9},{9,8},{10,11... | collective-permute-start | bytes 5505032 | tf_op jit(solution)/shard_map/gather/ppermute | solution.py:310
  60.5 14.6 %collective-permute-start.6 = (bf16[4,544,128]{2,1,0:T(8,128)(2,1)}, bf16[4,544,128]{2,1,0:T(8,128)(2,1)S(1)}, u32[]{:S(2)}, u32[]{:S(2)}) collective-permute-start(bf16[4,544,128]{2,1,0:T(8,128)(2,1)} %copy-done.3), channel_id=1, source_target_pairs={{0,2},{2,4},{4,6},{6,8},{8,10},{10,12},{12,14},{14,0},{1,3},{3,5},... | collective-permute-start | bytes 1671176 | tf_op jit(solution)/shard_map/gather/ppermute | solution.py:310
  60.6 14.5 %collective-permute-start.7 = (bf16[4,544,128]{2,1,0:T(8,128)(2,1)}, bf16[4,544,128]{2,1,0:T(8,128)(2,1)S(1)}, u32[]{:S(2)}, u32[]{:S(2)}) collective-permute-start(bf16[4,544,128]{2,1,0:T(8,128)(2,1)} %collective-permute-done.4.b1), channel_id=1, source_target_pairs={{0,14},{2,0},{4,2},{6,4},{8,6},{10,8},{12,10},{14,12},{1,15},{3,1}... | collective-permute-start | bytes 1671176 | tf_op jit(solution)/shard_map/gather/ppermute | solution.py:310
  64.0 10.9 %collective-permute-start.8 = (bf16[4,432,128]{2,1,0:T(8,128)(2,1)S(1)}, bf16[4,432,128]{2,1,0:T(8,128)(2,1)S(1)}, u32[]{:S(2)}, u32[]{:S(2)}) collective-permute-start(bf16[4,432,128]{2,1,0:T(8,128)(2,1)S(1)} %get-tuple-element.96), channel_id=1, source_target_pairs={{0,16},{16,32},{32,48},{48,0},{1,17},{17,33},{33,49},{49,1},{2,18}... | collective-permute-start | bytes 1327112 | tf_op jit(solution)/shard_map/gather/ppermute | solution.py:310
  65.4 9.5 %collective-permute-start.9 = (bf16[4,432,128]{2,1,0:T(8,128)(2,1)S(1)}, bf16[4,432,128]{2,1,0:T(8,128)(2,1)S(1)}, u32[]{:S(2)}, u32[]{:S(2)}) collective-permute-start(bf16[4,432,128]{2,1,0:T(8,128)(2,1)S(1)} %get-tuple-element.96), channel_id=1, source_target_pairs={{0,48},{16,0},{32,16},{48,32},{1,49},{17,1},{33,17},{49,33},{2,50}... | collective-permute-start | bytes 1327112 | tf_op jit(solution)/shard_map/gather/ppermute | solution.py:310
  75.1 12.5 %collective-permute-start.10 = (bf16[4,544,128]{2,1,0:T(8,128)(2,1)S(1)}, bf16[4,544,128]{2,1,0:T(8,128)(2,1)S(1)}, u32[]{:S(2)}, u32[]{:S(2)}) collective-permute-start(bf16[4,544,128]{2,1,0:T(8,128)(2,1)S(1)} %collective-permute-done.6.b6), channel_id=1, source_target_pairs={{0,2},{2,4},{4,6},{6,8},{8,10},{10,12},{12,14},{14,0},{1,3},{3,5},... | collective-permute-start | bytes 1671176 | tf_op jit(solution)/shard_map/gather/ppermute | solution.py:310
  75.1 12.5 %collective-permute-start.11 = (bf16[4,544,128]{2,1,0:T(8,128)(2,1)S(1)}, bf16[4,544,128]{2,1,0:T(8,128)(2,1)S(1)}, u32[]{:S(2)}, u32[]{:S(2)}) collective-permute-start(bf16[4,544,128]{2,1,0:T(8,128)(2,1)S(1)} %collective-permute-done.7.b2), channel_id=1, source_target_pairs={{0,14},{2,0},{4,2},{6,4},{8,6},{10,8},{12,10},{14,12},{1,15},{3,1}... | collective-permute-start | bytes 1671176 | tf_op jit(solution)/shard_map/gather/ppermute | solution.py:310
  77.8 9.6 %collective-permute-start.12 = (bf16[4,432,128]{2,1,0:T(8,128)(2,1)S(1)}, bf16[4,432,128]{2,1,0:T(8,128)(2,1)S(1)}, u32[]{:S(2)}, u32[]{:S(2)}) collective-permute-start(bf16[4,432,128]{2,1,0:T(8,128)(2,1)S(1)} %get-tuple-element.95), channel_id=1, source_target_pairs={{0,16},{16,32},{32,48},{48,0},{1,17},{17,33},{33,49},{49,1},{2,18}... | collective-permute-start | bytes 1327112 | tf_op jit(solution)/shard_map/gather/ppermute | solution.py:310
  79.1 8.4 %collective-permute-start.13 = (bf16[4,432,128]{2,1,0:T(8,128)(2,1)S(1)}, bf16[4,432,128]{2,1,0:T(8,128)(2,1)S(1)}, u32[]{:S(2)}, u32[]{:S(2)}) collective-permute-start(bf16[4,432,128]{2,1,0:T(8,128)(2,1)S(1)} %get-tuple-element.95), channel_id=1, source_target_pairs={{0,48},{16,0},{32,16},{48,32},{1,49},{17,1},{33,17},{49,33},{2,50}... | collective-permute-start | bytes 1327112 | tf_op jit(solution)/shard_map/gather/ppermute | solution.py:310
  87.4 16.7 %collective-permute-start.14 = (bf16[4,432,128]{2,1,0:T(8,128)(2,1)S(1)}, bf16[4,432,128]{2,1,0:T(8,128)(2,1)S(1)}, u32[]{:S(2)}, u32[]{:S(2)}) collective-permute-start(bf16[4,432,128]{2,1,0:T(8,128)(2,1)S(1)} %collective-permute-done.8.near3_ref), channel_id=1, source_target_pairs={{0,16},{16,32},{32,48},{48,0},{1,17},{17,33},{33,49},{49,1},{2,18}... | collective-permute-start | bytes 1327112 | tf_op jit(solution)/shard_map/gather/ppermute | solution.py:310
  87.7 21.4 %collective-permute-start.15 = (bf16[4,432,128]{2,1,0:T(8,128)(2,1)S(1)}, bf16[4,432,128]{2,1,0:T(8,128)(2,1)S(1)}, u32[]{:S(2)}, u32[]{:S(2)}) collective-permute-start(bf16[4,432,128]{2,1,0:T(8,128)(2,1)S(1)} %collective-permute-done.13.far1_ref), channel_id=1, source_target_pairs={{0,48},{16,0},{32,16},{48,32},{1,49},{17,1},{33,17},{49,33},{2,50}... | collective-permute-start | bytes 1327112 | tf_op jit(solution)/shard_map/gather/ppermute | solution.py:310
  98.5 10.6 %collective-permute-start.17 = (bf16[2,544,128]{2,1,0:T(8,128)(2,1)S(1)}, bf16[2,544,128]{2,1,0:T(8,128)(2,1)S(1)}, u32[]{:S(2)}, u32[]{:S(2)}) collective-permute-start(bf16[2,544,128]{2,1,0:T(8,128)(2,1)S(1)} %slice.16), channel_id=1, source_target_pairs={{0,2},{2,4},{4,6},{6,8},{8,10},{10,12},{12,14},{14,0},{1,3},{3,5},... | collective-permute-start | bytes 835592 | tf_op jit(solution)/shard_map/gather/ppermute | solution.py:310
  99.4 9.7 %collective-permute-start.18 = (bf16[2,544,128]{2,1,0:T(8,128)(2,1)S(1)}, bf16[2,544,128]{2,1,0:T(8,128)(2,1)S(1)}, u32[]{:S(2)}, u32[]{:S(2)}) collective-permute-start(bf16[2,544,128]{2,1,0:T(8,128)(2,1)S(1)} %slice.17), channel_id=1, source_target_pairs={{0,14},{2,0},{4,2},{6,4},{8,6},{10,8},{12,10},{14,12},{1,15},{3,1}... | collective-permute-start | bytes 835592 | tf_op jit(solution)/shard_map/gather/ppermute | solution.py:310
  123.7 30.0 %all-to-all-start.2 = ((bf16[8,4,112,128]{3,2,1,0:T(8,128)(2,1)}), bf16[8,4,112,128]{3,2,1,0:T(8,128)(2,1)S(1)}, u32[]{:S(2)}, u32[]{:S(2)}) async-start(bf16[8,4,112,128]{3,2,1,0:T(8,128)(2,1)} %get-tuple-element.83), calls=%async_computation.2 | async-start | bytes 1835008 | tf_op jit(solution)/shard_map/scatter/all_to_all | solution.py:399
  128.8 9.7 %collective-permute-start.20 = (bf16[8,224,128]{2,1,0:T(8,128)(2,1)S(1)}, bf16[8,224,128]{2,1,0:T(8,128)(2,1)S(1)}, u32[]{:S(2)}, u32[]{:S(2)}) collective-permute-start(bf16[8,224,128]{2,1,0:T(8,128)(2,1)S(1)} %get-tuple-element.85), channel_id=1, source_target_pairs={{0,32},{16,48},{32,0},{48,16},{1,33},{17,49},{33,1},{49,17},{2,34}... | collective-permute-start | bytes 1376264 | tf_op jit(solution)/shard_map/scatter/ppermute | solution.py:310
  131.7 20.0 %collective-permute-start.21 = (bf16[8,224,128]{2,1,0:T(8,128)(2,1)S(1)}, bf16[8,224,128]{2,1,0:T(8,128)(2,1)S(1)}, u32[]{:S(2)}, u32[]{:S(2)}) collective-permute-start(bf16[8,224,128]{2,1,0:T(8,128)(2,1)S(1)} %get-tuple-element.86), channel_id=1, source_target_pairs={{0,16},{16,32},{32,48},{48,0},{1,17},{17,33},{33,49},{49,1},{2,18}... | collective-permute-start | bytes 1376264 | tf_op jit(solution)/shard_map/scatter/ppermute | solution.py:310
  132.1 19.6 %collective-permute-start.22 = (bf16[8,224,128]{2,1,0:T(8,128)(2,1)S(1)}, bf16[8,224,128]{2,1,0:T(8,128)(2,1)S(1)}, u32[]{:S(2)}, u32[]{:S(2)}) collective-permute-start(bf16[8,224,128]{2,1,0:T(8,128)(2,1)S(1)} %get-tuple-element.87), channel_id=1, source_target_pairs={{0,48},{16,0},{32,16},{48,32},{1,49},{17,1},{33,17},{49,33},{2,50}... | collective-permute-start | bytes 1376264 | tf_op jit(solution)/shard_map/scatter/ppermute | solution.py:310
  153.7 19.9 %all-to-all-start.3 = ((bf16[8,224,128]{2,1,0:T(8,128)(2,1)}), bf16[8,224,128]{2,1,0:T(8,128)(2,1)S(1)}, u32[]{:S(2)}, u32[]{:S(2)}) async-start(bf16[8,224,128]{2,1,0:T(8,128)(2,1)} %scatter.2), calls=%async_computation.3 | async-start | bytes 917504 | tf_op jit(solution)/shard_map/scatter/all_to_all | solution.py:404
  (15 other events, 95.0 us)

commit v8 on v7

--- a/solution.py
+++ b/solution.py
@@ -371,7 +371,6 @@
             *state, far[1], far[0], b_got[3], b_got[5]
         )
     with jax.named_scope("act"):
-        wd, wup = lax.optimization_barrier((wd, wup))
         _, act, theirs = call(
             act_kernel,
             [placed[1], ((HALF, hidden), F32), ((HALF, hidden), BF16)],

time: 190 us -> 177 us (0.932)
  waiting for transfers between devices: 74.2 us -> 64.2 us
    ppermute x26, waiting for transfers between devices: 67.3 us -> 57.8 us  [shift(): return lax.ppermute(value, axis, [(i, (i + by) % n) for i in range(n)])]
    ppermute x26, starting transfers between devices: 41.6 us -> 39.2 us  [shift(): return lax.ppermute(value, axis, [(i, (i + by) % n) for i in range(n)])]
  transfers between devices with their start and end apart: 29 -> 29, of which waited for: 14 -> 14; matrix products, arithmetic and copies ran while one was open for 0% -> 0% of each run, Pallas kernels for 6% -> 7%
where the time goes in v8:
time: 177 us; the launch traced here: 176 us
  waiting for transfers between devices  64.2 us (36%)
  starting transfers between devices  58.9 us (33%)
  blocking collectives  26.9 us (15%)
  Pallas kernels  22 us (12%)
  local copies, waits for them, and re-layouts  3.76 us (2%)
    ppermute x26, waiting for transfers between devices, shift(): return lax.ppermute(value, axis, [(i, (i + by) % n) for i in range(n)])  57.8 us
    ppermute x26, starting transfers between devices, shift(): return lax.ppermute(value, axis, [(i, (i + by) % n) for i in range(n)])  39.2 us
    pallas_call x11, Pallas kernels, run(): pl.pallas_call(kernel, in_specs=[here] * len(arrays), out_specs=[here] *...  22 us
    all_to_all x1, blocking collectives, shards(): lax.all_to_all(routed.reshape(2 * GROUPS, CAP, LANES), LINE, 0, 0, tiled=...  14.1 us
    all_to_all x1, blocking collectives, shards(): got = lax.all_to_all(pieces, LINE, 0, 0, tiled=True)  12.8 us
    all_to_all x1, starting transfers between devices, shards(): line_a = lax.all_to_all(copies, 'tensor_1', 0, 0, tiled=True)  7.41 us
    all_to_all x1, starting transfers between devices, shards(): low = lax.all_to_all(low, 'tensor_1', 0, 0, tiled=True)  6.37 us
    all_to_all x1, waiting for transfers between devices, shards(): low = lax.all_to_all(low, 'tensor_1', 0, 0, tiled=True)  6.33 us
  transfers between devices with their start and end apart: 29, of which 14 were waited for; matrix products, arithmetic and copies ran while one was open for 0% of the time, Pallas kernels for 7%

profile of v8, /device:TPU:1, one launch (start us, length us, event | category | flops | bytes accessed | tf_op | source)
XLA Modules:
  0.0 175.9 jit_solution(5833475108619073143)
XLA Ops:
  0.0 2.2 %dispatch.2 = bf16[4,2,160,128]{3,2,1,0:T(8,128)(2,1)} custom-call(s32[2,256]{1,0:T(2,128)} %bitcast.26, f32[2,256]{1,0:T(2,128)} %bitcast.35, bf16[64,256]{1,0:T(8,128)(2,1)} %bitcast.24, bf16[64,256]{1,0:T(8,128)(2,1)} %bitcast.34, bf16[1,64]{1,0:T(2,128)(2,1)} %bitcast.28), custom_call_target="tpu_custom_call" | custom-call | flops 2000000000 | tf_op jit(solution)/shard_map/dispatch/pallas_call | solution.py:38
  2.2 14.1 %all_to_all.25 = bf16[8,160,128]{2,1,0:T(8,128)(2,1)S(1)} all-to-all(bf16[8,160,128]{2,1,0:T(8,128)(2,1)} %bitcast.30), channel_id=1, replica_groups=mesh['expert'=4,'tensor_0'=4,'tensor_1'=8,'kv'=2] {'expert','kv'}, dimensions={0} | all-to-all | bytes 655360 | tf_op jit(solution)/shard_map/dispatch/all_to_all | solution.py:336
  18.2 7.4 %all-to-all-start.1 = ((bf16[8,432,128]{2,1,0:T(8,128)(2,1)}), bf16[8,432,128]{2,1,0:T(8,128)(2,1)S(1)}, u32[]{:S(2)}, u32[]{:S(2)}) async-start(bf16[8,432,128]{2,1,0:T(8,128)(2,1)} %get-tuple-element.51), calls=%async_computation.1 | async-start | bytes 1769472 | tf_op jit(solution)/shard_map/gather/all_to_all | solution.py:345
  25.7 2.9 %collective-permute-start.1 = (bf16[544,128]{1,0:T(8,128)(2,1)S(1)}, bf16[544,128]{1,0:T(8,128)(2,1)S(1)}, u32[]{:S(2)}, u32[]{:S(2)}) collective-permute-start(bf16[544,128]{1,0:T(8,128)(2,1)S(1)} %get-tuple-element.49), channel_id=1, source_target_pairs={{0,32},{16,48},{32,0},{48,16},{1,33},{17,49},{33,1},{49,17},{2,34}... | collective-permute-start | bytes 417800 | tf_op jit(solution)/shard_map/gather/ppermute | solution.py:310
  29.0 2.3 %collective-permute-start = (bf16[544,128]{1,0:T(8,128)(2,1)S(1)}, bf16[544,128]{1,0:T(8,128)(2,1)S(1)}, u32[]{:S(2)}, u32[]{:S(2)}) collective-permute-start(bf16[544,128]{1,0:T(8,128)(2,1)S(1)} %get-tuple-element.49), channel_id=1, source_target_pairs={{0,48},{16,0},{32,16},{48,32},{1,49},{17,1},{33,17},{49,33},{2,50}... | collective-permute-start | bytes 417800 | tf_op jit(solution)/shard_map/gather/ppermute | solution.py:310
  31.5 4.0 %collective-permute-done.2 = bf16[544,128]{1,0:T(8,128)(2,1)S(1)} collective-permute-done((bf16[544,128]{1,0:T(8,128)(2,1)S(1)}, bf16[544,128]{1,0:T(8,128)(2,1)S(1)}, u32[]{:S(2)}, u32[]{:S(2)}) %collective-permute-start.2) | collective-permute-done | bytes 139296 | tf_op jit(solution)/shard_map/gather/ppermute | solution.py:310
  40.4 19.3 %collective-permute-done.3.b7 = bf16[4,544,128]{2,1,0:T(8,128)(2,1)S(1)} collective-permute-done((bf16[4,544,128]{2,1,0:T(8,128)(2,1)S(1)}, bf16[4,544,128]{2,1,0:T(8,128)(2,1)S(1)}, u32[]{:S(2)}, u32[]{:S(2)}) %collective-permute-start.3) | collective-permute-done | bytes 557088 | tf_op jit(solution)/shard_map/gather/ppermute | solution.py:310
  60.6 3.3 %collective-permute-start.7 = (bf16[4,544,128]{2,1,0:T(8,128)(2,1)}, bf16[4,544,128]{2,1,0:T(8,128)(2,1)S(1)}, u32[]{:S(2)}, u32[]{:S(2)}) collective-permute-start(bf16[4,544,128]{2,1,0:T(8,128)(2,1)} %collective-permute-done.4.b1), channel_id=1, source_target_pairs={{0,14},{2,0},{4,2},{6,4},{8,6},{10,8},{12,10},{14,12},{1,15},{3,1}... | collective-permute-start | bytes 1671176 | tf_op jit(solution)/shard_map/gather/ppermute | solution.py:310
  66.9 7.9 %collective-permute-done.8.near3_ref = bf16[4,432,128]{2,1,0:T(8,128)(2,1)S(1)} collective-permute-done((bf16[4,432,128]{2,1,0:T(8,128)(2,1)S(1)}, bf16[4,432,128]{2,1,0:T(8,128)(2,1)S(1)}, u32[]{:S(2)}, u32[]{:S(2)}) %collective-permute-start.8) | collective-permute-done | bytes 442400 | tf_op jit(solution)/shard_map/gather/ppermute | solution.py:310
  75.1 2.7 %collective-permute-start.11 = (bf16[4,544,128]{2,1,0:T(8,128)(2,1)S(1)}, bf16[4,544,128]{2,1,0:T(8,128)(2,1)S(1)}, u32[]{:S(2)}, u32[]{:S(2)}) collective-permute-start(bf16[4,544,128]{2,1,0:T(8,128)(2,1)S(1)} %collective-permute-done.7.b2), channel_id=1, source_target_pairs={{0,14},{2,0},{4,2},{6,4},{8,6},{10,8},{12,10},{14,12},{1,15},{3,1}... | collective-permute-start | bytes 1671176 | tf_op jit(solution)/shard_map/gather/ppermute | solution.py:310
  81.6 2.3 %gather.1 = (bf16[320,4096]{1,0:T(8,128)(2,1)S(1)}, bf16[640,4096]{1,0:T(8,128)(2,1)S(1)}, f32[320,128]{1,0:T(8,128)S(1)}) custom-call(bf16[8,432,128]{2,1,0:T(8,128)(2,1)S(1)} %all-to-all-done.1.line_ref, bf16[4,432,128]{2,1,0:T(8,128)(2,1)S(1)} %collective-permute-done.9.near1_ref, bf16[4,432,128]{2,1,0:T(8,128)(2,1)S(1)} %collective-permute-done.8.near3_ref, ...), custom_call_target="tpu_custom_call" | custom-call | flops 5000000000 | tf_op jit(solution)/shard_map/gather/pallas_call | solution.py:38
  84.0 3.5 %collective-permute-done.12.far3_ref = bf16[4,432,128]{2,1,0:T(8,128)(2,1)S(1)} collective-permute-done((bf16[4,432,128]{2,1,0:T(8,128)(2,1)S(1)}, bf16[4,432,128]{2,1,0:T(8,128)(2,1)S(1)}, u32[]{:S(2)}, u32[]{:S(2)}) %collective-permute-start.12) | collective-permute-done | bytes 442400 | tf_op jit(solution)/shard_map/gather/ppermute | solution.py:310
  87.7 2.8 %collective-permute-start.15 = (bf16[4,432,128]{2,1,0:T(8,128)(2,1)S(1)}, bf16[4,432,128]{2,1,0:T(8,128)(2,1)S(1)}, u32[]{:S(2)}, u32[]{:S(2)}) collective-permute-start(bf16[4,432,128]{2,1,0:T(8,128)(2,1)S(1)} %collective-permute-done.13.far1_ref), channel_id=1, source_target_pairs={{0,48},{16,0},{32,16},{48,32},{1,49},{17,1},{33,17},{49,33},{2,50}... | collective-permute-start | bytes 1327112 | tf_op jit(solution)/shard_map/gather/ppermute | solution.py:310
  94.0 2.2 %collective-permute-done.14.refs_2_.lo_ref = bf16[4,432,128]{2,1,0:T(8,128)(2,1)S(1)} collective-permute-done((bf16[4,432,128]{2,1,0:T(8,128)(2,1)S(1)}, bf16[4,432,128]{2,1,0:T(8,128)(2,1)S(1)}, u32[]{:S(2)}, u32[]{:S(2)}) %collective-permute-start.14) | collective-permute-done | bytes 442400 | tf_op jit(solution)/shard_map/gather/ppermute | solution.py:310
  101.1 5.3 %forward.1 = (bf16[320,4096]{1,0:T(8,128)(2,1)S(1)}, f32[320,128]{1,0:T(8,128)S(1)}, f32[320,224]{1,0:T(8,128)S(1)}, f32[320,224]{1,0:T(8,128)S(1)}, f32[320,224...) custom-call(bf16[320,4096]{1,0:T(8,128)(2,1)S(1)} %get-tuple-element, ...), custom_call_target="tpu_custom_call", output_to_operand_aliasing={{0}: (0, {}), {1}: (1, {})} | custom-call | flops 5000000000 | tf_op jit(solution)/shard_map/forward/pallas_call | solution.py:38
  106.5 6.0 %back.1 = (bf16[8,4,112,128]{3,2,1,0:T(8,128)(2,1)}, bf16[8,224,128]{2,1,0:T(8,128)(2,1)S(1)}, bf16[8,224,128]{2,1,0:T(8,128)(2,1)S(1)}, bf16[8,224,128]{2,1,0:T(8,128)(2,1)S(1)}, bf16[8,224,128]{2,1,0:T(8,128)(2,1)S(1)}) custom-call(f32[320,224]{1,0:T(8,128)S(1)} %get-tuple-element.70.refs_0_, f32[320,224]{1,0:T(8,128)S(1)} %get-tuple-element.71.refs_1_, ...), custom_call_target="tpu_custom_call" | custom-call | flops 8000000000 | tf_op jit(solution)/shard_map/back/pallas_call | solution.py:38
  113.3 6.0 %all-to-all-start.2 = ((bf16[8,4,112,128]{3,2,1,0:T(8,128)(2,1)}), bf16[8,4,112,128]{3,2,1,0:T(8,128)(2,1)S(1)}, u32[]{:S(2)}, u32[]{:S(2)}) async-start(bf16[8,4,112,128]{3,2,1,0:T(8,128)(2,1)} %get-tuple-element.79), calls=%async_computation.2 | async-start | bytes 1835008 | tf_op jit(solution)/shard_map/scatter/all_to_all | solution.py:398
  123.6 4.6 %collective-permute-done.20.refs_1_ = bf16[8,224,128]{2,1,0:T(8,128)(2,1)S(1)} collective-permute-done((bf16[8,224,128]{2,1,0:T(8,128)(2,1)S(1)}, bf16[8,224,128]{2,1,0:T(8,128)(2,1)S(1)}, u32[]{:S(2)}, u32[]{:S(2)}) %collective-permute-start.20) | collective-permute-done | bytes 458784 | tf_op jit(solution)/shard_map/scatter/ppermute | solution.py:310
  128.2 12.8 %collective-permute-done.21.refs_2_ = bf16[8,224,128]{2,1,0:T(8,128)(2,1)S(1)} collective-permute-done((bf16[8,224,128]{2,1,0:T(8,128)(2,1)S(1)}, bf16[8,224,128]{2,1,0:T(8,128)(2,1)S(1)}, u32[]{:S(2)}, u32[]{:S(2)}) %collective-permute-start.21) | collective-permute-done | bytes 458784 | tf_op jit(solution)/shard_map/scatter/ppermute | solution.py:310
  143.0 6.4 %all-to-all-start.3 = ((bf16[8,224,128]{2,1,0:T(8,128)(2,1)}), bf16[8,224,128]{2,1,0:T(8,128)(2,1)S(1)}, u32[]{:S(2)}, u32[]{:S(2)}) async-start(bf16[8,224,128]{2,1,0:T(8,128)(2,1)} %scatter.2), calls=%async_computation.3 | async-start | bytes 917504 | tf_op jit(solution)/shard_map/scatter/all_to_all | solution.py:403
  149.5 2.1 %collective-permute-start.23 = (bf16[112,128]{1,0:T(8,128)(2,1)S(1)}, bf16[112,128]{1,0:T(8,128)(2,1)S(1)}, u32[]{:S(2)}, u32[]{:S(2)}) collective-permute-start(bf16[112,128]{1,0:T(8,128)(2,1)S(1)} %get-tuple-element.86), channel_id=1, source_target_pairs={{0,32},{16,48},{32,0},{48,16},{1,33},{17,49},{33,1},{49,17},{2,34}... | collective-permute-start | bytes 86024 | tf_op jit(solution)/shard_map/scatter/ppermute | solution.py:310
  151.8 2.5 %collective-permute-start.25 = (bf16[112,128]{1,0:T(8,128)(2,1)S(1)}, bf16[112,128]{1,0:T(8,128)(2,1)S(1)}, u32[]{:S(2)}, u32[]{:S(2)}) collective-permute-start(bf16[112,128]{1,0:T(8,128)(2,1)S(1)} %get-tuple-element.88), channel_id=1, source_target_pairs={{0,48},{16,0},{32,16},{48,32},{1,49},{17,1},{33,17},{49,33},{2,50}... | collective-permute-start | bytes 86024 | tf_op jit(solution)/shard_map/scatter/ppermute | solution.py:310
  155.6 6.3 %all-to-all-done.3.refs_4_ = bf16[8,224,128]{2,1,0:T(8,128)(2,1)S(1)} async-done(((bf16[8,224,128]{2,1,0:T(8,128)(2,1)}), bf16[8,224,128]{2,1,0:T(8,128)(2,1)S(1)}, u32[]{:S(2)}, u32[]{:S(2)}) %all-to-all-start.3) | async-done | bytes 458784 | tf_op jit(solution)/shard_map/scatter/all_to_all | solution.py:403
  162.0 12.8 %all_to_all.26.got_ref = bf16[8,96,128]{2,1,0:T(8,128)(2,1)S(1)} all-to-all(bf16[8,96,128]{2,1,0:T(8,128)(2,1)S(1)} %combine.2), channel_id=1, replica_groups=mesh['expert'=4,'tensor_0'=4,'tensor_1'=8,'kv'=2] {'expert','kv'}, dimensions={0} | all-to-all | bytes 393216 | tf_op jit(solution)/shard_map/combine/all_to_all | solution.py:408
  (71 shorter events, 34.0 us)
Async XLA Ops:
  16.3 44.2 %collective-permute-start.5 = (bf16[224,4096]{1,0:T(8,128)(2,1)S(1)}, bf16[224,4096]{1,0:T(8,128)(2,1)}, u32[]{:S(2)}, u32[]{:S(2)}) collective-permute-start(bf16[224,4096]{1,0:T(8,128)(2,1)S(1)} %bitcast.18), channel_id=1, source_target_pairs={{0,1},{1,0},{2,3},{3,2},{4,5},{5,4},{6,7},{7,6},{8,9},{9,8},{10,11... | collective-permute-start | bytes 5505032 | tf_op jit(solution)/shard_map/weights/ppermute | solution.py:310
  18.2 42.3 %all-to-all-start.1 = ((bf16[8,432,128]{2,1,0:T(8,128)(2,1)}), bf16[8,432,128]{2,1,0:T(8,128)(2,1)S(1)}, u32[]{:S(2)}, u32[]{:S(2)}) async-start(bf16[8,432,128]{2,1,0:T(8,128)(2,1)} %get-tuple-element.51), calls=%async_computation.1 | async-start | bytes 1769472 | tf_op jit(solution)/shard_map/gather/all_to_all | solution.py:345
  28.6 6.9 %collective-permute-start.2 = (bf16[544,128]{1,0:T(8,128)(2,1)S(1)}, bf16[544,128]{1,0:T(8,128)(2,1)S(1)}, u32[]{:S(2)}, u32[]{:S(2)}) collective-permute-start(bf16[544,128]{1,0:T(8,128)(2,1)S(1)} %get-tuple-element.49), channel_id=1, source_target_pairs={{0,16},{16,32},{32,48},{48,0},{1,17},{17,33},{33,49},{49,1},{2,18}... | collective-permute-start | bytes 417800 | tf_op jit(solution)/shard_map/gather/ppermute | solution.py:310
  29.0 6.5 %collective-permute-start = (bf16[544,128]{1,0:T(8,128)(2,1)S(1)}, bf16[544,128]{1,0:T(8,128)(2,1)S(1)}, u32[]{:S(2)}, u32[]{:S(2)}) collective-permute-start(bf16[544,128]{1,0:T(8,128)(2,1)S(1)} %get-tuple-element.49), channel_id=1, source_target_pairs={{0,48},{16,0},{32,16},{48,32},{1,49},{17,1},{33,17},{49,33},{2,50}... | collective-permute-start | bytes 417800 | tf_op jit(solution)/shard_map/gather/ppermute | solution.py:310
  35.5 24.2 %collective-permute-start.3 = (bf16[4,544,128]{2,1,0:T(8,128)(2,1)S(1)}, bf16[4,544,128]{2,1,0:T(8,128)(2,1)S(1)}, u32[]{:S(2)}, u32[]{:S(2)}) collective-permute-start(bf16[4,544,128]{2,1,0:T(8,128)(2,1)S(1)} %pad_maximum_fusion.b0), channel_id=1, source_target_pairs={{0,2},{2,4},{4,6},{6,8},{8,10},{10,12},{12,14},{14,0},{1,3},{3,5},... | collective-permute-start | bytes 1671176 | tf_op jit(solution)/shard_map/gather/ppermute | solution.py:310
  37.2 23.3 %collective-permute-start.4 = (bf16[4,544,128]{2,1,0:T(8,128)(2,1)S(1)}, bf16[4,544,128]{2,1,0:T(8,128)(2,1)}, u32[]{:S(2)}, u32[]{:S(2)}) collective-permute-start(bf16[4,544,128]{2,1,0:T(8,128)(2,1)S(1)} %pad_maximum_fusion.b0), channel_id=1, source_target_pairs={{0,14},{2,0},{4,2},{6,4},{8,6},{10,8},{12,10},{14,12},{1,15},{3,1}... | collective-permute-start | bytes 1671176 | tf_op jit(solution)/shard_map/gather/ppermute | solution.py:310
  38.5 62.7 %collective-permute-start.16 = (bf16[224,4096]{1,0:T(8,128)(2,1)}, bf16[224,4096]{1,0:T(8,128)(2,1)}, u32[]{:S(2)}, u32[]{:S(2)}) collective-permute-start(bf16[224,4096]{1,0:T(8,128)(2,1)} %bitcast.21), channel_id=1, source_target_pairs={{0,1},{1,0},{2,3},{3,2},{4,5},{5,4},{6,7},{7,6},{8,9},{9,8},{10,11... | collective-permute-start | bytes 5505032 | tf_op jit(solution)/shard_map/gather/ppermute | solution.py:310
  60.5 14.6 %collective-permute-start.6 = (bf16[4,544,128]{2,1,0:T(8,128)(2,1)}, bf16[4,544,128]{2,1,0:T(8,128)(2,1)S(1)}, u32[]{:S(2)}, u32[]{:S(2)}) collective-permute-start(bf16[4,544,128]{2,1,0:T(8,128)(2,1)} %copy-done.3), channel_id=1, source_target_pairs={{0,2},{2,4},{4,6},{6,8},{8,10},{10,12},{12,14},{14,0},{1,3},{3,5},... | collective-permute-start | bytes 1671176 | tf_op jit(solution)/shard_map/gather/ppermute | solution.py:310
  60.6 14.5 %collective-permute-start.7 = (bf16[4,544,128]{2,1,0:T(8,128)(2,1)}, bf16[4,544,128]{2,1,0:T(8,128)(2,1)S(1)}, u32[]{:S(2)}, u32[]{:S(2)}) collective-permute-start(bf16[4,544,128]{2,1,0:T(8,128)(2,1)} %collective-permute-done.4.b1), channel_id=1, source_target_pairs={{0,14},{2,0},{4,2},{6,4},{8,6},{10,8},{12,10},{14,12},{1,15},{3,1}... | collective-permute-start | bytes 1671176 | tf_op jit(solution)/shard_map/gather/ppermute | solution.py:310
  64.0 10.9 %collective-permute-start.8 = (bf16[4,432,128]{2,1,0:T(8,128)(2,1)S(1)}, bf16[4,432,128]{2,1,0:T(8,128)(2,1)S(1)}, u32[]{:S(2)}, u32[]{:S(2)}) collective-permute-start(bf16[4,432,128]{2,1,0:T(8,128)(2,1)S(1)} %get-tuple-element.92), channel_id=1, source_target_pairs={{0,16},{16,32},{32,48},{48,0},{1,17},{17,33},{33,49},{49,1},{2,18}... | collective-permute-start | bytes 1327112 | tf_op jit(solution)/shard_map/gather/ppermute | solution.py:310
  65.4 9.5 %collective-permute-start.9 = (bf16[4,432,128]{2,1,0:T(8,128)(2,1)S(1)}, bf16[4,432,128]{2,1,0:T(8,128)(2,1)S(1)}, u32[]{:S(2)}, u32[]{:S(2)}) collective-permute-start(bf16[4,432,128]{2,1,0:T(8,128)(2,1)S(1)} %get-tuple-element.92), channel_id=1, source_target_pairs={{0,48},{16,0},{32,16},{48,32},{1,49},{17,1},{33,17},{49,33},{2,50}... | collective-permute-start | bytes 1327112 | tf_op jit(solution)/shard_map/gather/ppermute | solution.py:310
  75.1 12.5 %collective-permute-start.10 = (bf16[4,544,128]{2,1,0:T(8,128)(2,1)S(1)}, bf16[4,544,128]{2,1,0:T(8,128)(2,1)S(1)}, u32[]{:S(2)}, u32[]{:S(2)}) collective-permute-start(bf16[4,544,128]{2,1,0:T(8,128)(2,1)S(1)} %collective-permute-done.6.b6), channel_id=1, source_target_pairs={{0,2},{2,4},{4,6},{6,8},{8,10},{10,12},{12,14},{14,0},{1,3},{3,5},... | collective-permute-start | bytes 1671176 | tf_op jit(solution)/shard_map/gather/ppermute | solution.py:310
  75.1 12.5 %collective-permute-start.11 = (bf16[4,544,128]{2,1,0:T(8,128)(2,1)S(1)}, bf16[4,544,128]{2,1,0:T(8,128)(2,1)S(1)}, u32[]{:S(2)}, u32[]{:S(2)}) collective-permute-start(bf16[4,544,128]{2,1,0:T(8,128)(2,1)S(1)} %collective-permute-done.7.b2), channel_id=1, source_target_pairs={{0,14},{2,0},{4,2},{6,4},{8,6},{10,8},{12,10},{14,12},{1,15},{3,1}... | collective-permute-start | bytes 1671176 | tf_op jit(solution)/shard_map/gather/ppermute | solution.py:310
  77.8 9.6 %collective-permute-start.12 = (bf16[4,432,128]{2,1,0:T(8,128)(2,1)S(1)}, bf16[4,432,128]{2,1,0:T(8,128)(2,1)S(1)}, u32[]{:S(2)}, u32[]{:S(2)}) collective-permute-start(bf16[4,432,128]{2,1,0:T(8,128)(2,1)S(1)} %get-tuple-element.91), channel_id=1, source_target_pairs={{0,16},{16,32},{32,48},{48,0},{1,17},{17,33},{33,49},{49,1},{2,18}... | collective-permute-start | bytes 1327112 | tf_op jit(solution)/shard_map/gather/ppermute | solution.py:310
  79.1 8.4 %collective-permute-start.13 = (bf16[4,432,128]{2,1,0:T(8,128)(2,1)S(1)}, bf16[4,432,128]{2,1,0:T(8,128)(2,1)S(1)}, u32[]{:S(2)}, u32[]{:S(2)}) collective-permute-start(bf16[4,432,128]{2,1,0:T(8,128)(2,1)S(1)} %get-tuple-element.91), channel_id=1, source_target_pairs={{0,48},{16,0},{32,16},{48,32},{1,49},{17,1},{33,17},{49,33},{2,50}... | collective-permute-start | bytes 1327112 | tf_op jit(solution)/shard_map/gather/ppermute | solution.py:310
  87.4 8.8 %collective-permute-start.14 = (bf16[4,432,128]{2,1,0:T(8,128)(2,1)S(1)}, bf16[4,432,128]{2,1,0:T(8,128)(2,1)S(1)}, u32[]{:S(2)}, u32[]{:S(2)}) collective-permute-start(bf16[4,432,128]{2,1,0:T(8,128)(2,1)S(1)} %collective-permute-done.8.near3_ref), channel_id=1, source_target_pairs={{0,16},{16,32},{32,48},{48,0},{1,17},{17,33},{33,49},{49,1},{2,18}... | collective-permute-start | bytes 1327112 | tf_op jit(solution)/shard_map/gather/ppermute | solution.py:310
  87.7 10.1 %collective-permute-start.15 = (bf16[4,432,128]{2,1,0:T(8,128)(2,1)S(1)}, bf16[4,432,128]{2,1,0:T(8,128)(2,1)S(1)}, u32[]{:S(2)}, u32[]{:S(2)}) collective-permute-start(bf16[4,432,128]{2,1,0:T(8,128)(2,1)S(1)} %collective-permute-done.13.far1_ref), channel_id=1, source_target_pairs={{0,48},{16,0},{32,16},{48,32},{1,49},{17,1},{33,17},{49,33},{2,50}... | collective-permute-start | bytes 1327112 | tf_op jit(solution)/shard_map/gather/ppermute | solution.py:310
  90.5 7.1 %collective-permute-start.17 = (bf16[2,544,128]{2,1,0:T(8,128)(2,1)S(1)}, bf16[2,544,128]{2,1,0:T(8,128)(2,1)S(1)}, u32[]{:S(2)}, u32[]{:S(2)}) collective-permute-start(bf16[2,544,128]{2,1,0:T(8,128)(2,1)S(1)} %slice.16), channel_id=1, source_target_pairs={{0,2},{2,4},{4,6},{6,8},{8,10},{10,12},{12,14},{14,0},{1,3},{3,5},... | collective-permute-start | bytes 835592 | tf_op jit(solution)/shard_map/gather/ppermute | solution.py:310
  99.8 6.7 %collective-permute-start.19 = (bf16[320,224]{1,0:T(8,128)(2,1)S(1)}, bf16[320,224]{1,0:T(8,128)(2,1)S(1)}, u32[]{:S(2)}, u32[]{:S(2)}) collective-permute-start(bf16[320,224]{1,0:T(8,128)(2,1)S(1)} %get-tuple-element.78), channel_id=1, source_target_pairs={{0,1},{1,0},{2,3},{3,2},{4,5},{5,4},{6,7},{7,6},{8,9},{9,8},{10,11... | collective-permute-start | bytes 430088 | tf_op jit(solution)/shard_map/act/ppermute | solution.py:310
  113.3 29.8 %all-to-all-start.2 = ((bf16[8,4,112,128]{3,2,1,0:T(8,128)(2,1)}), bf16[8,4,112,128]{3,2,1,0:T(8,128)(2,1)S(1)}, u32[]{:S(2)}, u32[]{:S(2)}) async-start(bf16[8,4,112,128]{3,2,1,0:T(8,128)(2,1)} %get-tuple-element.79), calls=%async_computation.2 | async-start | bytes 1835008 | tf_op jit(solution)/shard_map/scatter/all_to_all | solution.py:398
  119.2 8.9 %collective-permute-start.20 = (bf16[8,224,128]{2,1,0:T(8,128)(2,1)S(1)}, bf16[8,224,128]{2,1,0:T(8,128)(2,1)S(1)}, u32[]{:S(2)}, u32[]{:S(2)}) collective-permute-start(bf16[8,224,128]{2,1,0:T(8,128)(2,1)S(1)} %get-tuple-element.81), channel_id=1, source_target_pairs={{0,32},{16,48},{32,0},{48,16},{1,33},{17,49},{33,1},{49,17},{2,34}... | collective-permute-start | bytes 1376264 | tf_op jit(solution)/shard_map/scatter/ppermute | solution.py:310
  120.9 20.1 %collective-permute-start.21 = (bf16[8,224,128]{2,1,0:T(8,128)(2,1)S(1)}, bf16[8,224,128]{2,1,0:T(8,128)(2,1)S(1)}, u32[]{:S(2)}, u32[]{:S(2)}) collective-permute-start(bf16[8,224,128]{2,1,0:T(8,128)(2,1)S(1)} %get-tuple-element.82), channel_id=1, source_target_pairs={{0,16},{16,32},{32,48},{48,0},{1,17},{17,33},{33,49},{49,1},{2,18}... | collective-permute-start | bytes 1376264 | tf_op jit(solution)/shard_map/scatter/ppermute | solution.py:310
  121.6 19.4 %collective-permute-start.22 = (bf16[8,224,128]{2,1,0:T(8,128)(2,1)S(1)}, bf16[8,224,128]{2,1,0:T(8,128)(2,1)S(1)}, u32[]{:S(2)}, u32[]{:S(2)}) collective-permute-start(bf16[8,224,128]{2,1,0:T(8,128)(2,1)S(1)} %get-tuple-element.83), channel_id=1, source_target_pairs={{0,48},{16,0},{32,16},{48,32},{1,49},{17,1},{33,17},{49,33},{2,50}... | collective-permute-start | bytes 1376264 | tf_op jit(solution)/shard_map/scatter/ppermute | solution.py:310
  143.0 18.9 %all-to-all-start.3 = ((bf16[8,224,128]{2,1,0:T(8,128)(2,1)}), bf16[8,224,128]{2,1,0:T(8,128)(2,1)S(1)}, u32[]{:S(2)}, u32[]{:S(2)}) async-start(bf16[8,224,128]{2,1,0:T(8,128)(2,1)} %scatter.2), calls=%async_computation.3 | async-start | bytes 917504 | tf_op jit(solution)/shard_map/scatter/all_to_all | solution.py:403
  (15 other events, 90.7 us)

commit v9 on v8

--- a/solution.py
+++ b/solution.py
@@ -18,7 +18,7 @@
 GAIN_ROWS = 16
 MINE = CAP // 2
 XROWS = HALF + GAIN_ROWS
-SPLIT = 96
+SPLIT = 80
 PADDED = 384
 ZFIRST = 112
 YFIRST = HALF - ZFIRST

time: 177 us -> 177 us (level)
  transfers between devices with their start and end apart: 29 -> 29, of which waited for: 14 -> 13; matrix products, arithmetic and copies ran while one was open for 0% -> 0% of each run, Pallas kernels for 7% -> 7%
where the time goes in v9:
time: 177 us
  waiting for transfers between devices  64.3 us (36%)
  starting transfers between devices  58.3 us (33%)
  blocking collectives  28.2 us (16%)
  Pallas kernels  22 us (12%)
  local copies, waits for them, and re-layouts  3.77 us (2%)
    ppermute x26, waiting for transfers between devices, shift(): return lax.ppermute(value, axis, [(i, (i + by) % n) for i in range(n)])  58.1 us
    ppermute x26, starting transfers between devices, shift(): return lax.ppermute(value, axis, [(i, (i + by) % n) for i in range(n)])  39.3 us
    pallas_call x11, Pallas kernels, run(): pl.pallas_call(kernel, in_specs=[here] * len(arrays), out_specs=[here] *...  22 us
    all_to_all x1, blocking collectives, shards(): lax.all_to_all(routed.reshape(2 * GROUPS, CAP, LANES), LINE, 0, 0, tiled=...  14.1 us
    all_to_all x1, blocking collectives, shards(): got = lax.all_to_all(pieces, LINE, 0, 0, tiled=True)  14.1 us
    all_to_all x1, starting transfers between devices, shards(): line_a = lax.all_to_all(copies, 'tensor_1', 0, 0, tiled=True)  7.41 us
    all_to_all x1, starting transfers between devices, shards(): low = lax.all_to_all(low, 'tensor_1', 0, 0, tiled=True)  6.37 us
    all_to_all x1, waiting for transfers between devices, shards(): low = lax.all_to_all(low, 'tensor_1', 0, 0, tiled=True)  6.24 us
  transfers between devices with their start and end apart: 29, of which 13 were waited for; matrix products, arithmetic and copies ran while one was open for 0% of the time, Pallas kernels for 7%

profile of v9, /device:TPU:1, one launch (start us, length us, event | category | flops | bytes accessed | tf_op | source)
XLA Modules:
  0.0 176.8 jit_solution(16203780315702792994)
XLA Ops:
  0.0 2.2 %dispatch.2 = bf16[4,2,160,128]{3,2,1,0:T(8,128)(2,1)} custom-call(s32[2,256]{1,0:T(2,128)} %bitcast.26, f32[2,256]{1,0:T(2,128)} %bitcast.35, bf16[64,256]{1,0:T(8,128)(2,1)} %bitcast.24, bf16[64,256]{1,0:T(8,128)(2,1)} %bitcast.34, bf16[1,64]{1,0:T(2,128)(2,1)} %bitcast.28), custom_call_target="tpu_custom_call" | custom-call | flops 2000000000 | tf_op jit(solution)/shard_map/dispatch/pallas_call | solution.py:38
  2.2 14.1 %all_to_all.25 = bf16[8,160,128]{2,1,0:T(8,128)(2,1)S(1)} all-to-all(bf16[8,160,128]{2,1,0:T(8,128)(2,1)} %bitcast.30), channel_id=1, replica_groups=mesh['expert'=4,'tensor_0'=4,'tensor_1'=8,'kv'=2] {'expert','kv'}, dimensions={0} | all-to-all | bytes 655360 | tf_op jit(solution)/shard_map/dispatch/all_to_all | solution.py:336
  18.2 7.4 %all-to-all-start.1 = ((bf16[8,416,128]{2,1,0:T(8,128)(2,1)}), bf16[8,416,128]{2,1,0:T(8,128)(2,1)S(1)}, u32[]{:S(2)}, u32[]{:S(2)}) async-start(bf16[8,416,128]{2,1,0:T(8,128)(2,1)} %get-tuple-element.51), calls=%async_computation.1 | async-start | bytes 1703936 | tf_op jit(solution)/shard_map/gather/all_to_all | solution.py:345
  25.6 2.9 %collective-permute-start.1 = (bf16[560,128]{1,0:T(8,128)(2,1)S(1)}, bf16[560,128]{1,0:T(8,128)(2,1)S(1)}, u32[]{:S(2)}, u32[]{:S(2)}) collective-permute-start(bf16[560,128]{1,0:T(8,128)(2,1)S(1)} %get-tuple-element.49), channel_id=1, source_target_pairs={{0,32},{16,48},{32,0},{48,16},{1,33},{17,49},{33,1},{49,17},{2,34}... | collective-permute-start | bytes 430088 | tf_op jit(solution)/shard_map/gather/ppermute | solution.py:310
  29.0 2.3 %collective-permute-start = (bf16[560,128]{1,0:T(8,128)(2,1)S(1)}, bf16[560,128]{1,0:T(8,128)(2,1)S(1)}, u32[]{:S(2)}, u32[]{:S(2)}) collective-permute-start(bf16[560,128]{1,0:T(8,128)(2,1)S(1)} %get-tuple-element.49), channel_id=1, source_target_pairs={{0,48},{16,0},{32,16},{48,32},{1,49},{17,1},{33,17},{49,33},{2,50}... | collective-permute-start | bytes 430088 | tf_op jit(solution)/shard_map/gather/ppermute | solution.py:310
  31.5 4.1 %collective-permute-done.2 = bf16[560,128]{1,0:T(8,128)(2,1)S(1)} collective-permute-done((bf16[560,128]{1,0:T(8,128)(2,1)S(1)}, bf16[560,128]{1,0:T(8,128)(2,1)S(1)}, u32[]{:S(2)}, u32[]{:S(2)}) %collective-permute-start.2) | collective-permute-done | bytes 143392 | tf_op jit(solution)/shard_map/gather/ppermute | solution.py:310
  40.5 18.8 %collective-permute-done.3.b7 = bf16[4,560,128]{2,1,0:T(8,128)(2,1)S(1)} collective-permute-done((bf16[4,560,128]{2,1,0:T(8,128)(2,1)S(1)}, bf16[4,560,128]{2,1,0:T(8,128)(2,1)S(1)}, u32[]{:S(2)}, u32[]{:S(2)}) %collective-permute-start.3) | collective-permute-done | bytes 573472 | tf_op jit(solution)/shard_map/gather/ppermute | solution.py:310
  60.3 3.7 %collective-permute-start.7 = (bf16[4,560,128]{2,1,0:T(8,128)(2,1)}, bf16[4,560,128]{2,1,0:T(8,128)(2,1)S(1)}, u32[]{:S(2)}, u32[]{:S(2)}) collective-permute-start(bf16[4,560,128]{2,1,0:T(8,128)(2,1)} %collective-permute-done.4.b1), channel_id=1, source_target_pairs={{0,14},{2,0},{4,2},{6,4},{8,6},{10,8},{12,10},{14,12},{1,15},{3,1}... | collective-permute-start | bytes 1720328 | tf_op jit(solution)/shard_map/gather/ppermute | solution.py:310
  66.9 7.6 %collective-permute-done.8.near3_ref = bf16[4,416,128]{2,1,0:T(8,128)(2,1)S(1)} collective-permute-done((bf16[4,416,128]{2,1,0:T(8,128)(2,1)S(1)}, bf16[4,416,128]{2,1,0:T(8,128)(2,1)S(1)}, u32[]{:S(2)}, u32[]{:S(2)}) %collective-permute-start.8) | collective-permute-done | bytes 426016 | tf_op jit(solution)/shard_map/gather/ppermute | solution.py:310
  75.5 2.7 %collective-permute-start.11 = (bf16[4,560,128]{2,1,0:T(8,128)(2,1)S(1)}, bf16[4,560,128]{2,1,0:T(8,128)(2,1)S(1)}, u32[]{:S(2)}, u32[]{:S(2)}) collective-permute-start(bf16[4,560,128]{2,1,0:T(8,128)(2,1)S(1)} %collective-permute-done.7.b2), channel_id=1, source_target_pairs={{0,14},{2,0},{4,2},{6,4},{8,6},{10,8},{12,10},{14,12},{1,15},{3,1}... | collective-permute-start | bytes 1720328 | tf_op jit(solution)/shard_map/gather/ppermute | solution.py:310
  82.0 2.4 %gather.1 = (bf16[320,4096]{1,0:T(8,128)(2,1)S(1)}, bf16[640,4096]{1,0:T(8,128)(2,1)S(1)}, f32[320,128]{1,0:T(8,128)S(1)}) custom-call(bf16[8,416,128]{2,1,0:T(8,128)(2,1)S(1)} %all-to-all-done.1.line_ref, bf16[4,416,128]{2,1,0:T(8,128)(2,1)S(1)} %collective-permute-done.9.near1_ref, bf16[4,416,128]{2,1,0:T(8,128)(2,1)S(1)} %collective-permute-done.8.near3_ref, ...), custom_call_target="tpu_custom_call" | custom-call | flops 5000000000 | tf_op jit(solution)/shard_map/gather/pallas_call | solution.py:38
  84.3 3.4 %collective-permute-done.12.far3_ref = bf16[4,416,128]{2,1,0:T(8,128)(2,1)S(1)} collective-permute-done((bf16[4,416,128]{2,1,0:T(8,128)(2,1)S(1)}, bf16[4,416,128]{2,1,0:T(8,128)(2,1)S(1)}, u32[]{:S(2)}, u32[]{:S(2)}) %collective-permute-start.12) | collective-permute-done | bytes 426016 | tf_op jit(solution)/shard_map/gather/ppermute | solution.py:310
  88.7 2.7 %collective-permute-start.15 = (bf16[4,416,128]{2,1,0:T(8,128)(2,1)S(1)}, bf16[4,416,128]{2,1,0:T(8,128)(2,1)S(1)}, u32[]{:S(2)}, u32[]{:S(2)}) collective-permute-start(bf16[4,416,128]{2,1,0:T(8,128)(2,1)S(1)} %collective-permute-done.13.far1_ref), channel_id=1, source_target_pairs={{0,48},{16,0},{32,16},{48,32},{1,49},{17,1},{33,17},{49,33},{2,50}... | collective-permute-start | bytes 1277960 | tf_op jit(solution)/shard_map/gather/ppermute | solution.py:310
  96.5 2.1 %collective-permute-done.17.b4lo_ref = bf16[2,560,128]{2,1,0:T(8,128)(2,1)S(1)} collective-permute-done((bf16[2,560,128]{2,1,0:T(8,128)(2,1)S(1)}, bf16[2,560,128]{2,1,0:T(8,128)(2,1)S(1)}, u32[]{:S(2)}, u32[]{:S(2)}) %collective-permute-start.17) | collective-permute-done | bytes 286752 | tf_op jit(solution)/shard_map/gather/ppermute | solution.py:310
  101.7 5.2 %forward.1 = (bf16[320,4096]{1,0:T(8,128)(2,1)S(1)}, f32[320,128]{1,0:T(8,128)S(1)}, f32[320,224]{1,0:T(8,128)S(1)}, f32[320,224]{1,0:T(8,128)S(1)}, f32[320,224...) custom-call(bf16[320,4096]{1,0:T(8,128)(2,1)S(1)} %get-tuple-element, ...), custom_call_target="tpu_custom_call", output_to_operand_aliasing={{0}: (0, {}), {1}: (1, {})} | custom-call | flops 5000000000 | tf_op jit(solution)/shard_map/forward/pallas_call | solution.py:38
  106.9 6.0 %back.1 = (bf16[8,4,112,128]{3,2,1,0:T(8,128)(2,1)}, bf16[8,224,128]{2,1,0:T(8,128)(2,1)S(1)}, bf16[8,224,128]{2,1,0:T(8,128)(2,1)S(1)}, bf16[8,224,128]{2,1,0:T(8,128)(2,1)S(1)}, bf16[8,224,128]{2,1,0:T(8,128)(2,1)S(1)}) custom-call(f32[320,224]{1,0:T(8,128)S(1)} %get-tuple-element.70.refs_0_, f32[320,224]{1,0:T(8,128)S(1)} %get-tuple-element.71.refs_1_, ...), custom_call_target="tpu_custom_call" | custom-call | flops 8000000000 | tf_op jit(solution)/shard_map/back/pallas_call | solution.py:38
  113.7 5.2 %all-to-all-start.2 = ((bf16[8,4,112,128]{3,2,1,0:T(8,128)(2,1)}), bf16[8,4,112,128]{3,2,1,0:T(8,128)(2,1)S(1)}, u32[]{:S(2)}, u32[]{:S(2)}) async-start(bf16[8,4,112,128]{3,2,1,0:T(8,128)(2,1)} %get-tuple-element.79), calls=%async_computation.2 | async-start | bytes 1835008 | tf_op jit(solution)/shard_map/scatter/all_to_all | solution.py:398
  121.2 2.3 %collective-permute-start.22 = (bf16[8,224,128]{2,1,0:T(8,128)(2,1)S(1)}, bf16[8,224,128]{2,1,0:T(8,128)(2,1)S(1)}, u32[]{:S(2)}, u32[]{:S(2)}) collective-permute-start(bf16[8,224,128]{2,1,0:T(8,128)(2,1)S(1)} %get-tuple-element.83), channel_id=1, source_target_pairs={{0,48},{16,0},{32,16},{48,32},{1,49},{17,1},{33,17},{49,33},{2,50}... | collective-permute-start | bytes 1376264 | tf_op jit(solution)/shard_map/scatter/ppermute | solution.py:310
  123.5 4.3 %collective-permute-done.20.refs_1_ = bf16[8,224,128]{2,1,0:T(8,128)(2,1)S(1)} collective-permute-done((bf16[8,224,128]{2,1,0:T(8,128)(2,1)S(1)}, bf16[8,224,128]{2,1,0:T(8,128)(2,1)S(1)}, u32[]{:S(2)}, u32[]{:S(2)}) %collective-permute-start.20) | collective-permute-done | bytes 458784 | tf_op jit(solution)/shard_map/scatter/ppermute | solution.py:310
  127.9 12.8 %collective-permute-done.21.refs_2_ = bf16[8,224,128]{2,1,0:T(8,128)(2,1)S(1)} collective-permute-done((bf16[8,224,128]{2,1,0:T(8,128)(2,1)S(1)}, bf16[8,224,128]{2,1,0:T(8,128)(2,1)S(1)}, u32[]{:S(2)}, u32[]{:S(2)}) %collective-permute-start.21) | collective-permute-done | bytes 458784 | tf_op jit(solution)/shard_map/scatter/ppermute | solution.py:310
  142.7 6.4 %all-to-all-start.3 = ((bf16[8,224,128]{2,1,0:T(8,128)(2,1)}), bf16[8,224,128]{2,1,0:T(8,128)(2,1)S(1)}, u32[]{:S(2)}, u32[]{:S(2)}) async-start(bf16[8,224,128]{2,1,0:T(8,128)(2,1)} %scatter.2), calls=%async_computation.3 | async-start | bytes 917504 | tf_op jit(solution)/shard_map/scatter/all_to_all | solution.py:403
  151.3 2.7 %collective-permute-start.25 = (bf16[112,128]{1,0:T(8,128)(2,1)S(1)}, bf16[112,128]{1,0:T(8,128)(2,1)S(1)}, u32[]{:S(2)}, u32[]{:S(2)}) collective-permute-start(bf16[112,128]{1,0:T(8,128)(2,1)S(1)} %get-tuple-element.88), channel_id=1, source_target_pairs={{0,48},{16,0},{32,16},{48,32},{1,49},{17,1},{33,17},{49,33},{2,50}... | collective-permute-start | bytes 86024 | tf_op jit(solution)/shard_map/scatter/ppermute | solution.py:310
  155.2 6.2 %all-to-all-done.3.refs_4_ = bf16[8,224,128]{2,1,0:T(8,128)(2,1)S(1)} async-done(((bf16[8,224,128]{2,1,0:T(8,128)(2,1)}), bf16[8,224,128]{2,1,0:T(8,128)(2,1)S(1)}, u32[]{:S(2)}, u32[]{:S(2)}) %all-to-all-start.3) | async-done | bytes 458784 | tf_op jit(solution)/shard_map/scatter/all_to_all | solution.py:403
  161.6 14.1 %all_to_all.26.got_ref = bf16[8,96,128]{2,1,0:T(8,128)(2,1)S(1)} all-to-all(bf16[8,96,128]{2,1,0:T(8,128)(2,1)S(1)} %combine.2), channel_id=1, replica_groups=mesh['expert'=4,'tensor_0'=4,'tensor_1'=8,'kv'=2] {'expert','kv'}, dimensions={0} | all-to-all | bytes 393216 | tf_op jit(solution)/shard_map/combine/all_to_all | solution.py:408
  (71 shorter events, 35.0 us)
Async XLA Ops:
  16.3 43.9 %collective-permute-start.5 = (bf16[224,4096]{1,0:T(8,128)(2,1)S(1)}, bf16[224,4096]{1,0:T(8,128)(2,1)}, u32[]{:S(2)}, u32[]{:S(2)}) collective-permute-start(bf16[224,4096]{1,0:T(8,128)(2,1)S(1)} %bitcast.18), channel_id=1, source_target_pairs={{0,1},{1,0},{2,3},{3,2},{4,5},{5,4},{6,7},{7,6},{8,9},{9,8},{10,11... | collective-permute-start | bytes 5505032 | tf_op jit(solution)/shard_map/weights/ppermute | solution.py:310
  18.2 41.9 %all-to-all-start.1 = ((bf16[8,416,128]{2,1,0:T(8,128)(2,1)}), bf16[8,416,128]{2,1,0:T(8,128)(2,1)S(1)}, u32[]{:S(2)}, u32[]{:S(2)}) async-start(bf16[8,416,128]{2,1,0:T(8,128)(2,1)} %get-tuple-element.51), calls=%async_computation.1 | async-start | bytes 1703936 | tf_op jit(solution)/shard_map/gather/all_to_all | solution.py:345
  28.6 7.0 %collective-permute-start.2 = (bf16[560,128]{1,0:T(8,128)(2,1)S(1)}, bf16[560,128]{1,0:T(8,128)(2,1)S(1)}, u32[]{:S(2)}, u32[]{:S(2)}) collective-permute-start(bf16[560,128]{1,0:T(8,128)(2,1)S(1)} %get-tuple-element.49), channel_id=1, source_target_pairs={{0,16},{16,32},{32,48},{48,0},{1,17},{17,33},{33,49},{49,1},{2,18}... | collective-permute-start | bytes 430088 | tf_op jit(solution)/shard_map/gather/ppermute | solution.py:310
  29.0 6.6 %collective-permute-start = (bf16[560,128]{1,0:T(8,128)(2,1)S(1)}, bf16[560,128]{1,0:T(8,128)(2,1)S(1)}, u32[]{:S(2)}, u32[]{:S(2)}) collective-permute-start(bf16[560,128]{1,0:T(8,128)(2,1)S(1)} %get-tuple-element.49), channel_id=1, source_target_pairs={{0,48},{16,0},{32,16},{48,32},{1,49},{17,1},{33,17},{49,33},{2,50}... | collective-permute-start | bytes 430088 | tf_op jit(solution)/shard_map/gather/ppermute | solution.py:310
  35.7 23.7 %collective-permute-start.3 = (bf16[4,560,128]{2,1,0:T(8,128)(2,1)S(1)}, bf16[4,560,128]{2,1,0:T(8,128)(2,1)S(1)}, u32[]{:S(2)}, u32[]{:S(2)}) collective-permute-start(bf16[4,560,128]{2,1,0:T(8,128)(2,1)S(1)} %pad_maximum_fusion.b0), channel_id=1, source_target_pairs={{0,2},{2,4},{4,6},{6,8},{8,10},{10,12},{12,14},{14,0},{1,3},{3,5},... | collective-permute-start | bytes 1720328 | tf_op jit(solution)/shard_map/gather/ppermute | solution.py:310
  37.3 22.9 %collective-permute-start.4 = (bf16[4,560,128]{2,1,0:T(8,128)(2,1)S(1)}, bf16[4,560,128]{2,1,0:T(8,128)(2,1)}, u32[]{:S(2)}, u32[]{:S(2)}) collective-permute-start(bf16[4,560,128]{2,1,0:T(8,128)(2,1)S(1)} %pad_maximum_fusion.b0), channel_id=1, source_target_pairs={{0,14},{2,0},{4,2},{6,4},{8,6},{10,8},{12,10},{14,12},{1,15},{3,1}... | collective-permute-start | bytes 1720328 | tf_op jit(solution)/shard_map/gather/ppermute | solution.py:310
  38.6 63.1 %collective-permute-start.16 = (bf16[224,4096]{1,0:T(8,128)(2,1)}, bf16[224,4096]{1,0:T(8,128)(2,1)}, u32[]{:S(2)}, u32[]{:S(2)}) collective-permute-start(bf16[224,4096]{1,0:T(8,128)(2,1)} %bitcast.21), channel_id=1, source_target_pairs={{0,1},{1,0},{2,3},{3,2},{4,5},{5,4},{6,7},{7,6},{8,9},{9,8},{10,11... | collective-permute-start | bytes 5505032 | tf_op jit(solution)/shard_map/gather/ppermute | solution.py:310
  60.2 15.3 %collective-permute-start.6 = (bf16[4,560,128]{2,1,0:T(8,128)(2,1)}, bf16[4,560,128]{2,1,0:T(8,128)(2,1)S(1)}, u32[]{:S(2)}, u32[]{:S(2)}) collective-permute-start(bf16[4,560,128]{2,1,0:T(8,128)(2,1)} %copy-done.3), channel_id=1, source_target_pairs={{0,2},{2,4},{4,6},{6,8},{8,10},{10,12},{12,14},{14,0},{1,3},{3,5},... | collective-permute-start | bytes 1720328 | tf_op jit(solution)/shard_map/gather/ppermute | solution.py:310
  60.3 15.2 %collective-permute-start.7 = (bf16[4,560,128]{2,1,0:T(8,128)(2,1)}, bf16[4,560,128]{2,1,0:T(8,128)(2,1)S(1)}, u32[]{:S(2)}, u32[]{:S(2)}) collective-permute-start(bf16[4,560,128]{2,1,0:T(8,128)(2,1)} %collective-permute-done.4.b1), channel_id=1, source_target_pairs={{0,14},{2,0},{4,2},{6,4},{8,6},{10,8},{12,10},{14,12},{1,15},{3,1}... | collective-permute-start | bytes 1720328 | tf_op jit(solution)/shard_map/gather/ppermute | solution.py:310
  64.0 10.5 %collective-permute-start.8 = (bf16[4,416,128]{2,1,0:T(8,128)(2,1)S(1)}, bf16[4,416,128]{2,1,0:T(8,128)(2,1)S(1)}, u32[]{:S(2)}, u32[]{:S(2)}) collective-permute-start(bf16[4,416,128]{2,1,0:T(8,128)(2,1)S(1)} %get-tuple-element.92), channel_id=1, source_target_pairs={{0,16},{16,32},{32,48},{48,0},{1,17},{17,33},{33,49},{49,1},{2,18}... | collective-permute-start | bytes 1277960 | tf_op jit(solution)/shard_map/gather/ppermute | solution.py:310
  65.4 9.1 %collective-permute-start.9 = (bf16[4,416,128]{2,1,0:T(8,128)(2,1)S(1)}, bf16[4,416,128]{2,1,0:T(8,128)(2,1)S(1)}, u32[]{:S(2)}, u32[]{:S(2)}) collective-permute-start(bf16[4,416,128]{2,1,0:T(8,128)(2,1)S(1)} %get-tuple-element.92), channel_id=1, source_target_pairs={{0,48},{16,0},{32,16},{48,32},{1,49},{17,1},{33,17},{49,33},{2,50}... | collective-permute-start | bytes 1277960 | tf_op jit(solution)/shard_map/gather/ppermute | solution.py:310
  75.5 13.2 %collective-permute-start.10 = (bf16[4,560,128]{2,1,0:T(8,128)(2,1)S(1)}, bf16[4,560,128]{2,1,0:T(8,128)(2,1)S(1)}, u32[]{:S(2)}, u32[]{:S(2)}) collective-permute-start(bf16[4,560,128]{2,1,0:T(8,128)(2,1)S(1)} %collective-permute-done.6.b6), channel_id=1, source_target_pairs={{0,2},{2,4},{4,6},{6,8},{8,10},{10,12},{12,14},{14,0},{1,3},{3,5},... | collective-permute-start | bytes 1720328 | tf_op jit(solution)/shard_map/gather/ppermute | solution.py:310
  75.5 13.2 %collective-permute-start.11 = (bf16[4,560,128]{2,1,0:T(8,128)(2,1)S(1)}, bf16[4,560,128]{2,1,0:T(8,128)(2,1)S(1)}, u32[]{:S(2)}, u32[]{:S(2)}) collective-permute-start(bf16[4,560,128]{2,1,0:T(8,128)(2,1)S(1)} %collective-permute-done.7.b2), channel_id=1, source_target_pairs={{0,14},{2,0},{4,2},{6,4},{8,6},{10,8},{12,10},{14,12},{1,15},{3,1}... | collective-permute-start | bytes 1720328 | tf_op jit(solution)/shard_map/gather/ppermute | solution.py:310
  78.2 9.6 %collective-permute-start.12 = (bf16[4,416,128]{2,1,0:T(8,128)(2,1)S(1)}, bf16[4,416,128]{2,1,0:T(8,128)(2,1)S(1)}, u32[]{:S(2)}, u32[]{:S(2)}) collective-permute-start(bf16[4,416,128]{2,1,0:T(8,128)(2,1)S(1)} %get-tuple-element.91), channel_id=1, source_target_pairs={{0,16},{16,32},{32,48},{48,0},{1,17},{17,33},{33,49},{49,1},{2,18}... | collective-permute-start | bytes 1277960 | tf_op jit(solution)/shard_map/gather/ppermute | solution.py:310
  79.5 8.3 %collective-permute-start.13 = (bf16[4,416,128]{2,1,0:T(8,128)(2,1)S(1)}, bf16[4,416,128]{2,1,0:T(8,128)(2,1)S(1)}, u32[]{:S(2)}, u32[]{:S(2)}) collective-permute-start(bf16[4,416,128]{2,1,0:T(8,128)(2,1)S(1)} %get-tuple-element.91), channel_id=1, source_target_pairs={{0,48},{16,0},{32,16},{48,32},{1,49},{17,1},{33,17},{49,33},{2,50}... | collective-permute-start | bytes 1277960 | tf_op jit(solution)/shard_map/gather/ppermute | solution.py:310
  87.8 8.7 %collective-permute-start.14 = (bf16[4,416,128]{2,1,0:T(8,128)(2,1)S(1)}, bf16[4,416,128]{2,1,0:T(8,128)(2,1)S(1)}, u32[]{:S(2)}, u32[]{:S(2)}) collective-permute-start(bf16[4,416,128]{2,1,0:T(8,128)(2,1)S(1)} %collective-permute-done.8.near3_ref), channel_id=1, source_target_pairs={{0,16},{16,32},{32,48},{48,0},{1,17},{17,33},{33,49},{49,1},{2,18}... | collective-permute-start | bytes 1277960 | tf_op jit(solution)/shard_map/gather/ppermute | solution.py:310
  88.7 9.9 %collective-permute-start.15 = (bf16[4,416,128]{2,1,0:T(8,128)(2,1)S(1)}, bf16[4,416,128]{2,1,0:T(8,128)(2,1)S(1)}, u32[]{:S(2)}, u32[]{:S(2)}) collective-permute-start(bf16[4,416,128]{2,1,0:T(8,128)(2,1)S(1)} %collective-permute-done.13.far1_ref), channel_id=1, source_target_pairs={{0,48},{16,0},{32,16},{48,32},{1,49},{17,1},{33,17},{49,33},{2,50}... | collective-permute-start | bytes 1277960 | tf_op jit(solution)/shard_map/gather/ppermute | solution.py:310
  91.4 7.2 %collective-permute-start.17 = (bf16[2,560,128]{2,1,0:T(8,128)(2,1)S(1)}, bf16[2,560,128]{2,1,0:T(8,128)(2,1)S(1)}, u32[]{:S(2)}, u32[]{:S(2)}) collective-permute-start(bf16[2,560,128]{2,1,0:T(8,128)(2,1)S(1)} %slice.16), channel_id=1, source_target_pairs={{0,2},{2,4},{4,6},{6,8},{8,10},{10,12},{12,14},{14,0},{1,3},{3,5},... | collective-permute-start | bytes 860168 | tf_op jit(solution)/shard_map/gather/ppermute | solution.py:310
  100.7 6.2 %collective-permute-start.19 = (bf16[320,224]{1,0:T(8,128)(2,1)S(1)}, bf16[320,224]{1,0:T(8,128)(2,1)S(1)}, u32[]{:S(2)}, u32[]{:S(2)}) collective-permute-start(bf16[320,224]{1,0:T(8,128)(2,1)S(1)} %get-tuple-element.78), channel_id=1, source_target_pairs={{0,1},{1,0},{2,3},{3,2},{4,5},{5,4},{6,7},{7,6},{8,9},{9,8},{10,11... | collective-permute-start | bytes 430088 | tf_op jit(solution)/shard_map/act/ppermute | solution.py:310
  113.7 28.9 %all-to-all-start.2 = ((bf16[8,4,112,128]{3,2,1,0:T(8,128)(2,1)}), bf16[8,4,112,128]{3,2,1,0:T(8,128)(2,1)S(1)}, u32[]{:S(2)}, u32[]{:S(2)}) async-start(bf16[8,4,112,128]{3,2,1,0:T(8,128)(2,1)} %get-tuple-element.79), calls=%async_computation.2 | async-start | bytes 1835008 | tf_op jit(solution)/shard_map/scatter/all_to_all | solution.py:398
  118.9 8.9 %collective-permute-start.20 = (bf16[8,224,128]{2,1,0:T(8,128)(2,1)S(1)}, bf16[8,224,128]{2,1,0:T(8,128)(2,1)S(1)}, u32[]{:S(2)}, u32[]{:S(2)}) collective-permute-start(bf16[8,224,128]{2,1,0:T(8,128)(2,1)S(1)} %get-tuple-element.81), channel_id=1, source_target_pairs={{0,32},{16,48},{32,0},{48,16},{1,33},{17,49},{33,1},{49,17},{2,34}... | collective-permute-start | bytes 1376264 | tf_op jit(solution)/shard_map/scatter/ppermute | solution.py:310
  120.8 19.8 %collective-permute-start.21 = (bf16[8,224,128]{2,1,0:T(8,128)(2,1)S(1)}, bf16[8,224,128]{2,1,0:T(8,128)(2,1)S(1)}, u32[]{:S(2)}, u32[]{:S(2)}) collective-permute-start(bf16[8,224,128]{2,1,0:T(8,128)(2,1)S(1)} %get-tuple-element.82), channel_id=1, source_target_pairs={{0,16},{16,32},{32,48},{48,0},{1,17},{17,33},{33,49},{49,1},{2,18}... | collective-permute-start | bytes 1376264 | tf_op jit(solution)/shard_map/scatter/ppermute | solution.py:310
  121.2 19.4 %collective-permute-start.22 = (bf16[8,224,128]{2,1,0:T(8,128)(2,1)S(1)}, bf16[8,224,128]{2,1,0:T(8,128)(2,1)S(1)}, u32[]{:S(2)}, u32[]{:S(2)}) collective-permute-start(bf16[8,224,128]{2,1,0:T(8,128)(2,1)S(1)} %get-tuple-element.83), channel_id=1, source_target_pairs={{0,48},{16,0},{32,16},{48,32},{1,49},{17,1},{33,17},{49,33},{2,50}... | collective-permute-start | bytes 1376264 | tf_op jit(solution)/shard_map/scatter/ppermute | solution.py:310
  142.7 18.8 %all-to-all-start.3 = ((bf16[8,224,128]{2,1,0:T(8,128)(2,1)}), bf16[8,224,128]{2,1,0:T(8,128)(2,1)S(1)}, u32[]{:S(2)}, u32[]{:S(2)}) async-start(bf16[8,224,128]{2,1,0:T(8,128)(2,1)} %scatter.2), calls=%async_computation.3 | async-start | bytes 917504 | tf_op jit(solution)/shard_map/scatter/all_to_all | solution.py:403
  (15 other events, 94.5 us)
